TPU v7x, 512 devices: a whole 4x4x16 slice. The times are simulated.
512 devices in a mesh: ctx: 32 (over z, core), head: 16 (over y, x).
Axes of the slice: x: 4, y: 4, z: 16, core: 2. Of those that a mesh axis runs over, the one named last changes fastest.
Arguments:
- q_latent: bfloat16 [4096, 65536], P('ctx', 'head'), may hold values from -8 to 8
- q_rope: bfloat16 [4096, 8192], P('ctx', 'head'), may hold values from -15 to 15
- kv_latent: bfloat16 [512, 64, 512], P('ctx'), may hold values from -6 to 6
- k_rope: bfloat16 [512, 4096], P('ctx'), may hold values from -6 to 6
- selection: int32 [64, 32], P('ctx'), may hold values from 0 to 511, as said below
- w_uv: bfloat16 [128, 512, 128], P('head'), may hold values from -0.75 to 0.75
Outputs:
- attn_out: bfloat16 [4096, 16384], P('ctx', 'head')
Inputs may be any that keep to these rules, and one draw needn't show every extreme that they name: `selection`: each row lists 32 distinct blocks; block b is held by index b // 16 of ctx. The first 8 entries are the same in every row: the consecutive blocks of one tool result in increasing order, all held by one index of ctx, and no other block of that index appears in any row. Of the remaining entries of a row, at most 1 are held by any one index of ctx. For the 2 query blocks of each index of ctx (rows 2 d to 2 d + 1) there is an index of ctx from which each of them selects exactly 1 block.
All inputs are finite; a program needn't handle non-finite values.
Results may differ from a plain program's by a relative error of at most 0.0052.
Values may be sent and summed in bfloat16 or wider, within the bound.
No kernel may reach another device: no remote copies, remote signals or barrier semaphores. Data moves between devices by JAX's collectives and lax.ppermute only.
A program may use at most 64 MiB of HBM per device.

v0:
```python
import jax
import jax.numpy as jnp
from jax import lax
from jax.sharding import PartitionSpec as P

LAT = 512
ROPE = 64
VH = 128
HOT = 8


score_scale = 192.0 ** (-0.5)


def broadcast(x, axis, root):
    mine = lax.axis_index(axis) == root
    return lax.psum(jnp.where(mine, x, jnp.zeros_like(x)), axis)


def local(q_latent, q_rope, kv_latent, k_rope, selection, w_uv):
    owners = lax.axis_size("ctx")
    stored = kv_latent.shape[0]
    block_len = kv_latent.shape[1]
    query_blocks = selection.shape[0]
    chosen = selection.shape[1]
    cold_count = chosen - HOT
    per_owner = cold_count // (owners - 1) + 1
    slot_count = query_blocks * per_owner
    head_count = q_latent.shape[1] // LAT
    hot_ids = selection[0, :HOT]
    hot_owner = hot_ids[0] // stored
    hot_start = hot_ids[0] - hot_owner * stored
    hot_latent = lax.dynamic_slice_in_dim(kv_latent, hot_start, HOT, 0)
    hot_rope = lax.dynamic_slice_in_dim(k_rope, hot_start, HOT, 0)
    hot_latent, hot_rope = (
        broadcast(hot_latent, "ctx", hot_owner),
        broadcast(hot_rope, "ctx", hot_owner),
    )
    cold_ids = selection[:, HOT:]
    owner_ids = cold_ids // stored
    local_ids = cold_ids - owner_ids * stored
    same_owner = owner_ids[:, :, None] == owner_ids[:, None, :]
    earlier = jnp.arange(cold_count)[None, :] < jnp.arange(cold_count)[:, None]
    ranking = jnp.sum(same_owner & earlier[None], axis=2)
    slot_ids = jnp.arange(query_blocks, dtype=jnp.int32)[:, None] * per_owner + ranking
    matches = (owner_ids[None, None] == jnp.arange(owners)[:, None, None, None]) & (
        slot_ids[None, None] == jnp.arange(slot_count)[None, :, None, None]
    )
    wanted = jnp.sum(jnp.where(matches, local_ids[None, None], 0), axis=(2, 3))
    filled = jnp.any(matches, axis=(2, 3))
    requested = lax.all_to_all(wanted, "ctx", split_axis=0, concat_axis=0, tiled=True)
    sent_latent = kv_latent[requested]
    sent_rope = k_rope[requested]
    fetched_latent, fetched_rope = (
        lax.all_to_all(sent_latent, "ctx", split_axis=0, concat_axis=0, tiled=True),
        lax.all_to_all(sent_rope, "ctx", split_axis=0, concat_axis=0, tiled=True),
    )
    fetched_latent = fetched_latent.reshape(owners, query_blocks, per_owner, block_len, LAT)
    fetched_rope = fetched_rope.reshape(owners, query_blocks, per_owner, block_len * ROPE)
    filled = filled.reshape(owners, query_blocks, per_owner)
    query_latent = q_latent.reshape(query_blocks, block_len, head_count, LAT)
    query_rope = q_rope.reshape(query_blocks, block_len, head_count, ROPE)
    hot_keys = hot_latent.reshape(-1, LAT)
    hot_pos = hot_rope.reshape(-1, ROPE)
    results = []
    for member in range(query_blocks):
        cold_keys = fetched_latent[:, member].reshape(-1, LAT)
        cold_pos = fetched_rope[:, member].reshape(-1, ROPE)
        usable = jnp.broadcast_to(
            filled[:, member][:, :, None], (owners, per_owner, block_len)
        ).reshape(-1)
        hot_scores = jnp.einsum(
            "rhc,kc->hrk", query_latent[member], hot_keys, preferred_element_type=jnp.float32
        )
        hot_scores = (
            hot_scores
            + jnp.einsum(
                "rhe,ke->hrk", query_rope[member], hot_pos, preferred_element_type=jnp.float32
            )
        ) * score_scale
        cold_scores = jnp.einsum(
            "rhc,kc->hrk", query_latent[member], cold_keys, preferred_element_type=jnp.float32
        )
        cold_scores = (
            cold_scores
            + jnp.einsum(
                "rhe,ke->hrk", query_rope[member], cold_pos, preferred_element_type=jnp.float32
            )
        ) * score_scale
        cold_scores = jnp.where(usable[None, None, :], cold_scores, -jnp.inf)
        row_max = jnp.maximum(jnp.max(hot_scores, axis=2), jnp.max(cold_scores, axis=2))[:, :, None]
        hot_weights = jnp.exp(hot_scores - row_max)
        cold_weights = jnp.where(usable[None, None, :], jnp.exp(cold_scores - row_max), 0.0)
        row_total = jnp.sum(hot_weights, axis=2) + jnp.sum(cold_weights, axis=2)
        blended = jnp.einsum(
            "hrk,kc->hrc",
            hot_weights.astype(jnp.bfloat16),
            hot_keys,
            preferred_element_type=jnp.float32,
        )
        blended = blended + jnp.einsum(
            "hrk,kc->hrc",
            cold_weights.astype(jnp.bfloat16),
            cold_keys,
            preferred_element_type=jnp.float32,
        )
        latent_out = (blended / row_total[:, :, None]).astype(jnp.bfloat16)
        projected = jnp.einsum("hrc,hcv->rhv", latent_out, w_uv, preferred_element_type=jnp.float32)
        results.append(projected.reshape(block_len, head_count * VH))
    return jnp.concatenate(results, axis=0).astype(jnp.bfloat16)


def solution(mesh):
    in_specs = (
        P("ctx", "head"),
        P("ctx", "head"),
        P("ctx", None, None),
        P("ctx", None),
        P("ctx", None),
        P("head", None, None),
    )
    out_specs = P("ctx", "head")
    return jax.shard_map(local, mesh=mesh, in_specs=in_specs, out_specs=out_specs, check_vma=False)
```

profile of v0, /device:TPU:1, one launch (start us, length us, event | category | flops | bytes accessed | tf_op | source)
XLA Modules:
  0.0 388.7 jit_solution(5934805390018977635)
XLA Ops:
  6.5 0.9 multiply_subtract_fusion
  7.5 0.2 convert_reduce_fusion
  7.7 0.1 fusion.72
  7.8 0.1 copy.44
  7.9 28.3 %all_to_all.22 = s32[32,1,2]{2,1,0:T(1,128)S(1)} all-to-all(s32[32,1,2]{2,1,0:T(1,128)S(1)} %copy.44), channel_id=1, replica_groups=mesh['ctx'=32,'head'=16] {'ctx'}, dimensions={0} | all-to-all | bytes 512 | tf_op jit(solution)/shard_map/all_to_all | solution.py:51
  36.3 0.1 copy.45
  36.4 0.1 copy.46
  36.4 0.1 reshape.138
  36.6 2.3 gather_fusion.1
  38.9 1.1 reshape.145
  40.0 4.4 %all-to-all-start.2 = ((bf16[32,2,4096]{2,1,0:T(2,128)(2,1)}), bf16[32,2,4096]{2,1,0:T(2,128)(2,1)S(1)}, u32[]{:S(2)}, u32[]{:S(2)}) async-start(bf16[32,2,4096]{2,1,0:T(2,128)(2,1)} %reshape.145), calls=%async_computation.2 | async-start | bytes 1048576 | tf_op jit(solution)/shard_map/all_to_all | solution.py:56
  44.5 2.7 gather_fusion
  47.2 30.8 %all-to-all-done.2 = bf16[32,2,4096]{2,1,0:T(2,128)(2,1)S(1)} async-done(((bf16[32,2,4096]{2,1,0:T(2,128)(2,1)}), bf16[32,2,4096]{2,1,0:T(2,128)(2,1)S(1)}, u32[]{:S(2)}, u32[]{:S(2)}) %all-to-all-start.2) | async-done | bytes 524320 | tf_op jit(solution)/shard_map/all_to_all | solution.py:56
  78.0 5.4 %all-to-all-start.1 = ((bf16[32,2,64,512]{3,2,1,0:T(8,128)(2,1)}), bf16[32,2,64,512]{3,2,1,0:T(8,128)(2,1)}, u32[]{:S(2)}, u32[]{:S(2)}) async-start(bf16[32,2,64,512]{3,2,1,0:T(8,128)(2,1)} %bitcast.111), calls=%async_computation.1 | async-start | bytes 8388608 | tf_op jit(solution)/shard_map/all_to_all | solution.py:55
  83.4 0.2 all-reduce.3.cloned.1.call-start
  83.6 0.5 slice.48
  87.5 0.2 reshape.130
  87.6 0.7 copy.42
  88.4 0.9 dynamic-slice_select_fusion
  89.3 0.1 squeeze.25
  89.4 1.3 fusion.76
  90.7 0.1 and_reduce_fusion
  90.9 0.1 broadcast_in_dim.98
  91.0 0.1 squeeze.23
  91.2 0.1 broadcast_in_dim.89
  91.3 259.4 %all-reduce.3.cloned.1.call-done = (bf16[512,512]{1,0:T(8,128)(2,1)}, bf16[512,64]{0,1:T(8,128)(2,1)}) async-done(((bf16[512,512]{1,0:T(8,128)(2,1)}, bf16[512,64]{0,1:T(8,128)(2,1)}), (bf16[512,512]{1,0:T(8,128)(2,1)}, bf16[512,64]{0,1:T(8,128)(2,1)})) %all-reduce.3.cloned.1.call-update) | async-done | bytes 589840 | tf_op jit(solution)/shard_map/psum | solution.py:17
  350.7 1.5 fusion.42
  352.2 1.5 fusion.46
  353.7 1.3 fusion.78
  355.1 1.3 fusion.79
  356.3 3.0 slice_reduce_fusion.1
  359.4 1.5 reshape_squeeze.15
  360.8 1.5 reshape_squeeze.13
  362.3 2.5 fusion.75
  364.8 1.3 fusion.40
  366.1 0.9 bitcast_reduce_fusion
  367.1 2.4 fusion.8
  369.4 0.8 fusion.6
  370.2 1.3 fusion.44
  371.5 0.9 bitcast_reduce_fusion.1
  372.5 2.6 fusion.10
  375.0 0.8 fusion.4
  375.9 0.4 copy-done.4
  376.3 0.4 fusion.34
  376.6 0.4 fusion.32
  377.0 2.0 fusion.30
  379.1 2.0 fusion.31
  381.1 0.7 pad_maximum_fusion
  (33 shorter events, 0.4 us)
Async XLA Ops:
  6.5 370.5 %copy-start = (bf16[8,512,128]{2,1,0:T(8,128)(2,1)S(1)}, bf16[8,512,128]{2,1,0:T(8,128)(2,1)}, u32[]{:S(2)}) copy-start(bf16[8,512,128]{2,1,0:T(8,128)(2,1)} %param.11) | copy-start | bytes 3145732
  6.5 37.9 %copy-start.2 = (bf16[16,64,512]{2,1,0:T(8,128)(2,1)S(1)}, bf16[16,64,512]{2,1,0:T(8,128)(2,1)}, u32[]{:S(2)}) copy-start(bf16[16,64,512]{2,1,0:T(8,128)(2,1)} %param.8) | copy-start | bytes 3145732
  40.0 38.0 %all-to-all-start.2 = ((bf16[32,2,4096]{2,1,0:T(2,128)(2,1)}), bf16[32,2,4096]{2,1,0:T(2,128)(2,1)S(1)}, u32[]{:S(2)}, u32[]{:S(2)}) async-start(bf16[32,2,4096]{2,1,0:T(2,128)(2,1)} %reshape.145), calls=%async_computation.2 | async-start | bytes 1048576 | tf_op jit(solution)/shard_map/all_to_all | solution.py:56
  78.0 5.6 %copy-start.7 = (s32[2,32]{1,0:T(2,128)S(1)}, s32[2,32]{1,0:T(2,128)}, u32[]{:S(2)}) copy-start(s32[2,32]{1,0:T(2,128)} %param.10) | copy-start | bytes 772
  78.0 9.4 %copy-start.1 = (bf16[16,4096]{1,0:T(8,128)(2,1)S(1)}, bf16[16,4096]{1,0:T(8,128)(2,1)}, u32[]{:S(2)}) copy-start(bf16[16,4096]{1,0:T(8,128)(2,1)} %param.9) | copy-start | bytes 393220
  78.0 11.3 %copy-start.6 = (bf16[128,512]{1,0:T(8,128)(2,1)S(1)}, bf16[128,512]{1,0:T(8,128)(2,1)}, u32[]{:S(2)}) copy-start(bf16[128,512]{1,0:T(8,128)(2,1)} %param.7) | copy-start | bytes 393220
  78.0 284.3 %all-to-all-start.1 = ((bf16[32,2,64,512]{3,2,1,0:T(8,128)(2,1)}), bf16[32,2,64,512]{3,2,1,0:T(8,128)(2,1)}, u32[]{:S(2)}, u32[]{:S(2)}) async-start(bf16[32,2,64,512]{3,2,1,0:T(8,128)(2,1)} %bitcast.111), calls=%async_computation.1 | async-start | bytes 8388608 | tf_op jit(solution)/shard_map/all_to_all | solution.py:55
  83.4 267.3 %all-reduce.3.cloned.1.call-start = ((), (), s32[]{:S(2)}) async-start(), calls=%async_computation.3 | async-start | bytes 1179648 | tf_op jit(solution)/shard_map/psum | solution.py:17
  350.7 3.1 copy-start.5
  375.0 1.2 copy-start.4
  375.0 1.6 copy-start.3
Sparse Core Ops, SparseCore 0:
  89.4 261.2 all-reduce.2
where the time goes:
time: 390 us; the launch traced here: 389 us
  waiting for transfers between devices  290 us (74%)
  blocking collectives  28.3 us (7%)
  matrix products  19.1 us (5%)
  local copies, waits for them, and re-layouts  18.8 us (5%)
  between operations  16.9 us (4%)
  starting transfers between devices  10 us (3%)
  other arithmetic  5.41 us (1%)
    psum x1, waiting for transfers between devices, broadcast(): return lax.psum(jnp.where(mine, x, jnp.zeros_like(x)), axis)  259 us
    all_to_all x1, waiting for transfers between devices, local(): lax.all_to_all(sent_rope, 'ctx', split_axis=0, concat_axis=0, tiled=True)  30.8 us
    all_to_all x1, blocking collectives, local(): lax.all_to_all(wanted, 'ctx', split_axis=0, concat_axis=0, tiled=True)  28.3 us
  transfers between devices with their start and end apart: 3, of which 2 were waited for; matrix products, arithmetic and copies ran while one was open for 5% of the time, Pallas kernels for 0%

commit v1 on v0

v1 whole, which is shorter than its diff:
```python
import jax
import jax.numpy as jnp
from jax import lax
from jax.experimental import pallas as pl
from jax.experimental.pallas import tpu as pltpu
from jax.sharding import Mesh
from jax.sharding import PartitionSpec as P

LAT = 512
ROPE = 64
VH = 128
HOT = 8
WIDE = 640
SHARE = 8
QB = 64
HEADS = 8

SCORE_SCALE = 192.0 ** (-0.5)
LOG2E = 1.4426950408889634
VMEM_LIMIT = 56 * 1024 * 1024

bf16 = jnp.bfloat16
f32 = jnp.float32


def pick_kernel(index_ref, blocks_ref, hot_ref, out_ref):
    hot = hot_ref[...]
    for z in range(16):
        for c in range(2):
            out_ref[z, c] = blocks_ref[index_ref[z * 2 + c]]
        out_ref[z, 2] = hot


def compact_kernel(index_ref, got_ref, out_ref):
    for i in range(24):
        slot = index_ref[i]
        out_ref[i * 8 : i * 8 + 8, :] = got_ref[slot // 2, slot % 2]
    for i in range(8):
        out_ref[192 + i * 8 : 200 + i * 8, :] = jnp.concatenate(
            [got_ref[2 * i, 2, 0:4], got_ref[2 * i + 1, 2, 0:4]], axis=0
        )


def attend_kernel(q0_ref, q1_ref, mine_ref, other_ref, w0_ref, w1_ref, o0_ref, o1_ref, q_scr):
    zeros = jnp.zeros((QB, WIDE - LAT - ROPE), bf16)
    for r, q_ref in enumerate((q0_ref, q1_ref)):
        for h in range(HEADS):
            base = HEADS * LAT + h * ROPE
            rows = pl.ds((r * HEADS + h) * QB, QB)
            q_scr[rows, 0:LAT] = q_ref[:, h * LAT : (h + 1) * LAT]
            q_scr[rows, LAT:WIDE] = jnp.concatenate([q_ref[:, base : base + ROPE], zeros], axis=1)

    for r, (w_ref, o_ref) in enumerate(((w0_ref, o0_ref), (w1_ref, o1_ref))):
        for part in range(2):
            q = q_scr[(r * 2 + part) * 256 : (r * 2 + part + 1) * 256, :]
            scores = []
            for ref in (mine_ref, other_ref):
                for i in range(4):
                    scores.append(
                        lax.dot_general(
                            q, ref[i], (((1,), (1,)), ((), ())), preferred_element_type=f32
                        )
                    )
            top = scores[0]
            for s in scores[1:]:
                top = jnp.maximum(top, s)
            top = jnp.max(top, axis=1, keepdims=True) * (SCORE_SCALE * LOG2E)
            blended = jnp.zeros((256, LAT), f32)
            total = jnp.zeros((256, 256), f32)
            for n, ref in enumerate((mine_ref, other_ref)):
                for i in range(4):
                    w = jnp.exp2(scores[n * 4 + i] * (SCORE_SCALE * LOG2E) - top)
                    total = total + w
                    blended = blended + jnp.dot(
                        w.astype(bf16), ref[i, :, 0:LAT], preferred_element_type=f32
                    )
            total = jnp.sum(total, axis=1, keepdims=True)
            latent = (blended / total).astype(bf16)
            for n in range(4):
                h = part * 4 + n
                o_ref[:, h * VH : (h + 1) * VH] = jnp.dot(
                    latent[n * QB : (n + 1) * QB], w_ref[h], preferred_element_type=f32
                ).astype(bf16)


def local(q_latent, q_rope, kv_latent, k_rope, selection, w_uv):
    z, k, y, x = (lax.axis_index(a) for a in ("z", "core", "y", "x"))
    vmem = pl.BlockSpec(memory_space=pltpu.VMEM)
    smem = pl.BlockSpec(memory_space=pltpu.SMEM)

    def pairs(r):
        return [
            (c * 4 + s, (s // 2) * 4 + 2 * c + (s + r) % 2) for c in range(2) for s in range(4)
        ]

    queries, ups = [], []
    for r in range(2):
        m = (x + r) % 2
        part = jnp.concatenate(
            [
                lax.dynamic_slice_in_dim(q_latent, m * QB, QB, 0),
                lax.dynamic_slice_in_dim(q_rope, m * QB, QB, 0),
            ],
            axis=1,
        )
        queries.append(lax.ppermute(part, ("core", "x"), pairs(r)))
    for r in range(2):
        ups.append(lax.ppermute(w_uv, ("core", "x"), pairs(r)))

    lat = lax.dynamic_slice_in_dim(kv_latent, y * 16, 16, 1)
    rope = lax.dynamic_slice_in_dim(k_rope, y * 1024, 1024, 1).reshape(16, 16, ROPE)
    share = jnp.concatenate([lat, rope, jnp.zeros((16, 16, WIDE - LAT - ROPE), bf16)], axis=2)
    own = lax.dynamic_slice_in_dim(share, k * SHARE, SHARE, 1)
    theirs = lax.dynamic_slice_in_dim(share, (1 - k) * SHARE, SHARE, 1)
    swapped = lax.ppermute(theirs, "core", [(0, 1), (1, 0)])
    blocks = jnp.where(k == 0, jnp.stack([own, swapped]), jnp.stack([swapped, own]))
    blocks = blocks.reshape(32, SHARE, WIDE)

    hot_first = selection[0, 0]
    hot_owner = hot_first // 16
    hot = lax.dynamic_slice_in_dim(share, hot_first - hot_owner * 16, HOT, 0)
    hot = hot.reshape(8, 2, 2, 4, WIDE).transpose(0, 2, 1, 3, 4).reshape(32, 4, WIDE)
    cold = selection[:, HOT:]
    owner = cold // 16
    place = cold - owner * 16 + 1
    match = owner[:, :, None] == jnp.arange(32)[None, None, :]
    wants = jnp.sum(jnp.where(match, place[:, :, None], 0), axis=1)
    wants = wants.reshape(2, 16, 2).transpose(1, 0, 2).reshape(16, 1, 4)
    wants = jnp.broadcast_to(wants, (16, 2, 4)).reshape(32, 4)
    notes = jnp.concatenate(
        [
            wants,
            jnp.broadcast_to(owner.reshape(1, 48), (32, 48)),
            jnp.zeros((32, 76), jnp.int32),
        ],
        axis=1,
    ).astype(bf16)
    first = jnp.concatenate(
        [
            hot[:, :, :LAT].reshape(32, 16, 128),
            hot[:, :, LAT : LAT + ROPE].reshape(32, 2, 128),
            notes[:, None, :],
            jnp.zeros((32, 5, 128), bf16),
        ],
        axis=1,
    )
    first = lax.all_to_all(first, ("z", "core"), split_axis=0, concat_axis=0, tiled=True)

    relay = lax.dynamic_index_in_dim(first, hot_owner, 0, keepdims=False)
    relay = jnp.concatenate(
        [
            relay[:16].reshape(4, LAT),
            relay[16:18].reshape(4, ROPE),
            jnp.zeros((4, WIDE - LAT - ROPE), bf16),
        ],
        axis=1,
    )
    relay = jnp.concatenate([relay, relay], axis=0)
    notes = first[:, 18, :].reshape(16, 2, 128)
    notes = lax.dynamic_index_in_dim(notes, x // 2, 1, keepdims=False)
    wants = lax.dynamic_slice_in_dim(notes, (x % 2) * 2, 2, 1).astype(jnp.int32)
    wants = jnp.maximum(wants - 1, 0) + jnp.arange(2)[None, :] * 16
    owners = lax.dynamic_index_in_dim(notes, z, 0, keepdims=False)
    owners = lax.dynamic_slice_in_dim(owners, 4 + (x % 2) * 24, 24, 0).astype(jnp.int32)

    second = pl.pallas_call(
        pick_kernel,
        out_shape=jax.ShapeDtypeStruct((16, 3, SHARE, WIDE), bf16),
        in_specs=[smem, vmem, vmem],
        out_specs=vmem,
    )(wants.reshape(32), blocks, relay)
    second = lax.all_to_all(second, "z", split_axis=0, concat_axis=0, tiled=True)

    keys = pl.pallas_call(
        compact_kernel,
        out_shape=jax.ShapeDtypeStruct((256, WIDE), bf16),
        in_specs=[smem, vmem],
        out_specs=vmem,
    )(owners, second)
    keys = jnp.broadcast_to(keys[None], (4, 256, WIDE))
    keys = lax.all_to_all(keys, "y", split_axis=0, concat_axis=0, tiled=True)
    other = lax.ppermute(keys, "core", [(0, 1), (1, 0)])

    out = jax.ShapeDtypeStruct((QB, HEADS * VH), bf16)
    outs = pl.pallas_call(
        attend_kernel,
        out_shape=[out, out],
        in_specs=[vmem] * 6,
        out_specs=[vmem] * 2,
        scratch_shapes=[pltpu.VMEM((2 * HEADS * QB, WIDE), bf16)],
        compiler_params=pltpu.CompilerParams(vmem_limit_bytes=VMEM_LIMIT),
    )(queries[0], queries[1], keys, other, ups[0], ups[1])

    back = [
        lax.ppermute(outs[r], ("core", "x"), [(d, s) for s, d in pairs(r)]) for r in range(2)
    ]
    even = x % 2 == 0
    return jnp.concatenate(
        [jnp.where(even, back[0], back[1]), jnp.where(even, back[1], back[0])], axis=0
    )


def solution(mesh):
    grid = Mesh(mesh.devices.reshape(16, 2, 4, 4), ("z", "core", "y", "x"))
    ctx, head = ("z", "core"), ("y", "x")
    in_specs = (
        P(ctx, head),
        P(ctx, head),
        P(ctx, None, None),
        P(ctx, None),
        P(ctx, None),
        P(head, None, None),
    )
    return jax.shard_map(
        local, mesh=grid, in_specs=in_specs, out_specs=P(ctx, head), check_vma=False
    )
```

time: 390 us -> 157 us (0.40)
  waiting for transfers between devices: 290 us -> 59.9 us
  starting transfers between devices: 10 us -> 61.6 us
  blocking collectives: 28.3 us -> 0 us
  matrix products: 19.1 us -> 0 us
  Pallas kernels: 0 us -> 15.2 us
  between operations: 16.9 us -> 3.72 us
  local copies, waits for them, and re-layouts: 18.8 us -> 10.6 us
    psum x1 -> x0, waiting for transfers between devices: 259 us -> none  [broadcast(): return lax.psum(jnp.where(mine, x, jnp.zeros_like(x)), axis)]
    ppermute x0 -> x8, starting transfers between devices: none -> 36.9 us  [the longest x2 13 us: local(): ups.append(lax.ppermute(w_uv, ('core', 'x'), pairs(r)))]
    all_to_all x1 -> x0, blocking collectives: 28.3 us -> none  [local(): lax.all_to_all(wanted, 'ctx', split_axis=0, concat_axis=0, tiled=True)]
    ppermute x0 -> x8, waiting for transfers between devices: none -> 24.4 us  [the longest x2 17.8 us: local(): queries.append(lax.ppermute(part, ('core', 'x'), pairs(r)))]
    dot_general x12 -> x0, matrix products: 19.1 us -> none  [the longest x2 4.93 us: local(): jnp.einsum('hrk,kc->hrc', cold_weights.astype(jnp.bfloat16), cold_keys, p...]
    pallas_call x0 -> x3, Pallas kernels: none -> 15.2 us  [the longest x1 11.5 us: local(): pl.pallas_call(attend_kernel, out_shape=[out, out], in_specs=[vmem] * 6,...]
    all_to_all x2 -> x3, starting transfers between devices: 9.82 us -> 24.6 us  [the longest x1 16.7 us: local(): lax.all_to_all(first, ('z', 'core'), split_axis=0, concat_axis=0, tiled=T...]
    gather x3 -> x0, local copies, waits for them, and re-layouts: 6.17 us -> none  [the longest x2 3.43 us: local(): sent_rope = k_rope[requested]]
  transfers between devices with their start and end apart: 3 -> 11, of which waited for: 2 -> 7; matrix products, arithmetic and copies ran while one was open for 5% -> 2% of each run, Pallas kernels for 0% -> 0%
where the time goes in v1:
time: 157 us; the launch traced here: 156 us
  starting transfers between devices  61.6 us (39%)
  waiting for transfers between devices  59.9 us (38%)
  Pallas kernels  15.2 us (10%)
  local copies, waits for them, and re-layouts  10.6 us (7%)
  other arithmetic  4.59 us (3%)
  between operations  3.72 us (2%)
    all_to_all x1, waiting for transfers between devices, local(): lax.all_to_all(second, 'z', split_axis=0, concat_axis=0, tiled=True)  21 us
    ppermute x2, waiting for transfers between devices, local(): queries.append(lax.ppermute(part, ('core', 'x'), pairs(r)))  17.8 us
    all_to_all x1, starting transfers between devices, local(): lax.all_to_all(first, ('z', 'core'), split_axis=0, concat_axis=0, tiled=T...  16.7 us
    all_to_all x1, waiting for transfers between devices, local(): lax.all_to_all(first, ('z', 'core'), split_axis=0, concat_axis=0, tiled=T...  14.4 us
    ppermute x2, starting transfers between devices, local(): ups.append(lax.ppermute(w_uv, ('core', 'x'), pairs(r)))  13 us
    pallas_call x1, Pallas kernels, local(): pl.pallas_call(attend_kernel, out_shape=[out, out], in_specs=[vmem] * 6,...  11.5 us
    ppermute x1, starting transfers between devices, local(): other = lax.ppermute(keys, 'core', [(0, 1), (1, 0)])  8.28 us
    ppermute x2, starting transfers between devices, local(): lax.ppermute(outs[r], ('core', 'x'), [(d, s) for s, d in pairs(r)])  6.75 us
  transfers between devices with their start and end apart: 11, of which 7 were waited for; matrix products, arithmetic and copies ran while one was open for 2% of the time, Pallas kernels for 0%

profile of v1, /device:TPU:1, one launch (start us, length us, event | category | flops | bytes accessed | tf_op | source)
XLA Modules:
  0.0 155.7 jit_solution(17080924241833957928)
XLA Ops:
  0.0 1.3 slice.23
  4.5 0.8 fusion
  5.3 0.8 constant_dynamic-slice_fusion.4
  6.1 0.1 reshape.112
  6.3 0.2 copy.29
  6.9 0.1 reshape.130
  7.1 0.1 select_reduce_fusion
  7.2 0.1 pad.16.clone
  7.3 0.1 reshape.123
  7.4 0.1 copy.24
  7.5 0.1 copy.25
  7.7 0.1 reshape.116
  7.8 0.8 maximum_maximum_fusion.1
  8.6 16.7 %all-to-all-start = ((bf16[32,24,128]{2,1,0:T(8,128)(2,1)}), bf16[32,24,128]{2,1,0:T(8,128)(2,1)S(1)}, u32[]{:S(2)}, u32[]{:S(2)}) async-start(bf16[32,24,128]{2,1,0:T(8,128)(2,1)} %maximum_maximum_fusion.1), calls=%async_computation | async-start | bytes 393216 | tf_op jit(solution)/shard_map/all_to_all | solution.py:147
  25.4 2.1 %collective-permute-start.2 = (bf16[16,8,640]{2,0,1:T(8,128)(2,1)S(1)}, bf16[16,8,640]{2,0,1:T(8,128)(2,1)S(1)}, u32[]{:S(2)}, u32[]{:S(2)}) collective-permute-start(bf16[16,8,640]{2,0,1:T(8,128)(2,1)S(1)} %get-tuple-element.14), channel_id=1, source_target_pairs={{0,16},{16,0},{1,17},{17,1},{2,18},{18,2},{3,19},{19,3},{4,20},{20... | collective-permute-start | bytes 491528 | tf_op jit(solution)/shard_map/ppermute | solution.py:115
  27.6 0.1 add.100
  27.7 1.0 collective-permute-done.2
  28.7 0.8 copy.27
  29.5 14.4 %all-to-all-done = bf16[32,24,128]{2,1,0:T(8,128)(2,1)S(1)} async-done(((bf16[32,24,128]{2,1,0:T(8,128)(2,1)}), bf16[32,24,128]{2,1,0:T(8,128)(2,1)S(1)}, u32[]{:S(2)}, u32[]{:S(2)}) %all-to-all-start) | async-done | bytes 196640 | tf_op jit(solution)/shard_map/all_to_all | solution.py:147
  44.0 0.1 reshape.119
  44.1 0.1 maximum_reduce_fusion
  44.2 0.1 max.12
  44.3 0.5 add.101.index_ref
  44.9 0.7 maximum_maximum_fusion.2.hot_ref
  45.5 1.8 %shard_map.64 = bf16[16,3,8,640]{3,2,1,0:T(8,128)(2,1)} custom-call(s32[32]{0:T(128)} %add.101.index_ref, bf16[32,8,640]{2,1,0:T(8,128)(2,1)} %bitcast.16, bf16[8,640]{1,0:T(8,128)(2,1)} %maximum_maximum_fusion.2.hot_ref), custom_call_target="tpu_custom_call" | custom-call | tf_op jit(solution)/shard_map/pallas_call | solution.py:166
  47.4 3.6 %all-to-all-start.1 = ((bf16[16,3,8,640]{3,2,1,0:T(8,128)(2,1)}), bf16[16,3,8,640]{3,2,1,0:T(8,128)(2,1)S(1)}, u32[]{:S(2)}, u32[]{:S(2)}) async-start(bf16[16,3,8,640]{3,2,1,0:T(8,128)(2,1)} %shard_map.64), calls=%async_computation.1 | async-start | bytes 983040 | tf_op jit(solution)/shard_map/all_to_all | solution.py:172
  50.9 0.6 bitcast_convert_fusion.index_ref
  51.5 21.0 %all-to-all-done.1.got_ref = bf16[16,3,8,640]{3,2,1,0:T(8,128)(2,1)S(1)} async-done(((bf16[16,3,8,640]{3,2,1,0:T(8,128)(2,1)}), bf16[16,3,8,640]{3,2,1,0:T(8,128)(2,1)S(1)}, u32[]{:S(2)}, u32[]{:S(2)}) %all-to-all-start.1) | async-done | bytes 491552 | tf_op jit(solution)/shard_map/all_to_all | solution.py:172
  72.6 0.8 copy-done.2
  73.4 1.9 %shard_map.65 = bf16[256,640]{1,0:T(8,128)(2,1)} custom-call(s32[24]{0:T(128)} %bitcast_convert_fusion.index_ref, bf16[16,3,8,640]{3,2,1,0:T(8,128)(2,1)} %copy-done.2), custom_call_target="tpu_custom_call" | custom-call | tf_op jit(solution)/shard_map/pallas_call | solution.py:174
  75.3 2.1 %broadcast_in_dim.59 = bf16[4,256,640]{2,1,0:T(8,128)(2,1)} broadcast(bf16[256,640]{1,0:T(8,128)(2,1)} %shard_map.65), dimensions={1,2} | broadcast | bytes 1638400 | tf_op jit(solution)/shard_map/broadcast_in_dim | solution.py:180
  77.4 4.3 %all-to-all-start.2 = ((bf16[4,256,640]{2,1,0:T(8,128)(2,1)}), bf16[4,256,640]{2,1,0:T(8,128)(2,1)S(1)}, u32[]{:S(2)}, u32[]{:S(2)}) async-start(bf16[4,256,640]{2,1,0:T(8,128)(2,1)} %broadcast_in_dim.59), calls=%async_computation.2 | async-start | bytes 2621440 | tf_op jit(solution)/shard_map/all_to_all | solution.py:181
  81.8 10.8 %collective-permute-start.5 = (bf16[8,512,128]{2,1,0:T(8,128)(2,1)}, bf16[8,512,128]{2,1,0:T(8,128)(2,1)}, u32[]{:S(2)}, u32[]{:S(2)}) collective-permute-start(bf16[8,512,128]{2,1,0:T(8,128)(2,1)} %param.11), channel_id=1, source_target_pairs={{0,1},{1,0},{2,17},{3,16},{16,3},{17,2},{18,19},{19,18},{4,5},{5,4... | collective-permute-start | bytes 3145736 | tf_op jit(solution)/shard_map/ppermute | solution.py:108
  92.6 2.2 %collective-permute-start.4 = (bf16[8,512,128]{2,1,0:T(8,128)(2,1)}, bf16[8,512,128]{2,1,0:T(8,128)(2,1)}, u32[]{:S(2)}, u32[]{:S(2)}) collective-permute-start(bf16[8,512,128]{2,1,0:T(8,128)(2,1)} %param.11), channel_id=1, source_target_pairs={{0,0},{1,1},{2,16},{3,17},{16,2},{17,3},{18,18},{19,19},{4,4},{5,5... | collective-permute-start | bytes 3145736 | tf_op jit(solution)/shard_map/ppermute | solution.py:108
  94.9 1.3 constant_dynamic-slice_fusion.7
  96.2 8.3 %collective-permute-start.3 = (bf16[4,256,640]{2,1,0:T(8,128)(2,1)S(1)}, bf16[4,256,640]{2,1,0:T(8,128)(2,1)S(1)}, u32[]{:S(2)}, u32[]{:S(2)}) collective-permute-start(bf16[4,256,640]{2,1,0:T(8,128)(2,1)S(1)} %all-to-all-done.2.mine_ref), channel_id=1, source_target_pairs={{0,16},{16,0},{1,17},{17,1},{2,18},{18,2},{3,19},{19,3},{4,20},{20... | collective-permute-start | bytes 3932168 | tf_op jit(solution)/shard_map/ppermute | solution.py:182
  104.5 2.6 %collective-permute-start = (bf16[64,4608]{1,0:T(8,128)(2,1)S(1)}, bf16[64,4608]{1,0:T(8,128)(2,1)S(1)}, u32[]{:S(2)}, u32[]{:S(2)}) collective-permute-start(bf16[64,4608]{1,0:T(8,128)(2,1)S(1)} %pad_maximum_fusion), channel_id=1, source_target_pairs={{0,0},{1,1},{2,16},{3,17},{16,2},{17,3},{18,18},{19,19},{4,4},{5,5... | collective-permute-start | bytes 1769480 | tf_op jit(solution)/shard_map/ppermute | solution.py:106
  107.2 4.1 %collective-permute-start.1 = (bf16[64,4608]{1,0:T(8,128)(2,1)S(1)}, bf16[64,4608]{1,0:T(8,128)(2,1)S(1)}, u32[]{:S(2)}, u32[]{:S(2)}) collective-permute-start(bf16[64,4608]{1,0:T(8,128)(2,1)S(1)} %pad_maximum_fusion.1), channel_id=1, source_target_pairs={{0,1},{1,0},{2,17},{3,16},{16,3},{17,2},{18,19},{19,18},{4,5},{5,4... | collective-permute-start | bytes 1769480 | tf_op jit(solution)/shard_map/ppermute | solution.py:106
  111.3 16.4 %collective-permute-done.q0_ref = bf16[64,4608]{1,0:T(8,128)(2,1)S(1)} collective-permute-done((bf16[64,4608]{1,0:T(8,128)(2,1)S(1)}, bf16[64,4608]{1,0:T(8,128)(2,1)S(1)}, u32[]{:S(2)}, u32[]{:S(2)}) %collective-permute-start) | collective-permute-done | bytes 589856 | tf_op jit(solution)/shard_map/ppermute | solution.py:106
  127.7 1.4 collective-permute-done.1.q1_ref
  129.2 0.8 copy-done.5
  130.0 1.1 copy-done.3
  131.0 11.5 %shard_map.66 = (bf16[64,1024]{1,0:T(8,128)(2,1)}, bf16[64,1024]{1,0:T(8,128)(2,1)}) custom-call(bf16[64,4608]{1,0:T(8,128)(2,1)} %copy-done.4, bf16[64,4608]{1,0:T(8,128)(2,1)} %copy-done.5, bf16[4,256,640]{2,1,0:T(8,128)(2,1)} %copy-done.1, bf16[4,256,640]{2,1,0:T(8,128)(2,1)} %copy-done.3, bf16[8,512,128]{2,1,0:T(8,128)(2,1)} %collective-permute-done.4.w0_ref, ...), custom_call_target="tpu_custom_call" | custom-call | tf_op jit(solution)/shard_map/pallas_call | solution.py:185
  142.6 4.7 %collective-permute-start.6 = (bf16[64,1024]{1,0:T(8,128)(2,1)}, bf16[64,1024]{1,0:T(8,128)(2,1)S(1)}, u32[]{:S(2)}, u32[]{:S(2)}) collective-permute-start(bf16[64,1024]{1,0:T(8,128)(2,1)} %get-tuple-element.7), channel_id=1, source_target_pairs={{0,0},{1,1},{16,2},{17,3},{2,16},{3,17},{18,18},{19,19},{4,4},{5,5... | collective-permute-start | bytes 393224 | tf_op jit(solution)/shard_map/ppermute | solution.py:195
  147.2 2.1 %collective-permute-start.7 = (bf16[64,1024]{1,0:T(8,128)(2,1)}, bf16[64,1024]{1,0:T(8,128)(2,1)S(1)}, u32[]{:S(2)}, u32[]{:S(2)}) collective-permute-start(bf16[64,1024]{1,0:T(8,128)(2,1)} %get-tuple-element.8), channel_id=1, source_target_pairs={{1,0},{0,1},{17,2},{16,3},{3,16},{2,17},{19,18},{18,19},{5,4},{4,5... | collective-permute-start | bytes 393224 | tf_op jit(solution)/shard_map/ppermute | solution.py:195
  149.3 1.2 collective-permute-done.6
  150.5 4.4 %collective-permute-done.7 = bf16[64,1024]{1,0:T(8,128)(2,1)S(1)} collective-permute-done((bf16[64,1024]{1,0:T(8,128)(2,1)}, bf16[64,1024]{1,0:T(8,128)(2,1)S(1)}, u32[]{:S(2)}, u32[]{:S(2)}) %collective-permute-start.7) | collective-permute-done | bytes 131104 | tf_op jit(solution)/shard_map/ppermute | solution.py:195
  154.9 0.7 pad_maximum_fusion.2
  (49 shorter events, 1.0 us)
Async XLA Ops:
  0.0 6.2 %copy-start = (bf16[16,64,512]{2,1,0:T(8,128)(2,1)S(1)}, bf16[16,64,512]{2,1,0:T(8,128)(2,1)}, u32[]{:S(2)}) copy-start(bf16[16,64,512]{2,1,0:T(8,128)(2,1)} %param.8) | copy-start | bytes 3145732
  6.2 0.7 copy-start.7
  8.6 35.4 %all-to-all-start = ((bf16[32,24,128]{2,1,0:T(8,128)(2,1)}), bf16[32,24,128]{2,1,0:T(8,128)(2,1)S(1)}, u32[]{:S(2)}, u32[]{:S(2)}) async-start(bf16[32,24,128]{2,1,0:T(8,128)(2,1)} %maximum_maximum_fusion.1), calls=%async_computation | async-start | bytes 393216 | tf_op jit(solution)/shard_map/all_to_all | solution.py:147
  25.4 3.3 %collective-permute-start.2 = (bf16[16,8,640]{2,0,1:T(8,128)(2,1)S(1)}, bf16[16,8,640]{2,0,1:T(8,128)(2,1)S(1)}, u32[]{:S(2)}, u32[]{:S(2)}) collective-permute-start(bf16[16,8,640]{2,0,1:T(8,128)(2,1)S(1)} %get-tuple-element.14), channel_id=1, source_target_pairs={{0,16},{16,0},{1,17},{17,1},{2,18},{18,2},{3,19},{19,3},{4,20},{20... | collective-permute-start | bytes 491528 | tf_op jit(solution)/shard_map/ppermute | solution.py:115
  47.4 25.2 %all-to-all-start.1 = ((bf16[16,3,8,640]{3,2,1,0:T(8,128)(2,1)}), bf16[16,3,8,640]{3,2,1,0:T(8,128)(2,1)S(1)}, u32[]{:S(2)}, u32[]{:S(2)}) async-start(bf16[16,3,8,640]{3,2,1,0:T(8,128)(2,1)} %shard_map.64), calls=%async_computation.1 | async-start | bytes 983040 | tf_op jit(solution)/shard_map/all_to_all | solution.py:172
  72.6 0.8 copy-start.2
  77.4 17.4 %copy-start.6 = (bf16[128,512]{1,0:T(8,128)(2,1)S(1)}, bf16[128,512]{1,0:T(8,128)(2,1)}, u32[]{:S(2)}) copy-start(bf16[128,512]{1,0:T(8,128)(2,1)} %param.7) | copy-start | bytes 393220
  77.4 18.7 %all-to-all-start.2 = ((bf16[4,256,640]{2,1,0:T(8,128)(2,1)}), bf16[4,256,640]{2,1,0:T(8,128)(2,1)S(1)}, u32[]{:S(2)}, u32[]{:S(2)}) async-start(bf16[4,256,640]{2,1,0:T(8,128)(2,1)} %broadcast_in_dim.59), calls=%async_computation.2 | async-start | bytes 2621440 | tf_op jit(solution)/shard_map/all_to_all | solution.py:181
  81.8 47.4 %collective-permute-start.5 = (bf16[8,512,128]{2,1,0:T(8,128)(2,1)}, bf16[8,512,128]{2,1,0:T(8,128)(2,1)}, u32[]{:S(2)}, u32[]{:S(2)}) collective-permute-start(bf16[8,512,128]{2,1,0:T(8,128)(2,1)} %param.11), channel_id=1, source_target_pairs={{0,1},{1,0},{2,17},{3,16},{16,3},{17,2},{18,19},{19,18},{4,5},{5,4... | collective-permute-start | bytes 3145736 | tf_op jit(solution)/shard_map/ppermute | solution.py:108
  92.6 36.6 %collective-permute-start.4 = (bf16[8,512,128]{2,1,0:T(8,128)(2,1)}, bf16[8,512,128]{2,1,0:T(8,128)(2,1)}, u32[]{:S(2)}, u32[]{:S(2)}) collective-permute-start(bf16[8,512,128]{2,1,0:T(8,128)(2,1)} %param.11), channel_id=1, source_target_pairs={{0,0},{1,1},{2,16},{3,17},{16,2},{17,3},{18,18},{19,19},{4,4},{5,5... | collective-permute-start | bytes 3145736 | tf_op jit(solution)/shard_map/ppermute | solution.py:108
  96.2 11.0 %copy-start.1 = (bf16[4,256,640]{2,1,0:T(8,128)(2,1)}, bf16[4,256,640]{2,1,0:T(8,128)(2,1)S(1)}, u32[]{:S(2)}) copy-start(bf16[4,256,640]{2,1,0:T(8,128)(2,1)S(1)} %all-to-all-done.2.mine_ref) | copy-start | bytes 3932164
  96.2 33.0 %collective-permute-start.3 = (bf16[4,256,640]{2,1,0:T(8,128)(2,1)S(1)}, bf16[4,256,640]{2,1,0:T(8,128)(2,1)S(1)}, u32[]{:S(2)}, u32[]{:S(2)}) collective-permute-start(bf16[4,256,640]{2,1,0:T(8,128)(2,1)S(1)} %all-to-all-done.2.mine_ref), channel_id=1, source_target_pairs={{0,16},{16,0},{1,17},{17,1},{2,18},{18,2},{3,19},{19,3},{4,20},{20... | collective-permute-start | bytes 3932168 | tf_op jit(solution)/shard_map/ppermute | solution.py:182
  104.5 23.2 %collective-permute-start = (bf16[64,4608]{1,0:T(8,128)(2,1)S(1)}, bf16[64,4608]{1,0:T(8,128)(2,1)S(1)}, u32[]{:S(2)}, u32[]{:S(2)}) collective-permute-start(bf16[64,4608]{1,0:T(8,128)(2,1)S(1)} %pad_maximum_fusion), channel_id=1, source_target_pairs={{0,0},{1,1},{2,16},{3,17},{16,2},{17,3},{18,18},{19,19},{4,4},{5,5... | collective-permute-start | bytes 1769480 | tf_op jit(solution)/shard_map/ppermute | solution.py:106
  107.2 22.0 %collective-permute-start.1 = (bf16[64,4608]{1,0:T(8,128)(2,1)S(1)}, bf16[64,4608]{1,0:T(8,128)(2,1)S(1)}, u32[]{:S(2)}, u32[]{:S(2)}) collective-permute-start(bf16[64,4608]{1,0:T(8,128)(2,1)S(1)} %pad_maximum_fusion.1), channel_id=1, source_target_pairs={{0,1},{1,0},{2,17},{3,16},{16,3},{17,2},{18,19},{19,18},{4,5},{5,4... | collective-permute-start | bytes 1769480 | tf_op jit(solution)/shard_map/ppermute | solution.py:106
  127.7 1.5 copy-start.4
  129.2 0.8 copy-start.5
  130.0 1.1 copy-start.3
  142.6 8.0 %collective-permute-start.6 = (bf16[64,1024]{1,0:T(8,128)(2,1)}, bf16[64,1024]{1,0:T(8,128)(2,1)S(1)}, u32[]{:S(2)}, u32[]{:S(2)}) collective-permute-start(bf16[64,1024]{1,0:T(8,128)(2,1)} %get-tuple-element.7), channel_id=1, source_target_pairs={{0,0},{1,1},{16,2},{17,3},{2,16},{3,17},{18,18},{19,19},{4,4},{5,5... | collective-permute-start | bytes 393224 | tf_op jit(solution)/shard_map/ppermute | solution.py:195
  147.2 7.7 %collective-permute-start.7 = (bf16[64,1024]{1,0:T(8,128)(2,1)}, bf16[64,1024]{1,0:T(8,128)(2,1)S(1)}, u32[]{:S(2)}, u32[]{:S(2)}) collective-permute-start(bf16[64,1024]{1,0:T(8,128)(2,1)} %get-tuple-element.8), channel_id=1, source_target_pairs={{1,0},{0,1},{17,2},{16,3},{3,16},{2,17},{19,18},{18,19},{5,4},{4,5... | collective-permute-start | bytes 393224 | tf_op jit(solution)/shard_map/ppermute | solution.py:195

commit v2 on v1

v2 whole, which is shorter than its diff:
```python
import jax
import jax.numpy as jnp
from jax import lax
from jax.experimental import pallas as pl
from jax.experimental.pallas import tpu as pltpu
from jax.sharding import Mesh
from jax.sharding import PartitionSpec as P

LAT = 512
ROPE = 64
VH = 128
HOT = 8
WIDE = 640
SHARE = 8
QB = 64
HEADS = 8

SCORE_SCALE = 192.0 ** (-0.5)
LOG2E = 1.4426950408889634
VMEM_LIMIT = 56 * 1024 * 1024

bf16 = jnp.bfloat16
f32 = jnp.float32


def pick_kernel(index_ref, blocks_ref, hot_ref, out_ref):
    hot = hot_ref[...]
    for z in range(16):
        for c in range(2):
            out_ref[z, c] = blocks_ref[index_ref[z * 2 + c]]
        out_ref[z, 2] = hot


def compact_kernel(index_ref, got_ref, out_ref):
    for i in range(24):
        slot = index_ref[i]
        out_ref[i * 8 : i * 8 + 8, :] = got_ref[slot // 2, slot % 2]
    for i in range(8):
        out_ref[192 + i * 8 : 200 + i * 8, :] = jnp.concatenate(
            [got_ref[2 * i, 2, 0:4], got_ref[2 * i + 1, 2, 0:4]], axis=0
        )


def layout_kernel(q_ref, out_ref):
    zeros = jnp.zeros((QB, WIDE - LAT - ROPE), bf16)
    for h in range(HEADS):
        base = HEADS * LAT + h * ROPE
        rows = pl.ds(h * QB, QB)
        out_ref[rows, 0:LAT] = q_ref[:, h * LAT : (h + 1) * LAT]
        out_ref[rows, LAT:WIDE] = jnp.concatenate([q_ref[:, base : base + ROPE], zeros], axis=1)


def attend_kernel(q_ref, *refs):
    pieces, w_ref, o_ref = refs[:8], refs[8], refs[9]
    q = q_ref[...]
    scores = [
        lax.dot_general(q, piece[...], (((1,), (1,)), ((), ())), preferred_element_type=f32)
        for piece in pieces
    ]
    top = scores[0]
    for s in scores[1:]:
        top = jnp.maximum(top, s)
    top = jnp.max(top, axis=1, keepdims=True) * (SCORE_SCALE * LOG2E)
    blended = jnp.zeros((HEADS * QB, LAT), f32)
    total = jnp.zeros((HEADS * QB, 256), f32)
    for s, piece in zip(scores, pieces):
        w = jnp.exp2(s * (SCORE_SCALE * LOG2E) - top)
        total = total + w
        blended = blended + jnp.dot(w.astype(bf16), piece[:, 0:LAT], preferred_element_type=f32)
    total = jnp.sum(total, axis=1, keepdims=True)
    latent = (blended / total).astype(bf16)
    for h in range(HEADS):
        o_ref[:, h * VH : (h + 1) * VH] = jnp.dot(
            latent[h * QB : (h + 1) * QB], w_ref[h], preferred_element_type=f32
        ).astype(bf16)


def local(q_latent, q_rope, kv_latent, k_rope, selection, w_uv):
    z, k, y, x = (lax.axis_index(a) for a in ("z", "core", "y", "x"))
    vmem = pl.BlockSpec(memory_space=pltpu.VMEM)
    smem = pl.BlockSpec(memory_space=pltpu.SMEM)
    params = pltpu.CompilerParams(vmem_limit_bytes=VMEM_LIMIT)
    swap = [(0, 1), (1, 0)]

    def pairs(r):
        return [
            (c * 4 + s, (s // 2) * 4 + 2 * c + (s + r) % 2) for c in range(2) for s in range(4)
        ]

    queries, ups = [], []
    for r in range(2):
        m = (x + r) % 2
        part = jnp.concatenate(
            [
                lax.dynamic_slice_in_dim(q_latent, m * QB, QB, 0),
                lax.dynamic_slice_in_dim(q_rope, m * QB, QB, 0),
            ],
            axis=1,
        )
        queries.append(lax.ppermute(part, ("core", "x"), pairs(r)))
    for r in range(2):
        ups.append(lax.ppermute(w_uv, ("core", "x"), pairs(r)))

    lat = lax.dynamic_slice_in_dim(kv_latent, y * 16, 16, 1)
    rope = lax.dynamic_slice_in_dim(k_rope, y * 1024, 1024, 1).reshape(16, 16, ROPE)
    share = jnp.concatenate([lat, rope, jnp.zeros((16, 16, WIDE - LAT - ROPE), bf16)], axis=2)
    own = lax.dynamic_slice_in_dim(share, k * SHARE, SHARE, 1)
    theirs = lax.dynamic_slice_in_dim(share, (1 - k) * SHARE, SHARE, 1)
    hot_first = jnp.max(selection[:, 0])
    cold = selection[:, HOT:]
    notes = jnp.concatenate([cold >> 4, cold & 15], axis=1).astype(bf16)
    notes = jnp.pad(notes, ((0, 6), (0, WIDE - 48)))
    swapped = lax.ppermute(jnp.concatenate([theirs, notes[None]], axis=0), "core", swap)
    blocks = jnp.where(
        k == 0, jnp.concatenate([own, swapped[:16]]), jnp.concatenate([swapped[:16], own])
    )
    notes = jnp.where(x // 2 == k, notes, swapped[16])
    notes = jnp.where(x % 2 == 0, notes[0, :48], notes[1, :48]).astype(jnp.int32)
    owners, places = notes[:24], notes[24:]

    match = owners[None, :] == jnp.arange(32)[:, None]
    wants = jnp.sum(jnp.where(match, places[None, :], 0), axis=1).reshape(16, 1, 2)
    hot = lax.dynamic_slice_in_dim(blocks, hot_first & 31, HOT, 0).reshape(16, 4, WIDE)
    first = jnp.concatenate(
        [
            hot[:, :, :LAT].reshape(16, 16, 128),
            hot[:, :, LAT : LAT + ROPE].reshape(16, 2, 128),
            jnp.pad(wants.astype(bf16), ((0, 0), (0, 5), (0, 126))),
        ],
        axis=1,
    )
    first = lax.all_to_all(first, "z", split_axis=0, concat_axis=0, tiled=True)
    first, ups[0] = lax.optimization_barrier((first, ups[0]))

    relay = lax.dynamic_index_in_dim(first, hot_first >> 5, 0, keepdims=False)
    relay = jnp.concatenate(
        [
            relay[:16].reshape(4, LAT),
            relay[16:18].reshape(4, ROPE),
            jnp.zeros((4, WIDE - LAT - ROPE), bf16),
        ],
        axis=1,
    )
    relay = jnp.concatenate([relay, relay], axis=0)
    wants = first[:, 18, 0:2].astype(jnp.int32) + jnp.arange(2)[None, :] * 16

    second = pl.pallas_call(
        pick_kernel,
        out_shape=jax.ShapeDtypeStruct((16, 3, SHARE, WIDE), bf16),
        in_specs=[smem, vmem, vmem],
        out_specs=vmem,
    )(wants.reshape(32), blocks, relay)
    second = lax.all_to_all(second, "z", split_axis=0, concat_axis=0, tiled=True)
    second, queries, ups[1] = lax.optimization_barrier((second, queries, ups[1]))

    mine = pl.pallas_call(
        compact_kernel,
        out_shape=jax.ShapeDtypeStruct((256, WIDE), bf16),
        in_specs=[smem, vmem],
        out_specs=vmem,
    )(owners, second)
    keys = [mine]
    for step in (1, 3, 2):
        keys.append(lax.ppermute(mine, "y", [(i, (i + step) % 4) for i in range(4)]))
    keys = keys + [lax.ppermute(piece, "core", swap) for piece in keys]

    outs = []
    for r in range(2):
        q = pl.pallas_call(
            layout_kernel,
            out_shape=jax.ShapeDtypeStruct((HEADS * QB, WIDE), bf16),
            in_specs=[vmem],
            out_specs=vmem,
        )(queries[r])
        out = pl.pallas_call(
            attend_kernel,
            out_shape=jax.ShapeDtypeStruct((QB, HEADS * VH), bf16),
            in_specs=[vmem] * 10,
            out_specs=vmem,
            compiler_params=params,
        )(q, *keys, ups[r])
        outs.append(lax.ppermute(out, ("core", "x"), [(d, s) for s, d in pairs(r)]))
    even = x % 2 == 0
    return jnp.concatenate(
        [jnp.where(even, outs[0], outs[1]), jnp.where(even, outs[1], outs[0])], axis=0
    )


def solution(mesh):
    grid = Mesh(mesh.devices.reshape(16, 2, 4, 4), ("z", "core", "y", "x"))
    ctx, head = ("z", "core"), ("y", "x")
    in_specs = (
        P(ctx, head),
        P(ctx, head),
        P(ctx, None, None),
        P(ctx, None),
        P(ctx, None),
        P(head, None, None),
    )
    return jax.shard_map(
        local, mesh=grid, in_specs=in_specs, out_specs=P(ctx, head), check_vma=False
    )
```

time: 157 us -> 139 us (0.89)
  waiting for transfers between devices: 59.9 us -> 30.9 us
  starting transfers between devices: 61.6 us -> 70.9 us
  Pallas kernels: 15.2 us -> 20.9 us
  local copies, waits for them, and re-layouts: 10.6 us -> 7.62 us
  between operations: 3.72 us -> 1.84 us
    all_to_all x1, waiting for transfers between devices: 21 us -> 0.01 us  [local(): lax.all_to_all(second, 'z', split_axis=0, concat_axis=0, tiled=True)]
    ppermute x4 -> x10, starting transfers between devices: 17.2 us -> 37.5 us  [the longest x4 15.2 us: local(): keys = keys + [lax.ppermute(piece, 'core', swap) for piece in keys]]
    all_to_all x2 -> x1, starting transfers between devices: 21.1 us -> 12.3 us  [local(): first = lax.all_to_all(first, 'z', split_axis=0, concat_axis=0, tiled=True)]
    pallas_call x1 -> x4, Pallas kernels: 11.5 us -> 17.2 us  [the longest x2 13.2 us: local(): pl.pallas_call(attend_kernel, out_shape=jax.ShapeDtypeStruct((QB, HEADS *...]
    ppermute x2, starting transfers between devices: 13 us -> 8.08 us  [local(): ups.append(lax.ppermute(w_uv, ('core', 'x'), pairs(r)))]
    all_to_all x2 -> x1, waiting for transfers between devices: 14.4 us -> 10.6 us  [local(): first = lax.all_to_all(first, 'z', split_axis=0, concat_axis=0, tiled=True)]
    ppermute x2, waiting for transfers between devices: 17.8 us -> 14.5 us  [local(): queries.append(lax.ppermute(part, ('core', 'x'), pairs(r)))]
    broadcast_in_dim x5 -> x0, local copies, waits for them, and re-layouts: 2.25 us -> none  [the longest x1 2.15 us: local(): keys = jnp.broadcast_to(keys[None], (4, 256, WIDE))]
  transfers between devices with their start and end apart: 11 -> 16, of which waited for: 7 -> 4; matrix products, arithmetic and copies ran while one was open for 2% -> 7% of each run, Pallas kernels for 0% -> 9%
where the time goes in v2:
time: 139 us; the launch traced here: 138 us
  starting transfers between devices  70.9 us (51%)
  waiting for transfers between devices  30.9 us (22%)
  Pallas kernels  20.9 us (15%)
  local copies, waits for them, and re-layouts  7.62 us (5%)
  other arithmetic  5.42 us (4%)
  between operations  1.84 us (1%)
    ppermute x4, starting transfers between devices, local(): keys = keys + [lax.ppermute(piece, 'core', swap) for piece in keys]  15.2 us
    ppermute x2, waiting for transfers between devices, local(): queries.append(lax.ppermute(part, ('core', 'x'), pairs(r)))  14.5 us
    pallas_call x2, Pallas kernels, local(): pl.pallas_call(attend_kernel, out_shape=jax.ShapeDtypeStruct((QB, HEADS *...  13.2 us
    all_to_all x1, starting transfers between devices, local(): first = lax.all_to_all(first, 'z', split_axis=0, concat_axis=0, tiled=True)  12.3 us
    all_to_all x1, waiting for transfers between devices, local(): first = lax.all_to_all(first, 'z', split_axis=0, concat_axis=0, tiled=True)  10.6 us
    ppermute x3, starting transfers between devices, local(): lax.ppermute(mine, 'y', [(i, (i + step) % 4) for i in range(4)])  10.1 us
    ppermute x2, starting transfers between devices, local(): queries.append(lax.ppermute(part, ('core', 'x'), pairs(r)))  8.15 us
    ppermute x2, starting transfers between devices, local(): ups.append(lax.ppermute(w_uv, ('core', 'x'), pairs(r)))  8.08 us
  transfers between devices with their start and end apart: 16, of which 4 were waited for; matrix products, arithmetic and copies ran while one was open for 7% of the time, Pallas kernels for 9%

profile of v2, /device:TPU:1, one launch (start us, length us, event | category | flops | bytes accessed | tf_op | source)
XLA Modules:
  0.0 137.7 jit_solution(18294117676103360226)
XLA Ops:
  0.0 5.9 %collective-permute-start.4 = (bf16[8,512,128]{2,1,0:T(8,128)(2,1)}, bf16[8,512,128]{2,1,0:T(8,128)(2,1)}, u32[]{:S(2)}, u32[]{:S(2)}) collective-permute-start(bf16[8,512,128]{2,1,0:T(8,128)(2,1)} %param.11), channel_id=1, source_target_pairs={{0,1},{1,0},{2,17},{3,16},{16,3},{17,2},{18,19},{19,18},{4,5},{5,4... | collective-permute-start | bytes 3145736 | tf_op jit(solution)/shard_map/ppermute | solution.py:102
  5.9 2.2 %collective-permute-start.1 = (bf16[8,512,128]{2,1,0:T(8,128)(2,1)}, bf16[8,512,128]{2,1,0:T(8,128)(2,1)S(1)}, u32[]{:S(2)}, u32[]{:S(2)}) collective-permute-start(bf16[8,512,128]{2,1,0:T(8,128)(2,1)} %param.11), channel_id=1, source_target_pairs={{0,0},{1,1},{2,16},{3,17},{16,2},{17,3},{18,18},{19,19},{4,4},{5,5... | collective-permute-start | bytes 3145736 | tf_op jit(solution)/shard_map/ppermute | solution.py:102
  8.1 0.8 shift-right-arithmetic_convert_fusion
  8.9 0.8 constant_dynamic-slice_fusion.9
  9.6 0.1 reshape.53
  10.1 4.6 %collective-permute-start = (bf16[17,8,640]{2,1,0:T(8,128)(2,1)S(1)}, bf16[17,8,640]{2,1,0:T(8,128)(2,1)S(1)}, u32[]{:S(2)}, u32[]{:S(2)}) collective-permute-start(bf16[17,8,640]{2,1,0:T(8,128)(2,1)S(1)} %pad_maximum_fusion.3), channel_id=1, source_target_pairs={{0,16},{16,0},{1,17},{17,1},{2,18},{18,2},{3,19},{19,3},{4,20},{20... | collective-permute-start | bytes 522248 | tf_op jit(solution)/shard_map/ppermute | solution.py:113
  14.8 0.6 slice_reduce_fusion
  17.2 0.1 select_reduce_fusion
  17.3 0.1 convert_element_type.36
  17.4 0.1 reshape.56
  17.5 0.7 fusion.1
  18.2 12.3 %all-to-all-start = ((bf16[16,24,128]{2,1,0:T(8,128)(2,1)}), bf16[16,24,128]{2,1,0:T(8,128)(2,1)}, u32[]{:S(2)}, u32[]{:S(2)}) async-start(bf16[16,24,128]{2,1,0:T(8,128)(2,1)} %fusion.1), calls=%async_computation | async-start | bytes 196608 | tf_op jit(solution)/shard_map/all_to_all | solution.py:132
  30.5 1.3 constant_dynamic-slice_fusion.2
  31.8 10.6 %all-to-all-done = bf16[16,24,128]{2,1,0:T(8,128)(2,1)} async-done(((bf16[16,24,128]{2,1,0:T(8,128)(2,1)}), bf16[16,24,128]{2,1,0:T(8,128)(2,1)}, u32[]{:S(2)}, u32[]{:S(2)}) %all-to-all-start) | async-done | bytes 98336 | tf_op jit(solution)/shard_map/all_to_all | solution.py:132
  42.4 0.9 convert_reduce_fusion
  43.3 0.7 constant_dynamic-slice_fusion
  44.0 0.7 constant_dynamic-slice_fusion.5
  44.7 0.1 reshape.58
  44.9 0.6 add.63.index_ref
  45.4 0.7 maximum_maximum_fusion.1.hot_ref
  46.1 1.8 %shard_map.64 = bf16[16,3,8,640]{3,2,1,0:T(8,128)(2,1)} custom-call(s32[32]{0:T(128)} %add.63.index_ref, bf16[32,8,640]{2,1,0:T(8,128)(2,1)} %copy-done.2, bf16[8,640]{1,0:T(8,128)(2,1)} %maximum_maximum_fusion.1.hot_ref), custom_call_target="tpu_custom_call" | custom-call | tf_op jit(solution)/shard_map/pallas_call | solution.py:147
  47.9 4.8 %all-to-all-start.1 = ((bf16[16,3,8,640]{3,2,1,0:T(8,128)(2,1)}), bf16[16,3,8,640]{3,2,1,0:T(8,128)(2,1)S(1)}, u32[]{:S(2)}, u32[]{:S(2)}) async-start(bf16[16,3,8,640]{3,2,1,0:T(8,128)(2,1)} %shard_map.64), calls=%async_computation.1 | async-start | bytes 983040 | tf_op jit(solution)/shard_map/all_to_all | solution.py:153
  52.9 6.2 %collective-permute-start.2 = (bf16[64,4608]{1,0:T(8,128)(2,1)S(1)}, bf16[64,4608]{1,0:T(8,128)(2,1)S(1)}, u32[]{:S(2)}, u32[]{:S(2)}) collective-permute-start(bf16[64,4608]{1,0:T(8,128)(2,1)S(1)} %pad_maximum_fusion), channel_id=1, source_target_pairs={{0,0},{1,1},{2,16},{3,17},{16,2},{17,3},{18,18},{19,19},{4,4},{5,5... | collective-permute-start | bytes 1769480 | tf_op jit(solution)/shard_map/ppermute | solution.py:100
  59.2 1.9 %collective-permute-start.3 = (bf16[64,4608]{1,0:T(8,128)(2,1)S(1)}, bf16[64,4608]{1,0:T(8,128)(2,1)S(1)}, u32[]{:S(2)}, u32[]{:S(2)}) collective-permute-start(bf16[64,4608]{1,0:T(8,128)(2,1)S(1)} %pad_maximum_fusion.1), channel_id=1, source_target_pairs={{0,1},{1,0},{2,17},{3,16},{16,3},{17,2},{18,19},{19,18},{4,5},{5,4... | collective-permute-start | bytes 1769480 | tf_op jit(solution)/shard_map/ppermute | solution.py:100
  61.1 11.9 %collective-permute-done.2.q_ref = bf16[64,4608]{1,0:T(8,128)(2,1)S(1)} collective-permute-done((bf16[64,4608]{1,0:T(8,128)(2,1)S(1)}, bf16[64,4608]{1,0:T(8,128)(2,1)S(1)}, u32[]{:S(2)}, u32[]{:S(2)}) %collective-permute-start.2) | collective-permute-done | bytes 589856 | tf_op jit(solution)/shard_map/ppermute | solution.py:100
  73.0 2.6 %collective-permute-done.3.q_ref = bf16[64,4608]{1,0:T(8,128)(2,1)S(1)} collective-permute-done((bf16[64,4608]{1,0:T(8,128)(2,1)S(1)}, bf16[64,4608]{1,0:T(8,128)(2,1)S(1)}, u32[]{:S(2)}, u32[]{:S(2)}) %collective-permute-start.3) | collective-permute-done | bytes 589856 | tf_op jit(solution)/shard_map/ppermute | solution.py:100
  75.6 0.8 copy-done.12
  76.4 0.8 copy-done.1
  77.2 1.9 %shard_map.66.refs_0_ = bf16[256,640]{1,0:T(8,128)(2,1)} custom-call(s32[24]{0:T(128)} %copy-done.14, bf16[16,3,8,640]{3,2,1,0:T(8,128)(2,1)} %copy-done.1), custom_call_target="tpu_custom_call" | custom-call | tf_op jit(solution)/shard_map/pallas_call | solution.py:156
  79.1 4.8 %collective-permute-start.7 = (bf16[256,640]{1,0:T(8,128)(2,1)}, bf16[256,640]{1,0:T(8,128)(2,1)S(1)}, u32[]{:S(2)}, u32[]{:S(2)}) collective-permute-start(bf16[256,640]{1,0:T(8,128)(2,1)} %shard_map.66.refs_0_), channel_id=1, source_target_pairs={{0,8},{4,12},{8,0},{12,4},{1,9},{5,13},{9,1},{13,5},{2,10},{6,14},... | collective-permute-start | bytes 983048 | tf_op jit(solution)/shard_map/ppermute | solution.py:164
  84.0 2.7 %collective-permute-start.6 = (bf16[256,640]{1,0:T(8,128)(2,1)}, bf16[256,640]{1,0:T(8,128)(2,1)S(1)}, u32[]{:S(2)}, u32[]{:S(2)}) collective-permute-start(bf16[256,640]{1,0:T(8,128)(2,1)} %shard_map.66.refs_0_), channel_id=1, source_target_pairs={{0,12},{4,0},{8,4},{12,8},{1,13},{5,1},{9,5},{13,9},{2,14},{6,2},{... | collective-permute-start | bytes 983048 | tf_op jit(solution)/shard_map/ppermute | solution.py:164
  86.7 2.6 %collective-permute-start.5 = (bf16[256,640]{1,0:T(8,128)(2,1)}, bf16[256,640]{1,0:T(8,128)(2,1)S(1)}, u32[]{:S(2)}, u32[]{:S(2)}) collective-permute-start(bf16[256,640]{1,0:T(8,128)(2,1)} %shard_map.66.refs_0_), channel_id=1, source_target_pairs={{0,4},{4,8},{8,12},{12,0},{1,5},{5,9},{9,13},{13,1},{2,6},{6,10},{... | collective-permute-start | bytes 983048 | tf_op jit(solution)/shard_map/ppermute | solution.py:164
  89.3 7.7 %collective-permute-start.8 = (bf16[256,640]{1,0:T(8,128)(2,1)}, bf16[256,640]{1,0:T(8,128)(2,1)S(1)}, u32[]{:S(2)}, u32[]{:S(2)}) collective-permute-start(bf16[256,640]{1,0:T(8,128)(2,1)} %shard_map.66.refs_0_), channel_id=1, source_target_pairs={{0,16},{16,0},{1,17},{17,1},{2,18},{18,2},{3,19},{19,3},{4,20},{20... | collective-permute-start | bytes 983048 | tf_op jit(solution)/shard_map/ppermute | solution.py:165
  97.0 2.7 %collective-permute-start.11 = (bf16[256,640]{1,0:T(8,128)(2,1)S(1)}, bf16[256,640]{1,0:T(8,128)(2,1)S(1)}, u32[]{:S(2)}, u32[]{:S(2)}) collective-permute-start(bf16[256,640]{1,0:T(8,128)(2,1)S(1)} %collective-permute-done.7.refs_3_), channel_id=1, source_target_pairs={{0,16},{16,0},{1,17},{17,1},{2,18},{18,2},{3,19},{19,3},{4,20},{20... | collective-permute-start | bytes 983048 | tf_op jit(solution)/shard_map/ppermute | solution.py:165
  99.8 2.4 %collective-permute-start.10 = (bf16[256,640]{1,0:T(8,128)(2,1)S(1)}, bf16[256,640]{1,0:T(8,128)(2,1)S(1)}, u32[]{:S(2)}, u32[]{:S(2)}) collective-permute-start(bf16[256,640]{1,0:T(8,128)(2,1)S(1)} %collective-permute-done.6.refs_2_), channel_id=1, source_target_pairs={{0,16},{16,0},{1,17},{17,1},{2,18},{18,2},{3,19},{19,3},{4,20},{20... | collective-permute-start | bytes 983048 | tf_op jit(solution)/shard_map/ppermute | solution.py:165
  102.2 2.3 %collective-permute-start.9 = (bf16[256,640]{1,0:T(8,128)(2,1)S(1)}, bf16[256,640]{1,0:T(8,128)(2,1)S(1)}, u32[]{:S(2)}, u32[]{:S(2)}) collective-permute-start(bf16[256,640]{1,0:T(8,128)(2,1)S(1)} %collective-permute-done.5.refs_1_), channel_id=1, source_target_pairs={{0,16},{16,0},{1,17},{17,1},{2,18},{18,2},{3,19},{19,3},{4,20},{20... | collective-permute-start | bytes 983048 | tf_op jit(solution)/shard_map/ppermute | solution.py:165
  104.5 2.0 %shard_map.65.q_ref = bf16[512,640]{1,0:T(8,128)(2,1)} custom-call(bf16[64,4608]{1,0:T(8,128)(2,1)} %copy-done.11), custom_call_target="tpu_custom_call" | custom-call | tf_op jit(solution)/shard_map/pallas_call | solution.py:169
  106.5 2.0 %shard_map.68.q_ref = bf16[512,640]{1,0:T(8,128)(2,1)} custom-call(bf16[64,4608]{1,0:T(8,128)(2,1)} %copy-done.12), custom_call_target="tpu_custom_call" | custom-call | tf_op jit(solution)/shard_map/pallas_call | solution.py:169
  108.6 0.7 copy-done.6
  109.2 0.1 copy-done.7
  109.3 0.1 copy-done.8
  109.5 0.7 copy-done.9
  110.2 6.6 %shard_map.67 = bf16[64,1024]{1,0:T(8,128)(2,1)} custom-call(bf16[512,640]{1,0:T(8,128)(2,1)} %shard_map.65.q_ref, bf16[256,640]{1,0:T(8,128)(2,1)} %shard_map.66.refs_0_, bf16[256,640]{1,0:T(8,128)(2,1)} %copy-done.5, bf16[256,640]{1,0:T(8,128)(2,1)} %copy-done.4, bf16[256,640]{1,0:T(8,128)(2,1)} %copy-done.3, bf16[256,640]{1,0:T(8,128)(2,1)} %copy-done.6, ...), custom_call_target="tpu_custom_call" | custom-call | tf_op jit(solution)/shard_map/pallas_call | solution.py:175
  116.8 5.8 %collective-permute-start.12 = (bf16[64,1024]{1,0:T(8,128)(2,1)}, bf16[64,1024]{1,0:T(8,128)(2,1)S(1)}, u32[]{:S(2)}, u32[]{:S(2)}) collective-permute-start(bf16[64,1024]{1,0:T(8,128)(2,1)} %shard_map.67), channel_id=1, source_target_pairs={{0,0},{1,1},{16,2},{17,3},{2,16},{3,17},{18,18},{19,19},{4,4},{5,5... | collective-permute-start | bytes 393224 | tf_op jit(solution)/shard_map/ppermute | solution.py:182
  122.6 6.6 %shard_map.69 = bf16[64,1024]{1,0:T(8,128)(2,1)} custom-call(bf16[512,640]{1,0:T(8,128)(2,1)} %shard_map.68.q_ref, bf16[256,640]{1,0:T(8,128)(2,1)} %shard_map.66.refs_0_, bf16[256,640]{1,0:T(8,128)(2,1)} %copy-done.5, bf16[256,640]{1,0:T(8,128)(2,1)} %copy-done.4, bf16[256,640]{1,0:T(8,128)(2,1)} %copy-done.3, bf16[256,640]{1,0:T(8,128)(2,1)} %copy-done.6, ...), custom_call_target="tpu_custom_call" | custom-call | tf_op jit(solution)/shard_map/pallas_call | solution.py:175
  129.2 1.9 %collective-permute-start.13 = (bf16[64,1024]{1,0:T(8,128)(2,1)}, bf16[64,1024]{1,0:T(8,128)(2,1)S(1)}, u32[]{:S(2)}, u32[]{:S(2)}) collective-permute-start(bf16[64,1024]{1,0:T(8,128)(2,1)} %shard_map.69), channel_id=1, source_target_pairs={{1,0},{0,1},{17,2},{16,3},{3,16},{2,17},{19,18},{18,19},{5,4},{4,5... | collective-permute-start | bytes 393224 | tf_op jit(solution)/shard_map/ppermute | solution.py:182
  131.1 5.8 %collective-permute-done.13 = bf16[64,1024]{1,0:T(8,128)(2,1)S(1)} collective-permute-done((bf16[64,1024]{1,0:T(8,128)(2,1)}, bf16[64,1024]{1,0:T(8,128)(2,1)S(1)}, u32[]{:S(2)}, u32[]{:S(2)}) %collective-permute-start.13) | collective-permute-done | bytes 131104 | tf_op jit(solution)/shard_map/ppermute | solution.py:182
  136.9 0.7 pad_maximum_fusion.2
  (66 shorter events, 1.1 us)
Async XLA Ops:
  0.0 9.9 %copy-start = (bf16[16,64,512]{2,1,0:T(8,128)(2,1)S(1)}, bf16[16,64,512]{2,1,0:T(8,128)(2,1)}, u32[]{:S(2)}) copy-start(bf16[16,64,512]{2,1,0:T(8,128)(2,1)} %param.8) | copy-start | bytes 3145732
  0.0 76.4 %collective-permute-start.4 = (bf16[8,512,128]{2,1,0:T(8,128)(2,1)}, bf16[8,512,128]{2,1,0:T(8,128)(2,1)}, u32[]{:S(2)}, u32[]{:S(2)}) collective-permute-start(bf16[8,512,128]{2,1,0:T(8,128)(2,1)} %param.11), channel_id=1, source_target_pairs={{0,1},{1,0},{2,17},{3,16},{16,3},{17,2},{18,19},{19,18},{4,5},{5,4... | collective-permute-start | bytes 3145736 | tf_op jit(solution)/shard_map/ppermute | solution.py:102
  5.9 36.5 %collective-permute-start.1 = (bf16[8,512,128]{2,1,0:T(8,128)(2,1)}, bf16[8,512,128]{2,1,0:T(8,128)(2,1)S(1)}, u32[]{:S(2)}, u32[]{:S(2)}) collective-permute-start(bf16[8,512,128]{2,1,0:T(8,128)(2,1)} %param.11), channel_id=1, source_target_pairs={{0,0},{1,1},{2,16},{3,17},{16,2},{17,3},{18,18},{19,19},{4,4},{5,5... | collective-permute-start | bytes 3145736 | tf_op jit(solution)/shard_map/ppermute | solution.py:102
  9.9 4.8 %copy-start.15 = (s32[2,32]{1,0:T(2,128)S(1)}, s32[2,32]{1,0:T(2,128)}, u32[]{:S(2)}) copy-start(s32[2,32]{1,0:T(2,128)} %param.10) | copy-start | bytes 772
  10.1 6.7 %collective-permute-start = (bf16[17,8,640]{2,1,0:T(8,128)(2,1)S(1)}, bf16[17,8,640]{2,1,0:T(8,128)(2,1)S(1)}, u32[]{:S(2)}, u32[]{:S(2)}) collective-permute-start(bf16[17,8,640]{2,1,0:T(8,128)(2,1)S(1)} %pad_maximum_fusion.3), channel_id=1, source_target_pairs={{0,16},{16,0},{1,17},{17,1},{2,18},{18,2},{3,19},{19,3},{4,20},{20... | collective-permute-start | bytes 522248 | tf_op jit(solution)/shard_map/ppermute | solution.py:113
  16.9 14.9 %copy-start.2 = (bf16[32,8,640]{2,1,0:T(8,128)(2,1)}, bf16[32,8,640]{2,1,0:T(8,128)(2,1)S(1)}, u32[]{:S(2)}) copy-start(bf16[32,8,640]{2,1,0:T(8,128)(2,1)S(1)} %maximum_select_fusion.blocks_ref) | copy-start | bytes 983044
  17.2 14.6 %copy-start.14 = (s32[24]{0:T(128)}, s32[24]{0:T(128)S(1)}, u32[]{:S(2)}) copy-start(s32[24]{0:T(128)S(1)} %get-tuple-element.27.index_ref) | copy-start | bytes 292
  18.2 24.2 %all-to-all-start = ((bf16[16,24,128]{2,1,0:T(8,128)(2,1)}), bf16[16,24,128]{2,1,0:T(8,128)(2,1)}, u32[]{:S(2)}, u32[]{:S(2)}) async-start(bf16[16,24,128]{2,1,0:T(8,128)(2,1)} %fusion.1), calls=%async_computation | async-start | bytes 196608 | tf_op jit(solution)/shard_map/all_to_all | solution.py:132
  42.4 10.4 %copy-start.13 = (bf16[128,512]{1,0:T(8,128)(2,1)S(1)}, bf16[128,512]{1,0:T(8,128)(2,1)}, u32[]{:S(2)}) copy-start(bf16[128,512]{1,0:T(8,128)(2,1)} %param.7) | copy-start | bytes 393220
  42.4 5.5 %copy-start.10 = (bf16[8,512,128]{2,1,0:T(8,128)(2,1)}, bf16[8,512,128]{2,1,0:T(8,128)(2,1)S(1)}, u32[]{:S(2)}) copy-start(bf16[8,512,128]{2,1,0:T(8,128)(2,1)S(1)} %collective-permute-done.1.refs_8_) | copy-start | bytes 3145732
  47.9 28.5 %all-to-all-start.1 = ((bf16[16,3,8,640]{3,2,1,0:T(8,128)(2,1)}), bf16[16,3,8,640]{3,2,1,0:T(8,128)(2,1)S(1)}, u32[]{:S(2)}, u32[]{:S(2)}) async-start(bf16[16,3,8,640]{3,2,1,0:T(8,128)(2,1)} %shard_map.64), calls=%async_computation.1 | async-start | bytes 983040 | tf_op jit(solution)/shard_map/all_to_all | solution.py:153
  52.9 20.1 %collective-permute-start.2 = (bf16[64,4608]{1,0:T(8,128)(2,1)S(1)}, bf16[64,4608]{1,0:T(8,128)(2,1)S(1)}, u32[]{:S(2)}, u32[]{:S(2)}) collective-permute-start(bf16[64,4608]{1,0:T(8,128)(2,1)S(1)} %pad_maximum_fusion), channel_id=1, source_target_pairs={{0,0},{1,1},{2,16},{3,17},{16,2},{17,3},{18,18},{19,19},{4,4},{5,5... | collective-permute-start | bytes 1769480 | tf_op jit(solution)/shard_map/ppermute | solution.py:100
  59.2 16.4 %collective-permute-start.3 = (bf16[64,4608]{1,0:T(8,128)(2,1)S(1)}, bf16[64,4608]{1,0:T(8,128)(2,1)S(1)}, u32[]{:S(2)}, u32[]{:S(2)}) collective-permute-start(bf16[64,4608]{1,0:T(8,128)(2,1)S(1)} %pad_maximum_fusion.1), channel_id=1, source_target_pairs={{0,1},{1,0},{2,17},{3,16},{16,3},{17,2},{18,19},{19,18},{4,5},{5,4... | collective-permute-start | bytes 1769480 | tf_op jit(solution)/shard_map/ppermute | solution.py:100
  73.0 2.6 %copy-start.11 = (bf16[64,4608]{1,0:T(8,128)(2,1)}, bf16[64,4608]{1,0:T(8,128)(2,1)S(1)}, u32[]{:S(2)}) copy-start(bf16[64,4608]{1,0:T(8,128)(2,1)S(1)} %collective-permute-done.2.q_ref) | copy-start | bytes 1769476
  75.6 0.8 copy-start.12
  76.4 0.8 copy-start.1
  79.1 17.9 %collective-permute-start.7 = (bf16[256,640]{1,0:T(8,128)(2,1)}, bf16[256,640]{1,0:T(8,128)(2,1)S(1)}, u32[]{:S(2)}, u32[]{:S(2)}) collective-permute-start(bf16[256,640]{1,0:T(8,128)(2,1)} %shard_map.66.refs_0_), channel_id=1, source_target_pairs={{0,8},{4,12},{8,0},{12,4},{1,9},{5,13},{9,1},{13,5},{2,10},{6,14},... | collective-permute-start | bytes 983048 | tf_op jit(solution)/shard_map/ppermute | solution.py:164
  84.0 15.8 %collective-permute-start.6 = (bf16[256,640]{1,0:T(8,128)(2,1)}, bf16[256,640]{1,0:T(8,128)(2,1)S(1)}, u32[]{:S(2)}, u32[]{:S(2)}) collective-permute-start(bf16[256,640]{1,0:T(8,128)(2,1)} %shard_map.66.refs_0_), channel_id=1, source_target_pairs={{0,12},{4,0},{8,4},{12,8},{1,13},{5,1},{9,5},{13,9},{2,14},{6,2},{... | collective-permute-start | bytes 983048 | tf_op jit(solution)/shard_map/ppermute | solution.py:164
  86.7 15.5 %collective-permute-start.5 = (bf16[256,640]{1,0:T(8,128)(2,1)}, bf16[256,640]{1,0:T(8,128)(2,1)S(1)}, u32[]{:S(2)}, u32[]{:S(2)}) collective-permute-start(bf16[256,640]{1,0:T(8,128)(2,1)} %shard_map.66.refs_0_), channel_id=1, source_target_pairs={{0,4},{4,8},{8,12},{12,0},{1,5},{5,9},{9,13},{13,1},{2,6},{6,10},{... | collective-permute-start | bytes 983048 | tf_op jit(solution)/shard_map/ppermute | solution.py:164
  89.3 19.2 %collective-permute-start.8 = (bf16[256,640]{1,0:T(8,128)(2,1)}, bf16[256,640]{1,0:T(8,128)(2,1)S(1)}, u32[]{:S(2)}, u32[]{:S(2)}) collective-permute-start(bf16[256,640]{1,0:T(8,128)(2,1)} %shard_map.66.refs_0_), channel_id=1, source_target_pairs={{0,16},{16,0},{1,17},{17,1},{2,18},{18,2},{3,19},{19,3},{4,20},{20... | collective-permute-start | bytes 983048 | tf_op jit(solution)/shard_map/ppermute | solution.py:165
  97.0 11.5 %copy-start.3 = (bf16[256,640]{1,0:T(8,128)(2,1)}, bf16[256,640]{1,0:T(8,128)(2,1)S(1)}, u32[]{:S(2)}) copy-start(bf16[256,640]{1,0:T(8,128)(2,1)S(1)} %collective-permute-done.7.refs_3_) | copy-start | bytes 983044
  97.0 11.5 %collective-permute-start.11 = (bf16[256,640]{1,0:T(8,128)(2,1)S(1)}, bf16[256,640]{1,0:T(8,128)(2,1)S(1)}, u32[]{:S(2)}, u32[]{:S(2)}) collective-permute-start(bf16[256,640]{1,0:T(8,128)(2,1)S(1)} %collective-permute-done.7.refs_3_), channel_id=1, source_target_pairs={{0,16},{16,0},{1,17},{17,1},{2,18},{18,2},{3,19},{19,3},{4,20},{20... | collective-permute-start | bytes 983048 | tf_op jit(solution)/shard_map/ppermute | solution.py:165
  99.8 8.7 %copy-start.4 = (bf16[256,640]{1,0:T(8,128)(2,1)}, bf16[256,640]{1,0:T(8,128)(2,1)S(1)}, u32[]{:S(2)}) copy-start(bf16[256,640]{1,0:T(8,128)(2,1)S(1)} %collective-permute-done.6.refs_2_) | copy-start | bytes 983044
  99.8 8.7 %collective-permute-start.10 = (bf16[256,640]{1,0:T(8,128)(2,1)S(1)}, bf16[256,640]{1,0:T(8,128)(2,1)S(1)}, u32[]{:S(2)}, u32[]{:S(2)}) collective-permute-start(bf16[256,640]{1,0:T(8,128)(2,1)S(1)} %collective-permute-done.6.refs_2_), channel_id=1, source_target_pairs={{0,16},{16,0},{1,17},{17,1},{2,18},{18,2},{3,19},{19,3},{4,20},{20... | collective-permute-start | bytes 983048 | tf_op jit(solution)/shard_map/ppermute | solution.py:165
  102.2 6.3 %copy-start.5 = (bf16[256,640]{1,0:T(8,128)(2,1)}, bf16[256,640]{1,0:T(8,128)(2,1)S(1)}, u32[]{:S(2)}) copy-start(bf16[256,640]{1,0:T(8,128)(2,1)S(1)} %collective-permute-done.5.refs_1_) | copy-start | bytes 983044
  102.2 6.4 %collective-permute-start.9 = (bf16[256,640]{1,0:T(8,128)(2,1)S(1)}, bf16[256,640]{1,0:T(8,128)(2,1)S(1)}, u32[]{:S(2)}, u32[]{:S(2)}) collective-permute-start(bf16[256,640]{1,0:T(8,128)(2,1)S(1)} %collective-permute-done.5.refs_1_), channel_id=1, source_target_pairs={{0,16},{16,0},{1,17},{17,1},{2,18},{18,2},{3,19},{19,3},{4,20},{20... | collective-permute-start | bytes 983048 | tf_op jit(solution)/shard_map/ppermute | solution.py:165
  108.5 0.7 copy-start.6
  108.5 0.8 copy-start.7
  108.5 0.9 copy-start.8
  109.5 0.7 copy-start.9
  116.8 14.3 %collective-permute-start.12 = (bf16[64,1024]{1,0:T(8,128)(2,1)}, bf16[64,1024]{1,0:T(8,128)(2,1)S(1)}, u32[]{:S(2)}, u32[]{:S(2)}) collective-permute-start(bf16[64,1024]{1,0:T(8,128)(2,1)} %shard_map.67), channel_id=1, source_target_pairs={{0,0},{1,1},{16,2},{17,3},{2,16},{3,17},{18,18},{19,19},{4,4},{5,5... | collective-permute-start | bytes 393224 | tf_op jit(solution)/shard_map/ppermute | solution.py:182
  129.2 7.7 %collective-permute-start.13 = (bf16[64,1024]{1,0:T(8,128)(2,1)}, bf16[64,1024]{1,0:T(8,128)(2,1)S(1)}, u32[]{:S(2)}, u32[]{:S(2)}) collective-permute-start(bf16[64,1024]{1,0:T(8,128)(2,1)} %shard_map.69), channel_id=1, source_target_pairs={{1,0},{0,1},{17,2},{16,3},{3,16},{2,17},{19,18},{18,19},{5,4},{4,5... | collective-permute-start | bytes 393224 | tf_op jit(solution)/shard_map/ppermute | solution.py:182

commit v3 on v2

v3 whole, which is shorter than its diff:
```python
import jax
import jax.numpy as jnp
from jax import lax
from jax.experimental import pallas as pl
from jax.experimental.pallas import tpu as pltpu
from jax.sharding import Mesh
from jax.sharding import PartitionSpec as P

LAT = 512
ROPE = 64
VH = 128
HOT = 8
COLD = 24
WIDE = LAT + 2 * ROPE
SHARE = 8
QB = 64
HEADS = 8
PACK = 24
ROWS = 288

SCORE_SCALE = 192.0 ** (-0.5)
LOG2E = 1.4426950408889634

bf16 = jnp.bfloat16
f32 = jnp.float32
i32 = jnp.int32


def iota(shape, axis):
    return lax.broadcasted_iota(i32, shape, axis)


def one_hot(index, width):
    return jnp.where(index == iota((index.shape[0], width), 1), 1.0, 0.0).astype(bf16)


def pick(selector, rows):
    return jnp.dot(selector, rows, preferred_element_type=f32)


def send_kernel(hot_ref, first_ref, lat_ref, rope_ref, out_ref):
    got = first_ref[...].reshape(16 * 8, LAT)
    row = iota((256, 1), 0)
    notes = pick(one_hot(row // 16 * 8 + 5, 128), got[:, 0:128])
    lane = iota((256, 128), 1)
    want = jnp.sum(jnp.where(lane == row // 8 % 2, notes, 0.0), axis=1, keepdims=True)
    lat = pick(one_hot(want.astype(i32) * 8 + row % 8, 256), lat_ref[...].reshape(256, LAT))
    row = iota((128, 1), 0)
    notes = pick(one_hot(row // 8 * 8 + 5, 128), got[:, 0:128])
    lane = iota((128, 128), 1)
    want = jnp.sum(jnp.where(lane == row % 8, notes, 0.0), axis=1, keepdims=True).astype(i32)
    want = jnp.where(row % 8 < 2, want, -1)
    rope = pick(one_hot(want, 32), rope_ref[...])
    row = iota((8, 1), 0)
    source = jnp.where(row == 2, 4, jnp.where(row >= 4, row - 4, -1))
    hot = pick(one_hot(hot_ref[0] * 8 + source, 128) * (source >= 0).astype(bf16), got)
    for z in range(16):
        out_ref[z, 0:16, :] = lat[z * 16 : z * 16 + 16].astype(bf16)
        out_ref[z, 16:24, :] = (rope[z * 8 : z * 8 + 8] + hot).astype(bf16)


def share_kernel(owners_ref, got_ref, out_ref, got, rows, sems):
    copy = pltpu.make_async_copy(got_ref, got, sems.at[0])
    copy.start()
    row = iota((256, 1), 0)
    slot, token = row % 32, row // 32
    index = (slot - COLD) * (2 * PACK) + token // 4 * PACK + 20 + token % 4
    rope_slot = iota((32, 1), 0)
    rope_index = (rope_slot - COLD) * (2 * PACK) + 18
    for i in range(COLD):
        owner = owners_ref[i]
        at, side = owner // 2 * PACK, owner % 2
        index = jnp.where(slot == i, at + side * SHARE + token, index)
        rope_index = jnp.where(rope_slot == i, at + 16 + side, rope_index)
    lat = one_hot(index, 16 * PACK)
    rope = one_hot(rope_index, 16 * PACK)
    copy.wait()
    table = got[...].reshape(16 * PACK, LAT)
    rows[0:256, :] = pick(lat, table).astype(bf16)
    rows[256:ROWS, :] = pick(rope, table).astype(bf16)
    copies = [pltpu.make_async_copy(rows, out_ref.at[n], sems.at[n]) for n in range(4)]
    for copy in copies:
        copy.start()
    for copy in copies:
        copy.wait()


def layout_kernel(q_ref, out_ref, q, sem):
    copy = pltpu.make_async_copy(q_ref, q, sem)
    copy.start()
    copy.wait()
    for h in range(HEADS):
        base = HEADS * LAT + h * ROPE
        rows = pl.ds(h * QB, QB)
        part = q[:, base : base + ROPE]
        out_ref[rows, 0:LAT] = q[:, h * LAT : (h + 1) * LAT]
        out_ref[rows, LAT:WIDE] = jnp.concatenate([part, part], axis=1)


def bring(ref, keys, ropes, sems):
    copies = []
    for n in range(4):
        copies.append(pltpu.make_async_copy(ref.at[n, 0:256], keys.at[n], sems.at[n]))
        copies.append(pltpu.make_async_copy(ref.at[n, 256:ROWS], ropes.at[n], sems.at[4 + n]))
    for copy in copies:
        copy.start()
    return copies


def spread(ropes, places):
    lane = iota((32, 2 * ROPE), 1)
    for n in range(4):
        for t in range(SHARE):
            pair = ropes[n, :, t // 2 * 128 : t // 2 * 128 + 128]
            own = lane < ROPE if t % 2 == 0 else lane >= ROPE
            places[n, t * 32 : t * 32 + 32, :] = jnp.where(own, pair, 0)


def attend(q_ref, keys, places):
    scores = []
    for n in range(4):
        scores.append(
            lax.dot_general(
                q_ref[...],
                jnp.concatenate([keys[n], places[n]], axis=1),
                (((1,), (1,)), ((), ())),
                preferred_element_type=f32,
            )
        )
    top = jnp.maximum(jnp.maximum(scores[0], scores[1]), jnp.maximum(scores[2], scores[3]))
    top = jnp.max(top, axis=1, keepdims=True) * (SCORE_SCALE * LOG2E)
    total = jnp.zeros((HEADS * QB, 256), f32)
    blended = jnp.zeros((HEADS * QB, LAT), f32)
    for n, s in enumerate(scores):
        p = jnp.exp2(s * (SCORE_SCALE * LOG2E) - top)
        total = total + p
        blended = blended + jnp.dot(p.astype(bf16), keys[n], preferred_element_type=f32)
    return top, jnp.sum(total, axis=1, keepdims=True), blended


def first_half_kernel(
    q0_ref, q1_ref, mine_ref, blend0_ref, stat0_ref, blend1_ref, stat1_ref, keys, ropes, places, sems
):
    copies = bring(mine_ref, keys, ropes, sems)
    for copy in copies:
        copy.wait()
    spread(ropes, places)
    outs = ((q0_ref, blend0_ref, stat0_ref), (q1_ref, blend1_ref, stat1_ref))
    for q_ref, blend_ref, stat_ref in outs:
        top, total, blended = attend(q_ref, keys, places)
        blend_ref[...] = blended
        stat_ref[:, 0:128] = jnp.broadcast_to(top, (HEADS * QB, 128))
        stat_ref[:, 128:256] = jnp.broadcast_to(total, (HEADS * QB, 128))


def second_half_kernel(
    q_ref, other_ref, blend_ref, stat_ref, w_ref, o_ref, keys, ropes, places, w, sems
):
    copies = bring(other_ref, keys, ropes, sems)
    up = pltpu.make_async_copy(w_ref, w, sems.at[8])
    up.start()
    for copy in copies:
        copy.wait()
    spread(ropes, places)
    top, total, blended = attend(q_ref, keys, places)
    top0, total0 = stat_ref[:, 0:1], stat_ref[:, 128:129]
    both = jnp.maximum(top, top0)
    mine, other = jnp.exp2(top0 - both), jnp.exp2(top - both)
    scale = 1.0 / (total0 * mine + total * other)
    latent = (blend_ref[...] * (mine * scale) + blended * (other * scale)).astype(bf16)
    up.wait()
    for h in range(HEADS):
        o_ref[:, h * VH : (h + 1) * VH] = jnp.dot(
            latent[h * QB : (h + 1) * QB], w[h], preferred_element_type=f32
        ).astype(bf16)


def local(q_latent, q_rope, kv_latent, k_rope, selection, w_uv):
    z, k, y, x = (lax.axis_index(a) for a in ("z", "core", "y", "x"))
    vmem = pl.BlockSpec(memory_space=pltpu.VMEM)
    smem = pl.BlockSpec(memory_space=pltpu.SMEM)
    anywhere = pl.BlockSpec(memory_space=pl.ANY)
    swap = [(0, 1), (1, 0)]

    lat = lax.dynamic_slice_in_dim(kv_latent, y * 16, 16, 1)
    rope = lax.dynamic_slice_in_dim(k_rope, y * 1024, 1024, 1)
    hot_first = jnp.max(selection[:, 0])
    cold = selection[:, HOT:]
    notes = jnp.concatenate([cold >> 4, cold & 15], axis=1).astype(bf16)
    notes = jnp.pad(notes, ((0, 6), (0, LAT - 2 * COLD)))
    theirs = jnp.concatenate(
        [
            lax.dynamic_slice_in_dim(lat, (1 - k) * SHARE, SHARE, 1).reshape(128, LAT),
            lax.dynamic_slice_in_dim(rope, (1 - k) * LAT, LAT, 1),
            notes,
        ],
        axis=0,
    )
    swapped = lax.ppermute(theirs, "core", swap)
    own = lax.dynamic_slice_in_dim(lat, k * SHARE, SHARE, 1)
    other = swapped[:128].reshape(16, SHARE, LAT)
    lat = jnp.where(k == 0, jnp.concatenate([own, other]), jnp.concatenate([other, own]))
    own, other = lax.dynamic_slice_in_dim(rope, k * LAT, LAT, 1), swapped[128:144]
    rope = jnp.where(k == 0, jnp.concatenate([own, other]), jnp.concatenate([other, own]))
    notes = jnp.where(x // 2 == k, notes, swapped[144:])
    notes = jnp.where(x % 2 == 0, notes[0, : 2 * COLD], notes[1, : 2 * COLD]).astype(i32)
    owners, places = notes[:COLD], notes[COLD:]

    match = owners[None, :] == jnp.arange(32)[:, None]
    wants = jnp.sum(jnp.where(match, places[None, :], 0), axis=1).reshape(16, 2)
    wants = wants + jnp.arange(2)[None, :] * 16
    hot = lax.dynamic_slice_in_dim(lat, hot_first & 31, HOT, 0).reshape(16, 4, LAT)
    hot_rope = lax.dynamic_slice_in_dim(rope, hot_first & 31, HOT, 0)
    hot_rope = jnp.broadcast_to(hot_rope[:, None, None, :], (HOT, 2, 1, LAT)).reshape(16, 1, LAT)
    wants = jnp.pad(wants.astype(bf16)[:, None, :], ((0, 0), (0, 2), (0, LAT - 2)))
    first = jnp.concatenate([hot, hot_rope, wants], axis=1)
    first, w_later = lax.optimization_barrier((first, w_uv))
    first = lax.all_to_all(first, "z", split_axis=0, concat_axis=0, tiled=True)

    def pairs(r):
        return [
            (c * 4 + s, (s // 2) * 4 + 2 * c + (s + r) % 2) for c in range(2) for s in range(4)
        ]

    ups = [lax.ppermute(w, ("core", "x"), pairs(r)) for r, w in enumerate((w_uv, w_later))]
    first, ups[0] = lax.optimization_barrier((first, ups[0]))
    queries = []
    for r in range(2):
        m = (x + r) % 2
        part = jnp.concatenate(
            [
                lax.dynamic_slice_in_dim(q_latent, m * QB, QB, 0),
                lax.dynamic_slice_in_dim(q_rope, m * QB, QB, 0),
            ],
            axis=1,
        )
        queries.append(lax.ppermute(part, ("core", "x"), pairs(r)))

    second = pl.pallas_call(
        send_kernel,
        out_shape=jax.ShapeDtypeStruct((16, PACK, LAT), bf16),
        in_specs=[smem, vmem, vmem, vmem],
        out_specs=vmem,
    )((hot_first >> 5)[None], first, lat, rope)
    second = lax.all_to_all(second, "z", split_axis=0, concat_axis=0, tiled=True)
    second, queries = lax.optimization_barrier((second, queries))

    keys = pl.pallas_call(
        share_kernel,
        out_shape=jax.ShapeDtypeStruct((4, ROWS, LAT), bf16),
        in_specs=[smem, anywhere],
        out_specs=anywhere,
        scratch_shapes=[
            pltpu.VMEM((16, PACK, LAT), bf16),
            pltpu.VMEM((ROWS, LAT), bf16),
            pltpu.SemaphoreType.DMA((4,)),
        ],
    )(owners, second)
    queries = [
        pl.pallas_call(
            layout_kernel,
            out_shape=jax.ShapeDtypeStruct((HEADS * QB, WIDE), bf16),
            in_specs=[anywhere],
            out_specs=vmem,
            scratch_shapes=[
                pltpu.VMEM((QB, HEADS * (LAT + ROPE)), bf16),
                pltpu.SemaphoreType.DMA,
            ],
        )(q)
        for q in queries
    ]
    mine = lax.all_to_all(keys, "y", split_axis=0, concat_axis=0, tiled=True)
    mine, queries, ups[1] = lax.optimization_barrier((mine, queries, ups[1]))
    other = lax.ppermute(mine, "core", swap)

    rows = HEADS * QB
    blend = jax.ShapeDtypeStruct((rows, LAT), f32)
    stat = jax.ShapeDtypeStruct((rows, 256), f32)
    scratch = [
        pltpu.VMEM((4, 256, LAT), bf16),
        pltpu.VMEM((4, 32, LAT), bf16),
        pltpu.VMEM((4, 256, 2 * ROPE), bf16),
    ]
    params = pltpu.CompilerParams(vmem_limit_bytes=24 * 1024 * 1024)
    halves = pl.pallas_call(
        first_half_kernel,
        out_shape=[blend, stat, blend, stat],
        in_specs=[vmem, vmem, anywhere],
        out_specs=[vmem] * 4,
        scratch_shapes=scratch + [pltpu.SemaphoreType.DMA((8,))],
        compiler_params=params,
    )(queries[0], queries[1], mine)
    outs = []
    for r in range(2):
        out = pl.pallas_call(
            second_half_kernel,
            out_shape=jax.ShapeDtypeStruct((QB, HEADS * VH), bf16),
            in_specs=[vmem, anywhere, vmem, vmem, anywhere],
            out_specs=vmem,
            scratch_shapes=scratch
            + [pltpu.VMEM((HEADS, LAT, VH), bf16), pltpu.SemaphoreType.DMA((9,))],
            compiler_params=params,
        )(queries[r], other, halves[2 * r], halves[2 * r + 1], ups[r])
        outs.append(lax.ppermute(out, ("core", "x"), [(d, s) for s, d in pairs(r)]))
    even = x % 2 == 0
    return jnp.concatenate(
        [jnp.where(even, outs[0], outs[1]), jnp.where(even, outs[1], outs[0])], axis=0
    )


def solution(mesh):
    grid = Mesh(mesh.devices.reshape(16, 2, 4, 4), ("z", "core", "y", "x"))
    ctx, head = ("z", "core"), ("y", "x")
    in_specs = (
        P(ctx, head),
        P(ctx, head),
        P(ctx, None, None),
        P(ctx, None),
        P(ctx, None),
        P(head, None, None),
    )
    return jax.shard_map(
        local, mesh=grid, in_specs=in_specs, out_specs=P(ctx, head), check_vma=False
    )
```

time: 139 us -> 120 us (0.86)
  starting transfers between devices: 70.9 us -> 56.9 us
  Pallas kernels: 20.9 us -> 18.4 us
  local copies, waits for them, and re-layouts: 7.62 us -> 6.18 us
    ppermute x10 -> x4, starting transfers between devices: 37.9 us -> 22.1 us  [the longest x1 8.92 us: local(): swapped = lax.ppermute(theirs, 'core', swap)]
    all_to_all x0 -> x1, waiting for transfers between devices: none -> 7.64 us  [local(): mine = lax.all_to_all(keys, 'y', split_axis=0, concat_axis=0, tiled=True)]
    ppermute x2, waiting for transfers between devices: 14.5 us -> 9.99 us  [local(): queries.append(lax.ppermute(part, ('core', 'x'), pairs(r)))]
    all_to_all x0 -> x1, starting transfers between devices: none -> 4.19 us  [local(): mine = lax.all_to_all(keys, 'y', split_axis=0, concat_axis=0, tiled=True)]
    ppermute x2, waiting for transfers between devices: 5.77 us -> 2.63 us  [local(): outs.append(lax.ppermute(out, ('core', 'x'), [(d, s) for s, d in pairs(r)]))]
    pallas_call x4 -> x5, Pallas kernels: 16.9 us -> 14.3 us  [the longest x2 5.16 us: local(): pl.pallas_call(second_half_kernel, out_shape=jax.ShapeDtypeStruct((QB, HE...]
    slice x6 -> x2, local copies, waits for them, and re-layouts: 1.49 us -> 0.08 us  [the longest x1 0.07 us: local(): owners, places = (notes[:COLD], notes[COLD:])]
    unnamed x32 -> x26, local copies, waits for them, and re-layouts: 3.28 us -> 3.17 us
  transfers between devices with their start and end apart: 16 -> 11, of which waited for: 4 -> 5; matrix products, arithmetic and copies ran while one was open for 7% -> 3% of each run, Pallas kernels for 9% -> 11%
where the time goes in v3:
time: 120 us; the launch traced here: 119 us
  starting transfers between devices  56.9 us (47%)
  waiting for transfers between devices  31.8 us (26%)
  Pallas kernels  18.4 us (15%)
  local copies, waits for them, and re-layouts  6.18 us (5%)
  other arithmetic  4.04 us (3%)
  between operations  1.8 us (2%)
    all_to_all x1, starting transfers between devices, local(): first = lax.all_to_all(first, 'z', split_axis=0, concat_axis=0, tiled=True)  12.2 us
    all_to_all x1, waiting for transfers between devices, local(): first = lax.all_to_all(first, 'z', split_axis=0, concat_axis=0, tiled=True)  11.5 us
    ppermute x2, waiting for transfers between devices, local(): queries.append(lax.ppermute(part, ('core', 'x'), pairs(r)))  9.99 us
    ppermute x1, starting transfers between devices, local(): swapped = lax.ppermute(theirs, 'core', swap)  8.92 us
    ppermute x2, starting transfers between devices, local(): queries.append(lax.ppermute(part, ('core', 'x'), pairs(r)))  7.88 us
    all_to_all x1, waiting for transfers between devices, local(): mine = lax.all_to_all(keys, 'y', split_axis=0, concat_axis=0, tiled=True)  7.64 us
    ppermute x1, starting transfers between devices, local(): other = lax.ppermute(mine, 'core', swap)  7.58 us
    ppermute x2, starting transfers between devices, local(): outs.append(lax.ppermute(out, ('core', 'x'), [(d, s) for s, d in pairs(r)]))  6.86 us
  transfers between devices with their start and end apart: 11, of which 5 were waited for; matrix products, arithmetic and copies ran while one was open for 3% of the time, Pallas kernels for 11%

profile of v3, /device:TPU:1, one launch (start us, length us, event | category | flops | bytes accessed | tf_op | source)
XLA Modules:
  0.0 119.1 jit_solution(15599377299403462133)
XLA Ops:
  0.0 0.8 shift-right-arithmetic_convert_fusion
  0.8 0.1 fusion.7
  0.8 0.9 constant_dynamic-slice_fusion.5
  1.7 1.1 constant_dynamic-slice_fusion.7
  2.8 0.0 copy-start.11
  2.8 0.0 copy-start.5
  2.9 8.9 %collective-permute-start = (bf16[152,512]{1,0:T(8,128)(2,1)S(1)}, bf16[152,512]{1,0:T(8,128)(2,1)S(1)}, u32[]{:S(2)}, u32[]{:S(2)}) collective-permute-start(bf16[152,512]{1,0:T(8,128)(2,1)S(1)} %pad_maximum_fusion.3), channel_id=1, source_target_pairs={{0,16},{16,0},{1,17},{17,1},{2,18},{18,2},{3,19},{19,3},{4,20},{20... | collective-permute-start | bytes 466952 | tf_op jit(solution)/shard_map/ppermute | solution.py:199
  11.8 1.9 %collective-permute-start.1 = (bf16[8,512,128]{2,1,0:T(8,128)(2,1)}, bf16[8,512,128]{2,1,0:T(8,128)(2,1)S(1)}, u32[]{:S(2)}, u32[]{:S(2)}) collective-permute-start(bf16[8,512,128]{2,1,0:T(8,128)(2,1)} %param.11), channel_id=1, source_target_pairs={{0,0},{1,1},{2,16},{3,17},{16,2},{17,3},{18,18},{19,19},{4,4},{5,5... | collective-permute-start | bytes 3145736 | tf_op jit(solution)/shard_map/ppermute | solution.py:225
  13.7 1.4 %slice_reduce_fusion = s32[]{:T(128)} fusion(s32[2,32]{1,0:T(2,128)} %param.10), kind=kLoop, calls=%fused_computation.34 | loop fusion | flops 1 | bytes 12 | tf_op jit(solution)/shard_map/reduce_max | solution.py:187
  15.8 0.0 collective-permute-done
  15.9 0.1 slice_select_fusion
  15.9 0.1 slice_bitcast_fusion.1
  16.0 0.1 select_reduce_fusion
  16.2 0.0 copy-start.4
  16.2 0.6 copy-done.10
  16.9 0.1 reshape.65
  17.1 0.7 fusion.1
  17.8 12.2 %all-to-all-start = ((bf16[16,8,512]{2,1,0:T(8,128)(2,1)}), bf16[16,8,512]{2,1,0:T(8,128)(2,1)S(1)}, u32[]{:S(2)}, u32[]{:S(2)}) async-start(bf16[16,8,512]{2,1,0:T(8,128)(2,1)} %fusion.1), calls=%async_computation | async-start | bytes 262144 | tf_op jit(solution)/shard_map/all_to_all | solution.py:218
  30.0 0.7 constant_dynamic-slice_fusion.3
  31.4 0.1 constant_dynamic-slice_fusion
  31.5 11.5 %all-to-all-done.first_ref = bf16[16,8,512]{2,1,0:T(8,128)(2,1)S(1)} async-done(((bf16[16,8,512]{2,1,0:T(8,128)(2,1)}), bf16[16,8,512]{2,1,0:T(8,128)(2,1)S(1)}, u32[]{:S(2)}, u32[]{:S(2)}) %all-to-all-start) | async-done | bytes 131104 | tf_op jit(solution)/shard_map/all_to_all | solution.py:218
  43.0 0.0 collective-permute-done.1.w_ref
  43.0 0.6 copy-done.7
  43.7 2.4 %shard_map.64 = bf16[16,24,512]{2,1,0:T(8,128)(2,1)} custom-call(s32[1]{0:T(128)} %bitcast.2.hot_ref, bf16[16,8,512]{2,1,0:T(8,128)(2,1)} %copy-done.7, bf16[32,8,512]{2,1,0:T(8,128)(2,1)} %copy-done.4, bf16[32,512]{1,0:T(8,128)(2,1)} %copy-done.10), custom_call_target="tpu_custom_call" | custom-call | tf_op jit(solution)/shard_map/pallas_call | solution.py:239
  46.1 3.7 %all-to-all-start.1 = ((bf16[16,24,512]{2,1,0:T(8,128)(2,1)}), bf16[16,24,512]{2,1,0:T(8,128)(2,1)S(1)}, u32[]{:S(2)}, u32[]{:S(2)}) async-start(bf16[16,24,512]{2,1,0:T(8,128)(2,1)} %shard_map.64), calls=%async_computation.1 | async-start | bytes 786432 | tf_op jit(solution)/shard_map/all_to_all | solution.py:245
  49.9 4.7 %collective-permute-start.2 = (bf16[64,4608]{1,0:T(8,128)(2,1)S(1)}, bf16[64,4608]{1,0:T(8,128)(2,1)S(1)}, u32[]{:S(2)}, u32[]{:S(2)}) collective-permute-start(bf16[64,4608]{1,0:T(8,128)(2,1)S(1)} %pad_maximum_fusion), channel_id=1, source_target_pairs={{0,0},{1,1},{2,16},{3,17},{16,2},{17,3},{18,18},{19,19},{4,4},{5,5... | collective-permute-start | bytes 1769480 | tf_op jit(solution)/shard_map/ppermute | solution.py:237
  54.7 3.1 %collective-permute-start.3 = (bf16[64,4608]{1,0:T(8,128)(2,1)S(1)}, bf16[64,4608]{1,0:T(8,128)(2,1)}, u32[]{:S(2)}, u32[]{:S(2)}) collective-permute-start(bf16[64,4608]{1,0:T(8,128)(2,1)S(1)} %pad_maximum_fusion.1), channel_id=1, source_target_pairs={{0,1},{1,0},{2,17},{3,16},{16,3},{17,2},{18,19},{19,18},{4,5},{5,4... | collective-permute-start | bytes 1769480 | tf_op jit(solution)/shard_map/ppermute | solution.py:237
  57.8 3.6 %collective-permute-start.4 = (bf16[8,512,128]{2,1,0:T(8,128)(2,1)}, bf16[8,512,128]{2,1,0:T(8,128)(2,1)}, u32[]{:S(2)}, u32[]{:S(2)}) collective-permute-start(bf16[8,512,128]{2,1,0:T(8,128)(2,1)} %param.11), channel_id=1, source_target_pairs={{0,1},{1,0},{2,17},{3,16},{16,3},{17,2},{18,19},{19,18},{4,5},{5,4... | collective-permute-start | bytes 3145736 | tf_op jit(solution)/shard_map/ppermute | solution.py:225
  61.5 7.7 %collective-permute-done.2.q_ref = bf16[64,4608]{1,0:T(8,128)(2,1)S(1)} collective-permute-done((bf16[64,4608]{1,0:T(8,128)(2,1)S(1)}, bf16[64,4608]{1,0:T(8,128)(2,1)S(1)}, u32[]{:S(2)}, u32[]{:S(2)}) %collective-permute-start.2) | collective-permute-done | bytes 589856 | tf_op jit(solution)/shard_map/ppermute | solution.py:237
  69.2 2.2 %collective-permute-done.3.q_ref = bf16[64,4608]{1,0:T(8,128)(2,1)} collective-permute-done((bf16[64,4608]{1,0:T(8,128)(2,1)S(1)}, bf16[64,4608]{1,0:T(8,128)(2,1)}, u32[]{:S(2)}, u32[]{:S(2)}) %collective-permute-start.3) | collective-permute-done | bytes 589856 | tf_op jit(solution)/shard_map/ppermute | solution.py:237
  71.4 0.0 all-to-all-done.1.got_ref
  71.5 0.8 copy-done.3
  72.2 3.0 %shard_map.65 = bf16[4,288,512]{2,1,0:T(8,128)(2,1)} custom-call(s32[24]{0:T(128)} %copy-done.12, bf16[16,24,512]{2,1,0:T(8,128)(2,1)} %copy-done.3), custom_call_target="tpu_custom_call" | custom-call | tf_op jit(solution)/shard_map/pallas_call | solution.py:248
  75.3 4.2 %all-to-all-start.2 = ((bf16[4,288,512]{2,1,0:T(8,128)(2,1)}), bf16[4,288,512]{2,1,0:T(8,128)(2,1)S(1)}, u32[]{:S(2)}, u32[]{:S(2)}) async-start(bf16[4,288,512]{2,1,0:T(8,128)(2,1)} %shard_map.65), calls=%async_computation.2 | async-start | bytes 2359296 | tf_op jit(solution)/shard_map/all_to_all | solution.py:272
  79.5 2.0 %shard_map.66.q0_ref.q_ref = bf16[512,640]{1,0:T(8,128)(2,1)} custom-call(bf16[64,4608]{1,0:T(8,128)(2,1)} %copy-done.6), custom_call_target="tpu_custom_call" | custom-call | tf_op jit(solution)/shard_map/pallas_call | solution.py:260
  81.5 2.1 %shard_map.67.q1_ref.q_ref = bf16[512,640]{1,0:T(8,128)(2,1)} custom-call(bf16[64,4608]{1,0:T(8,128)(2,1)} %collective-permute-done.3.q_ref), custom_call_target="tpu_custom_call" | custom-call | tf_op jit(solution)/shard_map/pallas_call | solution.py:260
  83.6 0.0 collective-permute-done.4.w_ref
  83.6 7.6 %all-to-all-done.2.mine_ref = bf16[4,288,512]{2,1,0:T(8,128)(2,1)S(1)} async-done(((bf16[4,288,512]{2,1,0:T(8,128)(2,1)}), bf16[4,288,512]{2,1,0:T(8,128)(2,1)S(1)}, u32[]{:S(2)}, u32[]{:S(2)}) %all-to-all-start.2) | async-done | bytes 1179680 | tf_op jit(solution)/shard_map/all_to_all | solution.py:272
  91.2 7.6 %collective-permute-start.5 = (bf16[4,288,512]{2,1,0:T(8,128)(2,1)S(1)}, bf16[4,288,512]{2,1,0:T(8,128)(2,1)S(1)}, u32[]{:S(2)}, u32[]{:S(2)}) collective-permute-start(bf16[4,288,512]{2,1,0:T(8,128)(2,1)S(1)} %all-to-all-done.2.mine_ref), channel_id=1, source_target_pairs={{0,16},{16,0},{1,17},{17,1},{2,18},{18,2},{3,19},{19,3},{4,20},{20... | collective-permute-start | bytes 3538952 | tf_op jit(solution)/shard_map/ppermute | solution.py:274
  98.8 1.1 copy-done
  99.9 3.7 %shard_map.68 = (f32[512,512]{1,0:T(8,128)S(1)}, f32[512,256]{1,0:T(8,128)S(1)}, f32[512,512]{1,0:T(8,128)S(1)}, f32[512,256]{1,0:T(8,128)S(1)}) custom-call(bf16[512,640]{1,0:T(8,128)(2,1)S(1)} %copy-done.2, bf16[512,640]{1,0:T(8,128)(2,1)S(1)} %copy-done, bf16[4,288,512]{2,1,0:T(8,128)(2,1)S(1)} %all-to-all-done.2.mine_ref), custom_call_target="tpu_custom_call" | custom-call | tf_op jit(solution)/shard_map/pallas_call | solution.py:285
  103.6 2.6 %shard_map.69 = bf16[64,1024]{1,0:T(8,128)(2,1)S(1)} custom-call(bf16[512,640]{1,0:T(8,128)(2,1)S(1)} %copy-done.2, bf16[4,288,512]{2,1,0:T(8,128)(2,1)S(1)} %collective-permute-done.5.other_ref, f32[512,512]{1,0:T(8,128)S(1)} %get-tuple-element.29.blend_ref, f32[512,256]{1,0:T(8,128)S(1)} %get-tuple-element.30.stat_ref, ...), custom_call_target="tpu_custom_call" | custom-call | tf_op jit(solution)/shard_map/pallas_call | solution.py:295
  106.3 1.9 %collective-permute-start.6 = (bf16[64,1024]{1,0:T(8,128)(2,1)S(1)}, bf16[64,1024]{1,0:T(8,128)(2,1)S(1)}, u32[]{:S(2)}, u32[]{:S(2)}) collective-permute-start(bf16[64,1024]{1,0:T(8,128)(2,1)S(1)} %shard_map.69), channel_id=1, source_target_pairs={{0,0},{1,1},{16,2},{17,3},{2,16},{3,17},{18,18},{19,19},{4,4},{5,5... | collective-permute-start | bytes 393224 | tf_op jit(solution)/shard_map/ppermute | solution.py:304
  108.2 2.5 %shard_map.70 = bf16[64,1024]{1,0:T(8,128)(2,1)S(1)} custom-call(bf16[512,640]{1,0:T(8,128)(2,1)S(1)} %copy-done.1, bf16[4,288,512]{2,1,0:T(8,128)(2,1)S(1)} %collective-permute-done.5.other_ref, f32[512,512]{1,0:T(8,128)S(1)} %get-tuple-element.32.blend_ref, f32[512,256]{1,0:T(8,128)S(1)} %get-tuple-element.33.stat_ref, ...), custom_call_target="tpu_custom_call" | custom-call | tf_op jit(solution)/shard_map/pallas_call | solution.py:295
  110.8 4.9 %collective-permute-start.7 = (bf16[64,1024]{1,0:T(8,128)(2,1)S(1)}, bf16[64,1024]{1,0:T(8,128)(2,1)S(1)}, u32[]{:S(2)}, u32[]{:S(2)}) collective-permute-start(bf16[64,1024]{1,0:T(8,128)(2,1)S(1)} %shard_map.70), channel_id=1, source_target_pairs={{1,0},{0,1},{17,2},{16,3},{3,16},{2,17},{19,18},{18,19},{5,4},{4,5... | collective-permute-start | bytes 393224 | tf_op jit(solution)/shard_map/ppermute | solution.py:304
  115.7 0.0 collective-permute-done.6
  115.7 2.6 %collective-permute-done.7 = bf16[64,1024]{1,0:T(8,128)(2,1)S(1)} collective-permute-done((bf16[64,1024]{1,0:T(8,128)(2,1)S(1)}, bf16[64,1024]{1,0:T(8,128)(2,1)S(1)}, u32[]{:S(2)}, u32[]{:S(2)}) %collective-permute-start.7) | collective-permute-done | bytes 131104 | tf_op jit(solution)/shard_map/ppermute | solution.py:304
  118.4 0.7 pad_maximum_fusion.2
  (36 shorter events, 0.3 us)
Async XLA Ops:
  2.8 27.1 %copy-start.11 = (bf16[128,512]{1,0:T(8,128)(2,1)S(1)}, bf16[128,512]{1,0:T(8,128)(2,1)}, u32[]{:S(2)}) copy-start(bf16[128,512]{1,0:T(8,128)(2,1)} %param.7) | copy-start | bytes 393220
  2.8 28.5 %copy-start.5 = (bf16[128,4096]{1,0:T(8,128)(2,1)S(1)}, bf16[128,4096]{1,0:T(8,128)(2,1)}, u32[]{:S(2)}) copy-start(bf16[128,4096]{1,0:T(8,128)(2,1)} %param.6) | copy-start | bytes 3145732
  2.9 13.0 %collective-permute-start = (bf16[152,512]{1,0:T(8,128)(2,1)S(1)}, bf16[152,512]{1,0:T(8,128)(2,1)S(1)}, u32[]{:S(2)}, u32[]{:S(2)}) collective-permute-start(bf16[152,512]{1,0:T(8,128)(2,1)S(1)} %pad_maximum_fusion.3), channel_id=1, source_target_pairs={{0,16},{16,0},{1,17},{17,1},{2,18},{18,2},{3,19},{19,3},{4,20},{20... | collective-permute-start | bytes 466952 | tf_op jit(solution)/shard_map/ppermute | solution.py:199
  11.8 31.2 %collective-permute-start.1 = (bf16[8,512,128]{2,1,0:T(8,128)(2,1)}, bf16[8,512,128]{2,1,0:T(8,128)(2,1)S(1)}, u32[]{:S(2)}, u32[]{:S(2)}) collective-permute-start(bf16[8,512,128]{2,1,0:T(8,128)(2,1)} %param.11), channel_id=1, source_target_pairs={{0,0},{1,1},{2,16},{3,17},{16,2},{17,3},{18,18},{19,19},{4,4},{5,5... | collective-permute-start | bytes 3145736 | tf_op jit(solution)/shard_map/ppermute | solution.py:225
  16.0 15.4 %copy-start.12 = (s32[24]{0:T(128)}, s32[24]{0:T(128)S(1)}, u32[]{:S(2)}) copy-start(s32[24]{0:T(128)S(1)} %get-tuple-element.48.owners_ref) | copy-start | bytes 292
  16.2 15.3 %copy-start.4 = (bf16[32,8,512]{2,1,0:T(8,128)(2,1)}, bf16[32,8,512]{2,1,0:T(8,128)(2,1)S(1)}, u32[]{:S(2)}) copy-start(bf16[32,8,512]{2,1,0:T(8,128)(2,1)S(1)} %maximum_select_fusion.lat_ref) | copy-start | bytes 786436
  16.2 0.6 copy-start.10
  17.8 25.2 %all-to-all-start = ((bf16[16,8,512]{2,1,0:T(8,128)(2,1)}), bf16[16,8,512]{2,1,0:T(8,128)(2,1)S(1)}, u32[]{:S(2)}, u32[]{:S(2)}) async-start(bf16[16,8,512]{2,1,0:T(8,128)(2,1)} %fusion.1), calls=%async_computation | async-start | bytes 262144 | tf_op jit(solution)/shard_map/all_to_all | solution.py:218
  31.5 18.3 %copy-start.9 = (bf16[64,512]{1,0:T(8,128)(2,1)S(1)}, bf16[64,512]{1,0:T(8,128)(2,1)}, u32[]{:S(2)}) copy-start(bf16[64,512]{1,0:T(8,128)(2,1)} %get-tuple-element.42) | copy-start | bytes 196612
  43.0 0.7 copy-start.7
  46.1 8.5 %copy-start.8 = (bf16[64,512]{1,0:T(8,128)(2,1)S(1)}, bf16[64,512]{1,0:T(8,128)(2,1)}, u32[]{:S(2)}) copy-start(bf16[64,512]{1,0:T(8,128)(2,1)} %get-tuple-element.41) | copy-start | bytes 196612
  46.1 25.4 %all-to-all-start.1 = ((bf16[16,24,512]{2,1,0:T(8,128)(2,1)}), bf16[16,24,512]{2,1,0:T(8,128)(2,1)S(1)}, u32[]{:S(2)}, u32[]{:S(2)}) async-start(bf16[16,24,512]{2,1,0:T(8,128)(2,1)} %shard_map.64), calls=%async_computation.1 | async-start | bytes 786432 | tf_op jit(solution)/shard_map/all_to_all | solution.py:245
  49.9 19.3 %collective-permute-start.2 = (bf16[64,4608]{1,0:T(8,128)(2,1)S(1)}, bf16[64,4608]{1,0:T(8,128)(2,1)S(1)}, u32[]{:S(2)}, u32[]{:S(2)}) collective-permute-start(bf16[64,4608]{1,0:T(8,128)(2,1)S(1)} %pad_maximum_fusion), channel_id=1, source_target_pairs={{0,0},{1,1},{2,16},{3,17},{16,2},{17,3},{18,18},{19,19},{4,4},{5,5... | collective-permute-start | bytes 1769480 | tf_op jit(solution)/shard_map/ppermute | solution.py:237
  54.7 16.8 %collective-permute-start.3 = (bf16[64,4608]{1,0:T(8,128)(2,1)S(1)}, bf16[64,4608]{1,0:T(8,128)(2,1)}, u32[]{:S(2)}, u32[]{:S(2)}) collective-permute-start(bf16[64,4608]{1,0:T(8,128)(2,1)S(1)} %pad_maximum_fusion.1), channel_id=1, source_target_pairs={{0,1},{1,0},{2,17},{3,16},{16,3},{17,2},{18,19},{19,18},{4,5},{5,4... | collective-permute-start | bytes 1769480 | tf_op jit(solution)/shard_map/ppermute | solution.py:237
  57.8 25.8 %collective-permute-start.4 = (bf16[8,512,128]{2,1,0:T(8,128)(2,1)}, bf16[8,512,128]{2,1,0:T(8,128)(2,1)}, u32[]{:S(2)}, u32[]{:S(2)}) collective-permute-start(bf16[8,512,128]{2,1,0:T(8,128)(2,1)} %param.11), channel_id=1, source_target_pairs={{0,1},{1,0},{2,17},{3,16},{16,3},{17,2},{18,19},{19,18},{4,5},{5,4... | collective-permute-start | bytes 3145736 | tf_op jit(solution)/shard_map/ppermute | solution.py:225
  69.2 10.3 %copy-start.6 = (bf16[64,4608]{1,0:T(8,128)(2,1)}, bf16[64,4608]{1,0:T(8,128)(2,1)S(1)}, u32[]{:S(2)}) copy-start(bf16[64,4608]{1,0:T(8,128)(2,1)S(1)} %collective-permute-done.2.q_ref) | copy-start | bytes 1769476
  71.4 0.8 copy-start.3
  75.3 16.0 %all-to-all-start.2 = ((bf16[4,288,512]{2,1,0:T(8,128)(2,1)}), bf16[4,288,512]{2,1,0:T(8,128)(2,1)S(1)}, u32[]{:S(2)}, u32[]{:S(2)}) async-start(bf16[4,288,512]{2,1,0:T(8,128)(2,1)} %shard_map.65), calls=%async_computation.2 | async-start | bytes 2359296 | tf_op jit(solution)/shard_map/all_to_all | solution.py:272
  81.5 17.3 %copy-start.2 = (bf16[512,640]{1,0:T(8,128)(2,1)S(1)}, bf16[512,640]{1,0:T(8,128)(2,1)}, u32[]{:S(2)}) copy-start(bf16[512,640]{1,0:T(8,128)(2,1)} %shard_map.66.q0_ref.q_ref) | copy-start | bytes 1966084
  91.2 12.4 %collective-permute-start.5 = (bf16[4,288,512]{2,1,0:T(8,128)(2,1)S(1)}, bf16[4,288,512]{2,1,0:T(8,128)(2,1)S(1)}, u32[]{:S(2)}, u32[]{:S(2)}) collective-permute-start(bf16[4,288,512]{2,1,0:T(8,128)(2,1)S(1)} %all-to-all-done.2.mine_ref), channel_id=1, source_target_pairs={{0,16},{16,0},{1,17},{17,1},{2,18},{18,2},{3,19},{19,3},{4,20},{20... | collective-permute-start | bytes 3538952 | tf_op jit(solution)/shard_map/ppermute | solution.py:274
  98.8 1.1 copy-start
  103.6 4.6 %copy-start.1 = (bf16[512,640]{1,0:T(8,128)(2,1)S(1)}, bf16[512,640]{1,0:T(8,128)(2,1)}, u32[]{:S(2)}) copy-start(bf16[512,640]{1,0:T(8,128)(2,1)} %shard_map.67.q1_ref.q_ref) | copy-start | bytes 1966084
  106.3 9.4 %collective-permute-start.6 = (bf16[64,1024]{1,0:T(8,128)(2,1)S(1)}, bf16[64,1024]{1,0:T(8,128)(2,1)S(1)}, u32[]{:S(2)}, u32[]{:S(2)}) collective-permute-start(bf16[64,1024]{1,0:T(8,128)(2,1)S(1)} %shard_map.69), channel_id=1, source_target_pairs={{0,0},{1,1},{16,2},{17,3},{2,16},{3,17},{18,18},{19,19},{4,4},{5,5... | collective-permute-start | bytes 393224 | tf_op jit(solution)/shard_map/ppermute | solution.py:304
  110.8 7.6 %collective-permute-start.7 = (bf16[64,1024]{1,0:T(8,128)(2,1)S(1)}, bf16[64,1024]{1,0:T(8,128)(2,1)S(1)}, u32[]{:S(2)}, u32[]{:S(2)}) collective-permute-start(bf16[64,1024]{1,0:T(8,128)(2,1)S(1)} %shard_map.70), channel_id=1, source_target_pairs={{1,0},{0,1},{17,2},{16,3},{3,16},{2,17},{19,18},{18,19},{5,4},{4,5... | collective-permute-start | bytes 393224 | tf_op jit(solution)/shard_map/ppermute | solution.py:304

commit v4 on v3

--- a/solution.py
+++ b/solution.py
@@ -59,9 +59,7 @@
         out_ref[z, 16:24, :] = (rope[z * 8 : z * 8 + 8] + hot).astype(bf16)
 
 
-def share_kernel(owners_ref, got_ref, out_ref, got, rows, sems):
-    copy = pltpu.make_async_copy(got_ref, got, sems.at[0])
-    copy.start()
+def share_kernel(owners_ref, got_ref, out_ref):
     row = iota((256, 1), 0)
     slot, token = row % 32, row // 32
     index = (slot - COLD) * (2 * PACK) + token // 4 * PACK + 20 + token % 4
@@ -74,57 +72,35 @@
         rope_index = jnp.where(rope_slot == i, at + 16 + side, rope_index)
     lat = one_hot(index, 16 * PACK)
     rope = one_hot(rope_index, 16 * PACK)
-    copy.wait()
-    table = got[...].reshape(16 * PACK, LAT)
-    rows[0:256, :] = pick(lat, table).astype(bf16)
-    rows[256:ROWS, :] = pick(rope, table).astype(bf16)
-    copies = [pltpu.make_async_copy(rows, out_ref.at[n], sems.at[n]) for n in range(4)]
-    for copy in copies:
-        copy.start()
-    for copy in copies:
-        copy.wait()
-
-
-def layout_kernel(q_ref, out_ref, q, sem):
-    copy = pltpu.make_async_copy(q_ref, q, sem)
-    copy.start()
-    copy.wait()
+    table = got_ref[...].reshape(16 * PACK, LAT)
+    lat = pick(lat, table).astype(bf16)
+    rope = pick(rope, table).astype(bf16)
+    for n in range(4):
+        out_ref[n, 0:256, :] = lat
+        out_ref[n, 256:ROWS, :] = rope
+
+
+def layout_kernel(q_ref, out_ref):
     for h in range(HEADS):
         base = HEADS * LAT + h * ROPE
         rows = pl.ds(h * QB, QB)
-        part = q[:, base : base + ROPE]
-        out_ref[rows, 0:LAT] = q[:, h * LAT : (h + 1) * LAT]
+        part = q_ref[:, base : base + ROPE]
+        out_ref[rows, 0:LAT] = q_ref[:, h * LAT : (h + 1) * LAT]
         out_ref[rows, LAT:WIDE] = jnp.concatenate([part, part], axis=1)
 
 
-def bring(ref, keys, ropes, sems):
-    copies = []
-    for n in range(4):
-        copies.append(pltpu.make_async_copy(ref.at[n, 0:256], keys.at[n], sems.at[n]))
-        copies.append(pltpu.make_async_copy(ref.at[n, 256:ROWS], ropes.at[n], sems.at[4 + n]))
-    for copy in copies:
-        copy.start()
-    return copies
-
-
-def spread(ropes, places):
+def attend(q_ref, ref, places):
     lane = iota((32, 2 * ROPE), 1)
+    scores = []
     for n in range(4):
         for t in range(SHARE):
-            pair = ropes[n, :, t // 2 * 128 : t // 2 * 128 + 128]
+            pair = ref[n, 256:ROWS, t // 2 * 128 : t // 2 * 128 + 128]
             own = lane < ROPE if t % 2 == 0 else lane >= ROPE
             places[n, t * 32 : t * 32 + 32, :] = jnp.where(own, pair, 0)
-
-
-def attend(q_ref, keys, places):
-    scores = []
-    for n in range(4):
+        keys = jnp.concatenate([ref[n, 0:256, :], places[n]], axis=1)
         scores.append(
             lax.dot_general(
-                q_ref[...],
-                jnp.concatenate([keys[n], places[n]], axis=1),
-                (((1,), (1,)), ((), ())),
-                preferred_element_type=f32,
+                q_ref[...], keys, (((1,), (1,)), ((), ())), preferred_element_type=f32
             )
         )
     top = jnp.maximum(jnp.maximum(scores[0], scores[1]), jnp.maximum(scores[2], scores[3]))
@@ -134,44 +110,31 @@
     for n, s in enumerate(scores):
         p = jnp.exp2(s * (SCORE_SCALE * LOG2E) - top)
         total = total + p
-        blended = blended + jnp.dot(p.astype(bf16), keys[n], preferred_element_type=f32)
+        blended = blended + jnp.dot(p.astype(bf16), ref[n, 0:256, :], preferred_element_type=f32)
     return top, jnp.sum(total, axis=1, keepdims=True), blended
 
 
 def first_half_kernel(
-    q0_ref, q1_ref, mine_ref, blend0_ref, stat0_ref, blend1_ref, stat1_ref, keys, ropes, places, sems
+    q0_ref, q1_ref, mine_ref, blend0_ref, stat0_ref, blend1_ref, stat1_ref, places
 ):
-    copies = bring(mine_ref, keys, ropes, sems)
-    for copy in copies:
-        copy.wait()
-    spread(ropes, places)
     outs = ((q0_ref, blend0_ref, stat0_ref), (q1_ref, blend1_ref, stat1_ref))
     for q_ref, blend_ref, stat_ref in outs:
-        top, total, blended = attend(q_ref, keys, places)
+        top, total, blended = attend(q_ref, mine_ref, places)
         blend_ref[...] = blended
         stat_ref[:, 0:128] = jnp.broadcast_to(top, (HEADS * QB, 128))
         stat_ref[:, 128:256] = jnp.broadcast_to(total, (HEADS * QB, 128))
 
 
-def second_half_kernel(
-    q_ref, other_ref, blend_ref, stat_ref, w_ref, o_ref, keys, ropes, places, w, sems
-):
-    copies = bring(other_ref, keys, ropes, sems)
-    up = pltpu.make_async_copy(w_ref, w, sems.at[8])
-    up.start()
-    for copy in copies:
-        copy.wait()
-    spread(ropes, places)
-    top, total, blended = attend(q_ref, keys, places)
+def second_half_kernel(q_ref, other_ref, blend_ref, stat_ref, w_ref, o_ref, places):
+    top, total, blended = attend(q_ref, other_ref, places)
     top0, total0 = stat_ref[:, 0:1], stat_ref[:, 128:129]
     both = jnp.maximum(top, top0)
     mine, other = jnp.exp2(top0 - both), jnp.exp2(top - both)
     scale = 1.0 / (total0 * mine + total * other)
     latent = (blend_ref[...] * (mine * scale) + blended * (other * scale)).astype(bf16)
-    up.wait()
     for h in range(HEADS):
         o_ref[:, h * VH : (h + 1) * VH] = jnp.dot(
-            latent[h * QB : (h + 1) * QB], w[h], preferred_element_type=f32
+            latent[h * QB : (h + 1) * QB], w_ref[h], preferred_element_type=f32
         ).astype(bf16)
 
 
@@ -179,7 +142,7 @@
     z, k, y, x = (lax.axis_index(a) for a in ("z", "core", "y", "x"))
     vmem = pl.BlockSpec(memory_space=pltpu.VMEM)
     smem = pl.BlockSpec(memory_space=pltpu.SMEM)
-    anywhere = pl.BlockSpec(memory_space=pl.ANY)
+    params = pltpu.CompilerParams(vmem_limit_bytes=12 * 1024 * 1024)
     swap = [(0, 1), (1, 0)]
 
     lat = lax.dynamic_slice_in_dim(kv_latent, y * 16, 16, 1)
@@ -214,7 +177,7 @@
     hot_rope = jnp.broadcast_to(hot_rope[:, None, None, :], (HOT, 2, 1, LAT)).reshape(16, 1, LAT)
     wants = jnp.pad(wants.astype(bf16)[:, None, :], ((0, 0), (0, 2), (0, LAT - 2)))
     first = jnp.concatenate([hot, hot_rope, wants], axis=1)
-    first, w_later = lax.optimization_barrier((first, w_uv))
+    first, w_uv, q_latent, q_rope = lax.optimization_barrier((first, w_uv, q_latent, q_rope))
     first = lax.all_to_all(first, "z", split_axis=0, concat_axis=0, tiled=True)
 
     def pairs(r):
@@ -222,8 +185,6 @@
             (c * 4 + s, (s // 2) * 4 + 2 * c + (s + r) % 2) for c in range(2) for s in range(4)
         ]
 
-    ups = [lax.ppermute(w, ("core", "x"), pairs(r)) for r, w in enumerate((w_uv, w_later))]
-    first, ups[0] = lax.optimization_barrier((first, ups[0]))
     queries = []
     for r in range(2):
         m = (x + r) % 2
@@ -234,60 +195,53 @@
             ],
             axis=1,
         )
-        queries.append(lax.ppermute(part, ("core", "x"), pairs(r)))
+        queries.append(part)
+
+    def travel(r):
+        return pl.pallas_call(
+            layout_kernel,
+            out_shape=jax.ShapeDtypeStruct((HEADS * QB, WIDE), bf16),
+            in_specs=[vmem],
+            out_specs=vmem,
+            compiler_params=params,
+        )(lax.ppermute(queries[r], ("core", "x"), pairs(r)))
+
+    ups = [lax.ppermute(w_uv, ("core", "x"), pairs(r)) for r in range(2)]
 
     second = pl.pallas_call(
         send_kernel,
         out_shape=jax.ShapeDtypeStruct((16, PACK, LAT), bf16),
         in_specs=[smem, vmem, vmem, vmem],
         out_specs=vmem,
+        compiler_params=params,
+        cost_estimate=pl.CostEstimate(flops=5000000000, bytes_accessed=0, transcendentals=0),
     )((hot_first >> 5)[None], first, lat, rope)
+    second, queries[0] = lax.optimization_barrier((second, travel(0)))
     second = lax.all_to_all(second, "z", split_axis=0, concat_axis=0, tiled=True)
-    second, queries = lax.optimization_barrier((second, queries))
 
     keys = pl.pallas_call(
         share_kernel,
         out_shape=jax.ShapeDtypeStruct((4, ROWS, LAT), bf16),
-        in_specs=[smem, anywhere],
-        out_specs=anywhere,
-        scratch_shapes=[
-            pltpu.VMEM((16, PACK, LAT), bf16),
-            pltpu.VMEM((ROWS, LAT), bf16),
-            pltpu.SemaphoreType.DMA((4,)),
-        ],
+        in_specs=[smem, vmem],
+        out_specs=vmem,
+        compiler_params=params,
     )(owners, second)
-    queries = [
-        pl.pallas_call(
-            layout_kernel,
-            out_shape=jax.ShapeDtypeStruct((HEADS * QB, WIDE), bf16),
-            in_specs=[anywhere],
-            out_specs=vmem,
-            scratch_shapes=[
-                pltpu.VMEM((QB, HEADS * (LAT + ROPE)), bf16),
-                pltpu.SemaphoreType.DMA,
-            ],
-        )(q)
-        for q in queries
-    ]
+    keys, queries[1] = lax.optimization_barrier((keys, queries[1]))
+    queries[1] = travel(1)
     mine = lax.all_to_all(keys, "y", split_axis=0, concat_axis=0, tiled=True)
-    mine, queries, ups[1] = lax.optimization_barrier((mine, queries, ups[1]))
+    mine, queries, ups = lax.optimization_barrier((mine, queries, ups))
     other = lax.ppermute(mine, "core", swap)
 
     rows = HEADS * QB
     blend = jax.ShapeDtypeStruct((rows, LAT), f32)
     stat = jax.ShapeDtypeStruct((rows, 256), f32)
-    scratch = [
-        pltpu.VMEM((4, 256, LAT), bf16),
-        pltpu.VMEM((4, 32, LAT), bf16),
-        pltpu.VMEM((4, 256, 2 * ROPE), bf16),
-    ]
-    params = pltpu.CompilerParams(vmem_limit_bytes=24 * 1024 * 1024)
+    scratch = [pltpu.VMEM((4, 256, 2 * ROPE), bf16)]
     halves = pl.pallas_call(
         first_half_kernel,
         out_shape=[blend, stat, blend, stat],
-        in_specs=[vmem, vmem, anywhere],
+        in_specs=[vmem] * 3,
         out_specs=[vmem] * 4,
-        scratch_shapes=scratch + [pltpu.SemaphoreType.DMA((8,))],
+        scratch_shapes=scratch,
         compiler_params=params,
     )(queries[0], queries[1], mine)
     outs = []
@@ -295,10 +249,9 @@
         out = pl.pallas_call(
             second_half_kernel,
             out_shape=jax.ShapeDtypeStruct((QB, HEADS * VH), bf16),
-            in_specs=[vmem, anywhere, vmem, vmem, anywhere],
+            in_specs=[vmem] * 5,
             out_specs=vmem,
-            scratch_shapes=scratch
-            + [pltpu.VMEM((HEADS, LAT, VH), bf16), pltpu.SemaphoreType.DMA((9,))],
+            scratch_shapes=scratch,
             compiler_params=params,
         )(queries[r], other, halves[2 * r], halves[2 * r + 1], ups[r])
         outs.append(lax.ppermute(out, ("core", "x"), [(d, s) for s, d in pairs(r)]))

time: 120 us -> 113 us (0.942); the launches traced: 119 us -> 111 us
  Pallas kernels: 18.4 us -> 11.4 us
  local copies, waits for them, and re-layouts: 6.18 us -> 4.03 us
  starting transfers between devices: 56.9 us -> 58.2 us
  waiting for transfers between devices: 31.8 us -> 30.5 us
    all_to_all x1, waiting for transfers between devices: 0.01 us -> 11.6 us  [local(): lax.all_to_all(second, 'z', split_axis=0, concat_axis=0, tiled=True)]
    all_to_all x1, waiting for transfers between devices: 7.64 us -> 0.01 us  [local(): mine = lax.all_to_all(keys, 'y', split_axis=0, concat_axis=0, tiled=True)]
    all_to_all x1, starting transfers between devices: 3.69 us -> 11.1 us  [local(): lax.all_to_all(second, 'z', split_axis=0, concat_axis=0, tiled=True)]
    ppermute x1, starting transfers between devices: 7.58 us -> 1.92 us  [local(): other = lax.ppermute(mine, 'core', swap)]
    all_to_all x1, waiting for transfers between devices: 11.5 us -> 6.18 us  [local(): first = lax.all_to_all(first, 'z', split_axis=0, concat_axis=0, tiled=True)]
    pallas_call x2, Pallas kernels: 4.09 us -> 0.21 us  [travel(): pl.pallas_call(layout_kernel, out_shape=jax.ShapeDtypeStruct((HEADS * QB,...]
    all_to_all x1, starting transfers between devices: 12.2 us -> 9.54 us  [local(): first = lax.all_to_all(first, 'z', split_axis=0, concat_axis=0, tiled=True)]
    ppermute x4, starting transfers between devices: 13.4 us -> 15.9 us  [the longest x2 8.58 us: travel(): lax.ppermute(queries[r], ('core', 'x'), pairs(r))]
  transfers between devices with their start and end apart: 11 -> 11, of which waited for: 5 -> 4; matrix products, arithmetic and copies ran while one was open for 3% -> 3% of each run, Pallas kernels for 11% -> 7%
where the time goes in v4:
time: 113 us; the launch traced here: 111 us
  starting transfers between devices  58.2 us (52%)
  waiting for transfers between devices  30.5 us (27%)
  Pallas kernels  11.4 us (10%)
  other arithmetic  4.83 us (4%)
  local copies, waits for them, and re-layouts  4.03 us (4%)
  between operations  1.59 us (1%)
    all_to_all x1, waiting for transfers between devices, local(): lax.all_to_all(second, 'z', split_axis=0, concat_axis=0, tiled=True)  11.6 us
    all_to_all x1, starting transfers between devices, local(): lax.all_to_all(second, 'z', split_axis=0, concat_axis=0, tiled=True)  11.1 us
    all_to_all x1, starting transfers between devices, local(): first = lax.all_to_all(first, 'z', split_axis=0, concat_axis=0, tiled=True)  9.54 us
    ppermute x1, starting transfers between devices, local(): swapped = lax.ppermute(theirs, 'core', swap)  8.92 us
    ppermute x2, waiting for transfers between devices, travel(): lax.ppermute(queries[r], ('core', 'x'), pairs(r))  8.65 us
    ppermute x2, starting transfers between devices, travel(): lax.ppermute(queries[r], ('core', 'x'), pairs(r))  8.58 us
    ppermute x2, starting transfers between devices, local(): ups = [lax.ppermute(w_uv, ('core', 'x'), pairs(r)) for r in range(2)]  7.32 us
    ppermute x2, starting transfers between devices, local(): outs.append(lax.ppermute(out, ('core', 'x'), [(d, s) for s, d in pairs(r)]))  6.51 us
  transfers between devices with their start and end apart: 11, of which 4 were waited for; matrix products, arithmetic and copies ran while one was open for 3% of the time, Pallas kernels for 7%

profile of v4, /device:TPU:1, one launch (start us, length us, event | category | flops | bytes accessed | tf_op | source)
XLA Modules:
  0.0 110.5 jit_solution(4459231098925708458)
XLA Ops:
  0.0 0.8 shift-right-arithmetic_convert_fusion
  0.8 0.1 fusion.7
  0.8 0.9 constant_dynamic-slice_fusion.5
  1.7 1.1 %constant_dynamic-slice_fusion.7 = (bf16[16,8,512]{2,1,0:T(8,128)(2,1)S(1)}, bf16[128,512]{1,0:T(8,128)(2,1)S(1)}) fusion(bf16[16,64,512]{2,1,0:T(8,128)(2,1)} %param.8, s32[]{:T(128)S(6)} %dynamic_slice.48, s32[]{:T(128)S(6)} %dynamic_slice.44), kind=kLoop, calls=%fused_computation.32 | loop fusion | bytes 524296 | tf_op jit(solution)/shard_map/dynamic_slice | solution.py:163
  2.8 0.0 copy-start.4
  2.8 0.0 copy-start.1
  2.9 8.9 %collective-permute-start = (bf16[152,512]{1,0:T(8,128)(2,1)S(1)}, bf16[152,512]{1,0:T(8,128)(2,1)S(1)}, u32[]{:S(2)}, u32[]{:S(2)}) collective-permute-start(bf16[152,512]{1,0:T(8,128)(2,1)S(1)} %pad_maximum_fusion.3), channel_id=1, source_target_pairs={{0,16},{16,0},{1,17},{17,1},{2,18},{18,2},{3,19},{19,3},{4,20},{20... | collective-permute-start | bytes 466952 | tf_op jit(solution)/shard_map/ppermute | solution.py:162
  11.8 1.3 %slice_reduce_fusion = s32[]{:T(128)} fusion(s32[2,32]{1,0:T(2,128)} %param.10), kind=kLoop, calls=%fused_computation.34 | loop fusion | flops 1 | bytes 12 | tf_op jit(solution)/shard_map/reduce_max | solution.py:150
  13.8 0.0 collective-permute-done
  13.8 0.1 slice_select_fusion
  13.9 0.1 slice_bitcast_fusion.1
  14.0 0.1 select_reduce_fusion
  14.1 0.1 reshape.65
  14.4 0.7 fusion.1
  15.1 9.5 %all-to-all-start = ((bf16[16,8,512]{2,1,0:T(8,128)(2,1)}), bf16[16,8,512]{2,1,0:T(8,128)(2,1)S(1)}, u32[]{:S(2)}, u32[]{:S(2)}) async-start(bf16[16,8,512]{2,1,0:T(8,128)(2,1)} %fusion.1), calls=%async_computation | async-start | bytes 262144 | tf_op jit(solution)/shard_map/all_to_all | solution.py:181
  24.7 0.0 copy-done.4
  24.7 0.6 constant_dynamic-slice_fusion.3
  25.3 0.0 copy-done.1
  25.3 0.1 constant_dynamic-slice_fusion
  25.5 4.8 %collective-permute-start.1 = (bf16[64,4608]{1,0:T(8,128)(2,1)S(1)}, bf16[64,4608]{1,0:T(8,128)(2,1)S(1)}, u32[]{:S(2)}, u32[]{:S(2)}) collective-permute-start(bf16[64,4608]{1,0:T(8,128)(2,1)S(1)} %pad_maximum_fusion), channel_id=1, source_target_pairs={{0,0},{1,1},{2,16},{3,17},{16,2},{17,3},{18,18},{19,19},{4,4},{5,5... | collective-permute-start | bytes 1769480 | tf_op jit(solution)/shard_map/ppermute | solution.py:207
  30.9 6.2 %all-to-all-done.first_ref = bf16[16,8,512]{2,1,0:T(8,128)(2,1)S(1)} async-done(((bf16[16,8,512]{2,1,0:T(8,128)(2,1)}), bf16[16,8,512]{2,1,0:T(8,128)(2,1)S(1)}, u32[]{:S(2)}, u32[]{:S(2)}) %all-to-all-start) | async-done | bytes 131104 | tf_op jit(solution)/shard_map/all_to_all | solution.py:181
  37.1 1.4 %shard_map.64 = bf16[16,24,512]{2,1,0:T(8,128)(2,1)} custom-call(s32[1]{0:T(128)} %bitcast.2.hot_ref, bf16[16,8,512]{2,1,0:T(8,128)(2,1)S(1)} %all-to-all-done.first_ref, bf16[32,8,512]{2,1,0:T(8,128)(2,1)S(1)} %maximum_select_fusion.lat_ref, bf16[32,512]{1,0:T(8,128)(2,1)S(1)} %maximum_select_fusion.1.rope_ref), custom_call_target="tpu_custom_call" | custom-call | flops 5000000000 | tf_op jit(solution)/shard_map/pallas_call | solution.py:211
  38.5 0.0 collective-permute-done.1.q_ref
  38.5 0.1 shard_map.65.q0_ref.q_ref
  38.7 11.1 %all-to-all-start.1 = ((bf16[16,24,512]{2,1,0:T(8,128)(2,1)}), bf16[16,24,512]{2,1,0:T(8,128)(2,1)S(1)}, u32[]{:S(2)}, u32[]{:S(2)}) async-start(bf16[16,24,512]{2,1,0:T(8,128)(2,1)} %shard_map.64), calls=%async_computation.1 | async-start | bytes 786432 | tf_op jit(solution)/shard_map/all_to_all | solution.py:220
  49.8 5.1 %collective-permute-start.4 = (bf16[8,512,128]{2,1,0:T(8,128)(2,1)}, bf16[8,512,128]{2,1,0:T(8,128)(2,1)S(1)}, u32[]{:S(2)}, u32[]{:S(2)}) collective-permute-start(bf16[8,512,128]{2,1,0:T(8,128)(2,1)} %param.11), channel_id=1, source_target_pairs={{0,1},{1,0},{2,17},{3,16},{16,3},{17,2},{18,19},{19,18},{4,5},{5,4... | collective-permute-start | bytes 3145736 | tf_op jit(solution)/shard_map/ppermute | solution.py:209
  54.9 2.2 %collective-permute-start.3 = (bf16[8,512,128]{2,1,0:T(8,128)(2,1)}, bf16[8,512,128]{2,1,0:T(8,128)(2,1)}, u32[]{:S(2)}, u32[]{:S(2)}) collective-permute-start(bf16[8,512,128]{2,1,0:T(8,128)(2,1)} %param.11), channel_id=1, source_target_pairs={{0,0},{1,1},{2,16},{3,17},{16,2},{17,3},{18,18},{19,19},{4,4},{5,5... | collective-permute-start | bytes 3145736 | tf_op jit(solution)/shard_map/ppermute | solution.py:209
  57.1 0.9 pad_maximum_fusion.1
  58.0 11.6 %all-to-all-done.1.got_ref = bf16[16,24,512]{2,1,0:T(8,128)(2,1)S(1)} async-done(((bf16[16,24,512]{2,1,0:T(8,128)(2,1)}), bf16[16,24,512]{2,1,0:T(8,128)(2,1)S(1)}, u32[]{:S(2)}, u32[]{:S(2)}) %all-to-all-start.1) | async-done | bytes 393248 | tf_op jit(solution)/shard_map/all_to_all | solution.py:220
  69.5 1.0 shard_map.66
  70.6 1.0 copy-done
  71.6 4.3 %all-to-all-start.2 = ((bf16[4,288,512]{2,1,0:T(8,128)(2,1)}), bf16[4,288,512]{2,1,0:T(8,128)(2,1)S(1)}, u32[]{:S(2)}, u32[]{:S(2)}) async-start(bf16[4,288,512]{2,1,0:T(8,128)(2,1)} %copy-done), calls=%async_computation.2 | async-start | bytes 2359296 | tf_op jit(solution)/shard_map/all_to_all | solution.py:231
  75.9 3.8 %collective-permute-start.2 = (bf16[64,4608]{1,0:T(8,128)(2,1)S(1)}, bf16[64,4608]{1,0:T(8,128)(2,1)S(1)}, u32[]{:S(2)}, u32[]{:S(2)}) collective-permute-start(bf16[64,4608]{1,0:T(8,128)(2,1)S(1)} %copy-done.2), channel_id=1, source_target_pairs={{0,1},{1,0},{2,17},{3,16},{16,3},{17,2},{18,19},{19,18},{4,5},{5,4... | collective-permute-start | bytes 1769480 | tf_op jit(solution)/shard_map/ppermute | solution.py:207
  79.7 8.6 %collective-permute-done.2.q_ref = bf16[64,4608]{1,0:T(8,128)(2,1)S(1)} collective-permute-done((bf16[64,4608]{1,0:T(8,128)(2,1)S(1)}, bf16[64,4608]{1,0:T(8,128)(2,1)S(1)}, u32[]{:S(2)}, u32[]{:S(2)}) %collective-permute-start.2) | collective-permute-done | bytes 589856 | tf_op jit(solution)/shard_map/ppermute | solution.py:207
  88.3 0.1 shard_map.67.q1_ref.q_ref
  88.4 0.0 collective-permute-done.4.w_ref
  88.4 0.0 collective-permute-done.3.w_ref
  88.4 0.0 all-to-all-done.2.mine_ref
  88.5 1.9 %collective-permute-start.5 = (bf16[4,288,512]{2,1,0:T(8,128)(2,1)S(1)}, bf16[4,288,512]{2,1,0:T(8,128)(2,1)S(1)}, u32[]{:S(2)}, u32[]{:S(2)}) collective-permute-start(bf16[4,288,512]{2,1,0:T(8,128)(2,1)S(1)} %all-to-all-done.2.mine_ref), channel_id=1, source_target_pairs={{0,16},{16,0},{1,17},{17,1},{2,18},{18,2},{3,19},{19,3},{4,20},{20... | collective-permute-start | bytes 3538952 | tf_op jit(solution)/shard_map/ppermute | solution.py:233
  90.4 3.4 %shard_map.68 = (f32[512,512]{1,0:T(8,128)S(1)}, f32[512,256]{1,0:T(8,128)S(1)}, f32[512,512]{1,0:T(8,128)S(1)}, f32[512,256]{1,0:T(8,128)S(1)}) custom-call(bf16[512,640]{1,0:T(8,128)(2,1)S(1)} %shard_map.65.q0_ref.q_ref, bf16[512,640]{1,0:T(8,128)(2,1)S(1)} %shard_map.67.q1_ref.q_ref, bf16[4,288,512]{2,1,0:T(8,128)(2,1)S(1)} %all-to-all-done.2.mine_ref), custom_call_target="tpu_custom_call" | custom-call | tf_op jit(solution)/shard_map/pallas_call | solution.py:239
  93.8 0.0 collective-permute-done.5.other_ref
  93.8 3.3 %shard_map.69 = bf16[64,1024]{1,0:T(8,128)(2,1)S(1)} custom-call(bf16[512,640]{1,0:T(8,128)(2,1)S(1)} %shard_map.65.q0_ref.q_ref, bf16[4,288,512]{2,1,0:T(8,128)(2,1)S(1)} %collective-permute-done.5.other_ref, f32[512,512]{1,0:T(8,128)S(1)} %get-tuple-element.33.blend_ref, f32[512,256]{1,0:T(8,128)S(1)} %get-tuple-element.34.stat_ref, ...), custom_call_target="tpu_custom_call" | custom-call | tf_op jit(solution)/shard_map/pallas_call | solution.py:249
  97.1 3.1 %collective-permute-start.6 = (bf16[64,1024]{1,0:T(8,128)(2,1)S(1)}, bf16[64,1024]{1,0:T(8,128)(2,1)S(1)}, u32[]{:S(2)}, u32[]{:S(2)}) collective-permute-start(bf16[64,1024]{1,0:T(8,128)(2,1)S(1)} %shard_map.69), channel_id=1, source_target_pairs={{0,0},{1,1},{16,2},{17,3},{2,16},{3,17},{18,18},{19,19},{4,4},{5,5... | collective-permute-start | bytes 393224 | tf_op jit(solution)/shard_map/ppermute | solution.py:257
  100.2 2.0 %shard_map.70 = bf16[64,1024]{1,0:T(8,128)(2,1)S(1)} custom-call(bf16[512,640]{1,0:T(8,128)(2,1)S(1)} %shard_map.67.q1_ref.q_ref, bf16[4,288,512]{2,1,0:T(8,128)(2,1)S(1)} %collective-permute-done.5.other_ref, f32[512,512]{1,0:T(8,128)S(1)} %get-tuple-element.36.blend_ref, f32[512,256]{1,0:T(8,128)S(1)} %get-tuple-element.37.stat_ref, ...), custom_call_target="tpu_custom_call" | custom-call | tf_op jit(solution)/shard_map/pallas_call | solution.py:249
  102.3 3.4 %collective-permute-start.7 = (bf16[64,1024]{1,0:T(8,128)(2,1)S(1)}, bf16[64,1024]{1,0:T(8,128)(2,1)S(1)}, u32[]{:S(2)}, u32[]{:S(2)}) collective-permute-start(bf16[64,1024]{1,0:T(8,128)(2,1)S(1)} %shard_map.70), channel_id=1, source_target_pairs={{1,0},{0,1},{17,2},{16,3},{3,16},{2,17},{19,18},{18,19},{5,4},{4,5... | collective-permute-start | bytes 393224 | tf_op jit(solution)/shard_map/ppermute | solution.py:257
  105.7 0.0 collective-permute-done.6
  105.7 4.1 %collective-permute-done.7 = bf16[64,1024]{1,0:T(8,128)(2,1)S(1)} collective-permute-done((bf16[64,1024]{1,0:T(8,128)(2,1)S(1)}, bf16[64,1024]{1,0:T(8,128)(2,1)S(1)}, u32[]{:S(2)}, u32[]{:S(2)}) %collective-permute-start.7) | collective-permute-done | bytes 131104 | tf_op jit(solution)/shard_map/ppermute | solution.py:257
  109.8 0.7 pad_maximum_fusion.2
  (20 shorter events, 0.3 us)
Async XLA Ops:
  2.8 21.8 %copy-start.4 = (bf16[128,512]{1,0:T(8,128)(2,1)S(1)}, bf16[128,512]{1,0:T(8,128)(2,1)}, u32[]{:S(2)}) copy-start(bf16[128,512]{1,0:T(8,128)(2,1)} %param.7) | copy-start | bytes 393220
  2.8 22.5 %copy-start.1 = (bf16[128,4096]{1,0:T(8,128)(2,1)S(1)}, bf16[128,4096]{1,0:T(8,128)(2,1)}, u32[]{:S(2)}) copy-start(bf16[128,4096]{1,0:T(8,128)(2,1)} %param.6) | copy-start | bytes 3145732
  2.9 10.9 %collective-permute-start = (bf16[152,512]{1,0:T(8,128)(2,1)S(1)}, bf16[152,512]{1,0:T(8,128)(2,1)S(1)}, u32[]{:S(2)}, u32[]{:S(2)}) collective-permute-start(bf16[152,512]{1,0:T(8,128)(2,1)S(1)} %pad_maximum_fusion.3), channel_id=1, source_target_pairs={{0,16},{16,0},{1,17},{17,1},{2,18},{18,2},{3,19},{19,3},{4,20},{20... | collective-permute-start | bytes 466952 | tf_op jit(solution)/shard_map/ppermute | solution.py:162
  15.1 22.0 %all-to-all-start = ((bf16[16,8,512]{2,1,0:T(8,128)(2,1)}), bf16[16,8,512]{2,1,0:T(8,128)(2,1)S(1)}, u32[]{:S(2)}, u32[]{:S(2)}) async-start(bf16[16,8,512]{2,1,0:T(8,128)(2,1)} %fusion.1), calls=%async_computation | async-start | bytes 262144 | tf_op jit(solution)/shard_map/all_to_all | solution.py:181
  25.5 13.1 %collective-permute-start.1 = (bf16[64,4608]{1,0:T(8,128)(2,1)S(1)}, bf16[64,4608]{1,0:T(8,128)(2,1)S(1)}, u32[]{:S(2)}, u32[]{:S(2)}) collective-permute-start(bf16[64,4608]{1,0:T(8,128)(2,1)S(1)} %pad_maximum_fusion), channel_id=1, source_target_pairs={{0,0},{1,1},{2,16},{3,17},{16,2},{17,3},{18,18},{19,19},{4,4},{5,5... | collective-permute-start | bytes 1769480 | tf_op jit(solution)/shard_map/ppermute | solution.py:207
  38.5 18.5 %copy-start.3 = (bf16[64,512]{1,0:T(8,128)(2,1)S(1)}, bf16[64,512]{1,0:T(8,128)(2,1)}, u32[]{:S(2)}) copy-start(bf16[64,512]{1,0:T(8,128)(2,1)} %get-tuple-element.45) | copy-start | bytes 196612
  38.7 30.9 %all-to-all-start.1 = ((bf16[16,24,512]{2,1,0:T(8,128)(2,1)}), bf16[16,24,512]{2,1,0:T(8,128)(2,1)S(1)}, u32[]{:S(2)}, u32[]{:S(2)}) async-start(bf16[16,24,512]{2,1,0:T(8,128)(2,1)} %shard_map.64), calls=%async_computation.1 | async-start | bytes 786432 | tf_op jit(solution)/shard_map/all_to_all | solution.py:220
  49.8 38.7 %collective-permute-start.4 = (bf16[8,512,128]{2,1,0:T(8,128)(2,1)}, bf16[8,512,128]{2,1,0:T(8,128)(2,1)S(1)}, u32[]{:S(2)}, u32[]{:S(2)}) collective-permute-start(bf16[8,512,128]{2,1,0:T(8,128)(2,1)} %param.11), channel_id=1, source_target_pairs={{0,1},{1,0},{2,17},{3,16},{16,3},{17,2},{18,19},{19,18},{4,5},{5,4... | collective-permute-start | bytes 3145736 | tf_op jit(solution)/shard_map/ppermute | solution.py:209
  54.9 33.6 %collective-permute-start.3 = (bf16[8,512,128]{2,1,0:T(8,128)(2,1)}, bf16[8,512,128]{2,1,0:T(8,128)(2,1)}, u32[]{:S(2)}, u32[]{:S(2)}) collective-permute-start(bf16[8,512,128]{2,1,0:T(8,128)(2,1)} %param.11), channel_id=1, source_target_pairs={{0,0},{1,1},{2,16},{3,17},{16,2},{17,3},{18,18},{19,19},{4,4},{5,5... | collective-permute-start | bytes 3145736 | tf_op jit(solution)/shard_map/ppermute | solution.py:209
  70.6 1.0 copy-start
  71.6 4.3 %copy-start.2 = (bf16[64,4608]{1,0:T(8,128)(2,1)S(1)}, bf16[64,4608]{1,0:T(8,128)(2,1)}, u32[]{:S(2)}) copy-start(bf16[64,4608]{1,0:T(8,128)(2,1)} %pad_maximum_fusion.1) | copy-start | bytes 1769476
  71.6 16.8 %all-to-all-start.2 = ((bf16[4,288,512]{2,1,0:T(8,128)(2,1)}), bf16[4,288,512]{2,1,0:T(8,128)(2,1)S(1)}, u32[]{:S(2)}, u32[]{:S(2)}) async-start(bf16[4,288,512]{2,1,0:T(8,128)(2,1)} %copy-done), calls=%async_computation.2 | async-start | bytes 2359296 | tf_op jit(solution)/shard_map/all_to_all | solution.py:231
  75.9 12.4 %collective-permute-start.2 = (bf16[64,4608]{1,0:T(8,128)(2,1)S(1)}, bf16[64,4608]{1,0:T(8,128)(2,1)S(1)}, u32[]{:S(2)}, u32[]{:S(2)}) collective-permute-start(bf16[64,4608]{1,0:T(8,128)(2,1)S(1)} %copy-done.2), channel_id=1, source_target_pairs={{0,1},{1,0},{2,17},{3,16},{16,3},{17,2},{18,19},{19,18},{4,5},{5,4... | collective-permute-start | bytes 1769480 | tf_op jit(solution)/shard_map/ppermute | solution.py:207
  88.5 5.4 %collective-permute-start.5 = (bf16[4,288,512]{2,1,0:T(8,128)(2,1)S(1)}, bf16[4,288,512]{2,1,0:T(8,128)(2,1)S(1)}, u32[]{:S(2)}, u32[]{:S(2)}) collective-permute-start(bf16[4,288,512]{2,1,0:T(8,128)(2,1)S(1)} %all-to-all-done.2.mine_ref), channel_id=1, source_target_pairs={{0,16},{16,0},{1,17},{17,1},{2,18},{18,2},{3,19},{19,3},{4,20},{20... | collective-permute-start | bytes 3538952 | tf_op jit(solution)/shard_map/ppermute | solution.py:233
  97.1 8.6 %collective-permute-start.6 = (bf16[64,1024]{1,0:T(8,128)(2,1)S(1)}, bf16[64,1024]{1,0:T(8,128)(2,1)S(1)}, u32[]{:S(2)}, u32[]{:S(2)}) collective-permute-start(bf16[64,1024]{1,0:T(8,128)(2,1)S(1)} %shard_map.69), channel_id=1, source_target_pairs={{0,0},{1,1},{16,2},{17,3},{2,16},{3,17},{18,18},{19,19},{4,4},{5,5... | collective-permute-start | bytes 393224 | tf_op jit(solution)/shard_map/ppermute | solution.py:257
  102.3 7.5 %collective-permute-start.7 = (bf16[64,1024]{1,0:T(8,128)(2,1)S(1)}, bf16[64,1024]{1,0:T(8,128)(2,1)S(1)}, u32[]{:S(2)}, u32[]{:S(2)}) collective-permute-start(bf16[64,1024]{1,0:T(8,128)(2,1)S(1)} %shard_map.70), channel_id=1, source_target_pairs={{1,0},{0,1},{17,2},{16,3},{3,16},{2,17},{19,18},{18,19},{5,4},{4,5... | collective-permute-start | bytes 393224 | tf_op jit(solution)/shard_map/ppermute | solution.py:257

commit v5 on v4

--- a/solution.py
+++ b/solution.py
@@ -15,6 +15,7 @@
 SHARE = 8
 QB = 64
 HEADS = 8
+NOTE = 24
 PACK = 24
 ROWS = 288
 
@@ -38,22 +39,85 @@
     return jnp.dot(selector, rows, preferred_element_type=f32)
 
 
-def send_kernel(hot_ref, first_ref, lat_ref, rope_ref, out_ref):
-    got = first_ref[...].reshape(16 * 8, LAT)
+def read_kernel(selection_ref, kv_ref, rope_ref, own_ref, theirs_ref, lat, rope, sems):
+    y, k = lax.axis_index("y"), lax.axis_index("core")
+    tokens = pl.ds(pl.multiple_of(y * 16, 16), 16)
+    columns = pl.ds(pl.multiple_of(y * 1024, 1024), 1024)
+    copies = [
+        pltpu.make_async_copy(kv_ref.at[:, tokens, :], lat, sems.at[0]),
+        pltpu.make_async_copy(rope_ref.at[:, columns], rope, sems.at[1]),
+    ]
+    for copy in copies:
+        copy.start()
+    row = iota((8, 32), 0)
+    one, two = selection_ref[0:1, :], selection_ref[1:2, :]
+    notes = jnp.where(row % 2 == 0, one, two)
+    notes = jnp.where(row < 2, notes >> 4, jnp.where(row < 4, notes & 15, 0))
+    notes = jnp.concatenate([notes.astype(f32), jnp.zeros((8, LAT - 32), f32)], axis=1)
+    for ref in (own_ref, theirs_ref):
+        ref[144:152, :] = notes.astype(bf16)
+    for copy in copies:
+        copy.wait()
+    low, high = lat[:, 0:8, :].reshape(128, LAT), lat[:, 8:16, :].reshape(128, LAT)
+    own_ref[0:128, :] = jnp.where(k == 0, low, high)
+    theirs_ref[0:128, :] = jnp.where(k == 0, high, low)
+    low, high = rope[:, 0:LAT], rope[:, LAT:]
+    own_ref[128:144, :] = jnp.where(k == 0, low, high)
+    theirs_ref[128:144, :] = jnp.where(k == 0, high, low)
+
+
+def join_kernel(selection_ref, own_ref, other_ref, lat_ref, rope_ref, first_ref, owners_ref):
+    k, x = lax.axis_index("core"), lax.axis_index("x")
+    hot = selection_ref[0:1, 0:1] & 31
+    own, other = own_ref[...], other_ref[...]
+    one, two = jnp.where(k == 0, own, other), jnp.where(k == 0, other, own)
+    lat_ref[0:128, :], lat_ref[128:256, :] = one[0:128], two[0:128]
+    rope_ref[0:16, :], rope_ref[16:32, :] = one[128:144], two[128:144]
+    notes = jnp.where(x // 2 == k, own[144:152, 0:128], other[144:152, 0:128]).astype(f32)
+    owner = jnp.where(x % 2 == 0, notes[0:1], notes[1:2])
+    place = jnp.where(x % 2 == 0, notes[2:3], notes[3:4])
+    owners_ref[...] = jnp.broadcast_to(owner, (8, 128)).astype(i32)
+    count = 16 * NOTE
+    lane, row = iota((count, 128), 1), iota((count, 1), 0)
+    z, part = row // NOTE, row % NOTE
+    cold = (lane >= HOT) & (lane < HOT + COLD)
+    rows = jnp.zeros((count, 128), f32)
+    for c in range(2):
+        match = cold & (owner.astype(i32) == z * 2 + c) & (part == 18)
+        want = jnp.sum(jnp.where(match, place, 0.0), axis=1, keepdims=True) + c * 16
+        rows = jnp.where((part == 18) & (lane == c), want, rows)
+    for c in range(4):
+        chosen = (part < 16) & (part % 4 == c)
+        index = jnp.where(chosen, hot * 8 + z * 4 + part // 4, -1)
+        rows = rows + pick(one_hot(index, 256), lat_ref[:, c * 128 : c * 128 + 128])
+        index = jnp.where(z % 2 * 2 + part - 16 == c, hot + z // 2, -1)
+        index = jnp.where((part == 16) | (part == 17), index, -1)
+        rows = rows + pick(one_hot(index, 32), rope_ref[:, c * 128 : c * 128 + 128])
+    first_ref[...] = rows.astype(bf16)
+
+
+def send_kernel(selection_ref, first_ref, lat_ref, rope_ref, out_ref):
+    got = first_ref[...]
     row = iota((256, 1), 0)
-    notes = pick(one_hot(row // 16 * 8 + 5, 128), got[:, 0:128])
+    notes = pick(one_hot(row // 16 * NOTE + 18, 16 * NOTE), got)
     lane = iota((256, 128), 1)
     want = jnp.sum(jnp.where(lane == row // 8 % 2, notes, 0.0), axis=1, keepdims=True)
-    lat = pick(one_hot(want.astype(i32) * 8 + row % 8, 256), lat_ref[...].reshape(256, LAT))
+    lat = pick(one_hot(want.astype(i32) * 8 + row % 8, 256), lat_ref[...])
     row = iota((128, 1), 0)
-    notes = pick(one_hot(row // 8 * 8 + 5, 128), got[:, 0:128])
+    notes = pick(one_hot(row // 8 * NOTE + 18, 16 * NOTE), got)
     lane = iota((128, 128), 1)
     want = jnp.sum(jnp.where(lane == row % 8, notes, 0.0), axis=1, keepdims=True).astype(i32)
     want = jnp.where(row % 8 < 2, want, -1)
     rope = pick(one_hot(want, 32), rope_ref[...])
     row = iota((8, 1), 0)
-    source = jnp.where(row == 2, 4, jnp.where(row >= 4, row - 4, -1))
-    hot = pick(one_hot(hot_ref[0] * 8 + source, 128) * (source >= 0).astype(bf16), got)
+    holder = (selection_ref[0:1, 0:1] >> 5) * NOTE
+    half = lax.axis_index("z") % 2
+    hot = []
+    for c in range(4):
+        index = jnp.where(row >= 4, holder + (row - 4) * 4 + c, -1)
+        index = jnp.where((row == 2) & (half == c // 2), holder + 16 + c % 2, index)
+        hot.append(pick(one_hot(index, 16 * NOTE), got))
+    hot = jnp.concatenate(hot, axis=1)
     for z in range(16):
         out_ref[z, 0:16, :] = lat[z * 16 : z * 16 + 16].astype(bf16)
         out_ref[z, 16:24, :] = (rope[z * 8 : z * 8 + 8] + hot).astype(bf16)
@@ -72,6 +136,7 @@
         rope_index = jnp.where(rope_slot == i, at + 16 + side, rope_index)
     lat = one_hot(index, 16 * PACK)
     rope = one_hot(rope_index, 16 * PACK)
+    rope = rope + one_hot(jnp.where(rope_slot >= COLD, rope_index + PACK, -1), 16 * PACK)
     table = got_ref[...].reshape(16 * PACK, LAT)
     lat = pick(lat, table).astype(bf16)
     rope = pick(rope, table).astype(bf16)
@@ -125,16 +190,19 @@
         stat_ref[:, 128:256] = jnp.broadcast_to(total, (HEADS * QB, 128))
 
 
-def second_half_kernel(q_ref, other_ref, blend_ref, stat_ref, w_ref, o_ref, places):
+def second_half_kernel(q_ref, other_ref, blend_ref, stat_ref, w_ref, o_ref, places, w, sem):
+    up = pltpu.make_async_copy(w_ref, w, sem)
+    up.start()
     top, total, blended = attend(q_ref, other_ref, places)
     top0, total0 = stat_ref[:, 0:1], stat_ref[:, 128:129]
     both = jnp.maximum(top, top0)
     mine, other = jnp.exp2(top0 - both), jnp.exp2(top - both)
     scale = 1.0 / (total0 * mine + total * other)
     latent = (blend_ref[...] * (mine * scale) + blended * (other * scale)).astype(bf16)
+    up.wait()
     for h in range(HEADS):
         o_ref[:, h * VH : (h + 1) * VH] = jnp.dot(
-            latent[h * QB : (h + 1) * QB], w_ref[h], preferred_element_type=f32
+            latent[h * QB : (h + 1) * QB], w[h], preferred_element_type=f32
         ).astype(bf16)
 
 
@@ -143,42 +211,41 @@
     vmem = pl.BlockSpec(memory_space=pltpu.VMEM)
     smem = pl.BlockSpec(memory_space=pltpu.SMEM)
     params = pltpu.CompilerParams(vmem_limit_bytes=12 * 1024 * 1024)
+    anywhere = pl.BlockSpec(memory_space=pl.ANY)
     swap = [(0, 1), (1, 0)]
 
-    lat = lax.dynamic_slice_in_dim(kv_latent, y * 16, 16, 1)
-    rope = lax.dynamic_slice_in_dim(k_rope, y * 1024, 1024, 1)
-    hot_first = jnp.max(selection[:, 0])
-    cold = selection[:, HOT:]
-    notes = jnp.concatenate([cold >> 4, cold & 15], axis=1).astype(bf16)
-    notes = jnp.pad(notes, ((0, 6), (0, LAT - 2 * COLD)))
-    theirs = jnp.concatenate(
-        [
-            lax.dynamic_slice_in_dim(lat, (1 - k) * SHARE, SHARE, 1).reshape(128, LAT),
-            lax.dynamic_slice_in_dim(rope, (1 - k) * LAT, LAT, 1),
-            notes,
+    pack = jax.ShapeDtypeStruct((152, LAT), bf16)
+    own, theirs = pl.pallas_call(
+        read_kernel,
+        out_shape=[pack, pack],
+        in_specs=[vmem, anywhere, anywhere],
+        out_specs=[vmem, vmem],
+        scratch_shapes=[
+            pltpu.VMEM((16, 16, LAT), bf16),
+            pltpu.VMEM((16, 2 * LAT), bf16),
+            pltpu.SemaphoreType.DMA((2,)),
         ],
-        axis=0,
-    )
+        compiler_params=params,
+    )(selection, kv_latent, k_rope)
     swapped = lax.ppermute(theirs, "core", swap)
-    own = lax.dynamic_slice_in_dim(lat, k * SHARE, SHARE, 1)
-    other = swapped[:128].reshape(16, SHARE, LAT)
-    lat = jnp.where(k == 0, jnp.concatenate([own, other]), jnp.concatenate([other, own]))
-    own, other = lax.dynamic_slice_in_dim(rope, k * LAT, LAT, 1), swapped[128:144]
-    rope = jnp.where(k == 0, jnp.concatenate([own, other]), jnp.concatenate([other, own]))
-    notes = jnp.where(x // 2 == k, notes, swapped[144:])
-    notes = jnp.where(x % 2 == 0, notes[0, : 2 * COLD], notes[1, : 2 * COLD]).astype(i32)
-    owners, places = notes[:COLD], notes[COLD:]
-
-    match = owners[None, :] == jnp.arange(32)[:, None]
-    wants = jnp.sum(jnp.where(match, places[None, :], 0), axis=1).reshape(16, 2)
-    wants = wants + jnp.arange(2)[None, :] * 16
-    hot = lax.dynamic_slice_in_dim(lat, hot_first & 31, HOT, 0).reshape(16, 4, LAT)
-    hot_rope = lax.dynamic_slice_in_dim(rope, hot_first & 31, HOT, 0)
-    hot_rope = jnp.broadcast_to(hot_rope[:, None, None, :], (HOT, 2, 1, LAT)).reshape(16, 1, LAT)
-    wants = jnp.pad(wants.astype(bf16)[:, None, :], ((0, 0), (0, 2), (0, LAT - 2)))
-    first = jnp.concatenate([hot, hot_rope, wants], axis=1)
+
+    lat, rope, first, owners = pl.pallas_call(
+        join_kernel,
+        out_shape=[
+            jax.ShapeDtypeStruct((256, LAT), bf16),
+            jax.ShapeDtypeStruct((32, LAT), bf16),
+            jax.ShapeDtypeStruct((16 * NOTE, 128), bf16),
+            jax.ShapeDtypeStruct((8, 128), i32),
+        ],
+        in_specs=[vmem] * 3,
+        out_specs=[vmem] * 4,
+        compiler_params=params,
+    )(selection, own, swapped)
+    owners = owners[0, HOT : HOT + COLD]
     first, w_uv, q_latent, q_rope = lax.optimization_barrier((first, w_uv, q_latent, q_rope))
+    first = first.reshape(16, NOTE, 128)
     first = lax.all_to_all(first, "z", split_axis=0, concat_axis=0, tiled=True)
+    first = first.reshape(16 * NOTE, 128)
 
     def pairs(r):
         return [
@@ -211,11 +278,11 @@
     second = pl.pallas_call(
         send_kernel,
         out_shape=jax.ShapeDtypeStruct((16, PACK, LAT), bf16),
-        in_specs=[smem, vmem, vmem, vmem],
+        in_specs=[vmem] * 4,
         out_specs=vmem,
         compiler_params=params,
         cost_estimate=pl.CostEstimate(flops=5000000000, bytes_accessed=0, transcendentals=0),
-    )((hot_first >> 5)[None], first, lat, rope)
+    )(selection, first, lat, rope)
     second, queries[0] = lax.optimization_barrier((second, travel(0)))
     second = lax.all_to_all(second, "z", split_axis=0, concat_axis=0, tiled=True)
 
@@ -249,9 +316,10 @@
         out = pl.pallas_call(
             second_half_kernel,
             out_shape=jax.ShapeDtypeStruct((QB, HEADS * VH), bf16),
-            in_specs=[vmem] * 5,
+            in_specs=[vmem] * 4 + [anywhere],
             out_specs=vmem,
-            scratch_shapes=scratch,
+            scratch_shapes=scratch
+            + [pltpu.VMEM((HEADS, LAT, VH), bf16), pltpu.SemaphoreType.DMA],
             compiler_params=params,
         )(queries[r], other, halves[2 * r], halves[2 * r + 1], ups[r])
         outs.append(lax.ppermute(out, ("core", "x"), [(d, s) for s, d in pairs(r)]))

time: 113 us -> 111 us (0.982); the launches traced: 111 us -> 110 us
  other arithmetic: 4.83 us -> 1.64 us
  starting transfers between devices: 58.2 us -> 60.9 us
  between operations: 1.59 us -> 0.25 us
  Pallas kernels: 11.4 us -> 12.6 us
    unnamed x10 -> x18, local copies, waits for them, and re-layouts: 1.05 us -> 3.87 us
    ppermute x2, starting transfers between devices: 8.58 us -> 10.6 us  [travel(): lax.ppermute(queries[r], ('core', 'x'), pairs(r))]
    dynamic_slice x4 -> x0, local copies, waits for them, and re-layouts: 2.03 us -> none  [the longest x1 1.12 us: local(): own = lax.dynamic_slice_in_dim(lat, k * SHARE, SHARE, 1)]
    pallas_call x0 -> x2, Pallas kernels: none -> 1.96 us  [the longest x1 1.88 us: local(): pl.pallas_call(join_kernel, out_shape=[jax.ShapeDtypeStruct((256, LAT), b...]
    all_to_all x1, waiting for transfers between devices: 11.6 us -> 9.8 us  [local(): lax.all_to_all(second, 'z', split_axis=0, concat_axis=0, tiled=True)]
    reduce_max x1 -> x0, other arithmetic: 1.34 us -> none  [local(): hot_first = jnp.max(selection[:, 0])]
  transfers between devices with their start and end apart: 11 -> 11, of which waited for: 4 -> 6; matrix products, arithmetic and copies ran while one was open for 3% -> 2% of each run, Pallas kernels for 7% -> 8%
where the time goes in v5:
time: 111 us; the launch traced here: 110 us
  starting transfers between devices  60.9 us (55%)
  waiting for transfers between devices  29.6 us (27%)
  Pallas kernels  12.6 us (11%)
  local copies, waits for them, and re-layouts  4.66 us (4%)
  other arithmetic  1.64 us (1%)
    all_to_all x1, starting transfers between devices, local(): lax.all_to_all(second, 'z', split_axis=0, concat_axis=0, tiled=True)  11.5 us
    ppermute x2, starting transfers between devices, travel(): lax.ppermute(queries[r], ('core', 'x'), pairs(r))  10.6 us
    all_to_all x1, waiting for transfers between devices, local(): lax.all_to_all(second, 'z', split_axis=0, concat_axis=0, tiled=True)  9.8 us
    all_to_all x1, starting transfers between devices, local(): first = lax.all_to_all(first, 'z', split_axis=0, concat_axis=0, tiled=True)  9.54 us
    ppermute x1, starting transfers between devices, local(): swapped = lax.ppermute(theirs, 'core', swap)  8.92 us
    ppermute x2, waiting for transfers between devices, travel(): lax.ppermute(queries[r], ('core', 'x'), pairs(r))  7.97 us
    ppermute x2, starting transfers between devices, local(): ups = [lax.ppermute(w_uv, ('core', 'x'), pairs(r)) for r in range(2)]  7.35 us
    ppermute x2, starting transfers between devices, local(): outs.append(lax.ppermute(out, ('core', 'x'), [(d, s) for s, d in pairs(r)]))  6.77 us
  transfers between devices with their start and end apart: 11, of which 6 were waited for; matrix products, arithmetic and copies ran while one was open for 2% of the time, Pallas kernels for 8%

profile of v5, /device:TPU:1, one launch (start us, length us, event | category | flops | bytes accessed | tf_op | source)
XLA Modules:
  0.0 109.7 jit_solution(3256481045639191417)
XLA Ops:
  0.0 0.0 copy-start.1
  0.0 1.2 %copy-done.1 = bf16[16,64,512]{2,1,0:T(8,128)(2,1)S(1)} copy-done((bf16[16,64,512]{2,1,0:T(8,128)(2,1)S(1)}, bf16[16,64,512]{2,1,0:T(8,128)(2,1)}, u32[]{:S(2)}) %copy-start.1) | copy-done | bytes 1048600
  1.2 0.0 copy-start.2
  1.2 0.9 copy-done.2
  2.1 0.7 copy-done.3
  2.8 0.1 shard_map.64
  2.9 8.9 %collective-permute-start = (bf16[152,512]{1,0:T(8,128)(2,1)S(1)}, bf16[152,512]{1,0:T(8,128)(2,1)S(1)}, u32[]{:S(2)}, u32[]{:S(2)}) collective-permute-start(bf16[152,512]{1,0:T(8,128)(2,1)S(1)} %get-tuple-element.29), channel_id=1, source_target_pairs={{0,16},{16,0},{1,17},{17,1},{2,18},{18,2},{3,19},{19,3},{4,20},{20... | collective-permute-start | bytes 466952 | tf_op jit(solution)/shard_map/ppermute | solution.py:230
  11.9 1.0 collective-permute-done.other_ref
  12.8 0.0 copy-done.4
  12.8 1.9 %shard_map.65 = (bf16[256,512]{1,0:T(8,128)(2,1)S(1)}, bf16[32,512]{1,0:T(8,128)(2,1)S(1)}, bf16[384,128]{1,0:T(8,128)(2,1)}, s32[8,128]{1,0:T(8,128)S(1)}) custom-call(s32[2,32]{1,0:T(2,128)S(1)} %copy-done.4, bf16[152,512]{1,0:T(8,128)(2,1)S(1)} %get-tuple-element.28.own_ref, bf16[152,512]{1,0:T(8,128)(2,1)S(1)} %collective-permute-done.other_ref), custom_call_target="tpu_custom_call" | custom-call | tf_op jit(solution)/shard_map/pallas_call | solution.py:232
  14.7 9.5 %all-to-all-start = ((bf16[16,24,128]{2,1,0:T(8,128)(2,1)}), bf16[16,24,128]{2,1,0:T(8,128)(2,1)S(1)}, u32[]{:S(2)}, u32[]{:S(2)}) async-start(bf16[16,24,128]{2,1,0:T(8,128)(2,1)} %bitcast.1), calls=%async_computation | async-start | bytes 196608 | tf_op jit(solution)/shard_map/all_to_all | solution.py:247
  24.3 0.0 copy-done.8
  24.3 0.6 constant_dynamic-slice_fusion
  24.9 0.0 copy-done.5
  24.9 0.1 constant_dynamic-slice_fusion.1
  25.1 5.2 %collective-permute-start.1 = (bf16[64,4608]{1,0:T(8,128)(2,1)S(1)}, bf16[64,4608]{1,0:T(8,128)(2,1)S(1)}, u32[]{:S(2)}, u32[]{:S(2)}) collective-permute-start(bf16[64,4608]{1,0:T(8,128)(2,1)S(1)} %pad_maximum_fusion), channel_id=1, source_target_pairs={{0,0},{1,1},{2,16},{3,17},{16,2},{17,3},{18,18},{19,19},{4,4},{5,5... | collective-permute-start | bytes 1769480 | tf_op jit(solution)/shard_map/ppermute | solution.py:274
  30.3 5.9 %all-to-all-done = bf16[16,24,128]{2,1,0:T(8,128)(2,1)S(1)} async-done(((bf16[16,24,128]{2,1,0:T(8,128)(2,1)}), bf16[16,24,128]{2,1,0:T(8,128)(2,1)S(1)}, u32[]{:S(2)}, u32[]{:S(2)}) %all-to-all-start) | async-done | bytes 98336 | tf_op jit(solution)/shard_map/all_to_all | solution.py:247
  36.2 1.5 %shard_map.66 = bf16[16,24,512]{2,1,0:T(8,128)(2,1)} custom-call(s32[2,32]{1,0:T(2,128)S(1)} %copy-done.4, bf16[384,128]{1,0:T(8,128)(2,1)S(1)} %bitcast.4, bf16[256,512]{1,0:T(8,128)(2,1)S(1)} %get-tuple-element.33.lat_ref, bf16[32,512]{1,0:T(8,128)(2,1)S(1)} %get-tuple-element.34.rope_ref), custom_call_target="tpu_custom_call" | custom-call | flops 5000000000 | tf_op jit(solution)/shard_map/pallas_call | solution.py:278
  37.7 0.4 collective-permute-done.1.q_ref
  38.1 0.1 shard_map.67.q0_ref.q_ref
  38.2 11.5 %all-to-all-start.1 = ((bf16[16,24,512]{2,1,0:T(8,128)(2,1)}), bf16[16,24,512]{2,1,0:T(8,128)(2,1)S(1)}, u32[]{:S(2)}, u32[]{:S(2)}) async-start(bf16[16,24,512]{2,1,0:T(8,128)(2,1)} %shard_map.66), calls=%async_computation.1 | async-start | bytes 786432 | tf_op jit(solution)/shard_map/all_to_all | solution.py:287
  49.7 5.2 %collective-permute-start.4 = (bf16[8,512,128]{2,1,0:T(8,128)(2,1)}, bf16[8,512,128]{2,1,0:T(8,128)(2,1)S(1)}, u32[]{:S(2)}, u32[]{:S(2)}) collective-permute-start(bf16[8,512,128]{2,1,0:T(8,128)(2,1)} %param.11), channel_id=1, source_target_pairs={{0,1},{1,0},{2,17},{3,16},{16,3},{17,2},{18,19},{19,18},{4,5},{5,4... | collective-permute-start | bytes 3145736 | tf_op jit(solution)/shard_map/ppermute | solution.py:276
  54.8 2.2 %collective-permute-start.3 = (bf16[8,512,128]{2,1,0:T(8,128)(2,1)}, bf16[8,512,128]{2,1,0:T(8,128)(2,1)}, u32[]{:S(2)}, u32[]{:S(2)}) collective-permute-start(bf16[8,512,128]{2,1,0:T(8,128)(2,1)} %param.11), channel_id=1, source_target_pairs={{0,0},{1,1},{2,16},{3,17},{16,2},{17,3},{18,18},{19,19},{4,4},{5,5... | collective-permute-start | bytes 3145736 | tf_op jit(solution)/shard_map/ppermute | solution.py:276
  57.0 0.0 copy-done.7
  57.0 0.9 pad_maximum_fusion.1
  57.9 0.1 slice_bitcast_fusion.owners_ref
  58.0 9.8 %all-to-all-done.1.got_ref = bf16[16,24,512]{2,1,0:T(8,128)(2,1)S(1)} async-done(((bf16[16,24,512]{2,1,0:T(8,128)(2,1)}), bf16[16,24,512]{2,1,0:T(8,128)(2,1)S(1)}, u32[]{:S(2)}, u32[]{:S(2)}) %all-to-all-start.1) | async-done | bytes 393248 | tf_op jit(solution)/shard_map/all_to_all | solution.py:287
  67.8 1.0 shard_map.68
  68.8 0.0 copy-start
  68.8 1.0 copy-done
  69.8 4.3 %all-to-all-start.2 = ((bf16[4,288,512]{2,1,0:T(8,128)(2,1)}), bf16[4,288,512]{2,1,0:T(8,128)(2,1)S(1)}, u32[]{:S(2)}, u32[]{:S(2)}) async-start(bf16[4,288,512]{2,1,0:T(8,128)(2,1)} %copy-done), calls=%async_computation.2 | async-start | bytes 2359296 | tf_op jit(solution)/shard_map/all_to_all | solution.py:298
  74.2 0.0 copy-done.6
  74.2 5.5 %collective-permute-start.2 = (bf16[64,4608]{1,0:T(8,128)(2,1)S(1)}, bf16[64,4608]{1,0:T(8,128)(2,1)S(1)}, u32[]{:S(2)}, u32[]{:S(2)}) collective-permute-start(bf16[64,4608]{1,0:T(8,128)(2,1)S(1)} %copy-done.6), channel_id=1, source_target_pairs={{0,1},{1,0},{2,17},{3,16},{16,3},{17,2},{18,19},{19,18},{4,5},{5,4... | collective-permute-start | bytes 1769480 | tf_op jit(solution)/shard_map/ppermute | solution.py:274
  79.6 7.6 %collective-permute-done.2.q_ref = bf16[64,4608]{1,0:T(8,128)(2,1)S(1)} collective-permute-done((bf16[64,4608]{1,0:T(8,128)(2,1)S(1)}, bf16[64,4608]{1,0:T(8,128)(2,1)S(1)}, u32[]{:S(2)}, u32[]{:S(2)}) %collective-permute-start.2) | collective-permute-done | bytes 589856 | tf_op jit(solution)/shard_map/ppermute | solution.py:274
  87.2 0.1 shard_map.69.q1_ref.q_ref
  87.3 0.0 collective-permute-done.4.w_ref
  87.3 0.0 collective-permute-done.3.w_ref
  87.3 0.0 all-to-all-done.2.mine_ref
  87.3 1.9 %collective-permute-start.5 = (bf16[4,288,512]{2,1,0:T(8,128)(2,1)S(1)}, bf16[4,288,512]{2,1,0:T(8,128)(2,1)S(1)}, u32[]{:S(2)}, u32[]{:S(2)}) collective-permute-start(bf16[4,288,512]{2,1,0:T(8,128)(2,1)S(1)} %all-to-all-done.2.mine_ref), channel_id=1, source_target_pairs={{0,16},{16,0},{1,17},{17,1},{2,18},{18,2},{3,19},{19,3},{4,20},{20... | collective-permute-start | bytes 3538952 | tf_op jit(solution)/shard_map/ppermute | solution.py:300
  89.3 3.4 %shard_map.70 = (f32[512,512]{1,0:T(8,128)S(1)}, f32[512,256]{1,0:T(8,128)S(1)}, f32[512,512]{1,0:T(8,128)S(1)}, f32[512,256]{1,0:T(8,128)S(1)}) custom-call(bf16[512,640]{1,0:T(8,128)(2,1)S(1)} %shard_map.67.q0_ref.q_ref, bf16[512,640]{1,0:T(8,128)(2,1)S(1)} %shard_map.69.q1_ref.q_ref, bf16[4,288,512]{2,1,0:T(8,128)(2,1)S(1)} %all-to-all-done.2.mine_ref), custom_call_target="tpu_custom_call" | custom-call | tf_op jit(solution)/shard_map/pallas_call | solution.py:306
  92.7 0.0 collective-permute-done.5.other_ref
  92.7 2.2 %shard_map.71 = bf16[64,1024]{1,0:T(8,128)(2,1)S(1)} custom-call(bf16[512,640]{1,0:T(8,128)(2,1)S(1)} %shard_map.67.q0_ref.q_ref, bf16[4,288,512]{2,1,0:T(8,128)(2,1)S(1)} %collective-permute-done.5.other_ref, f32[512,512]{1,0:T(8,128)S(1)} %get-tuple-element.45.blend_ref, f32[512,256]{1,0:T(8,128)S(1)} %get-tuple-element.46.stat_ref, ...), custom_call_target="tpu_custom_call" | custom-call | tf_op jit(solution)/shard_map/pallas_call | solution.py:316
  94.9 4.2 %collective-permute-start.6 = (bf16[64,1024]{1,0:T(8,128)(2,1)S(1)}, bf16[64,1024]{1,0:T(8,128)(2,1)S(1)}, u32[]{:S(2)}, u32[]{:S(2)}) collective-permute-start(bf16[64,1024]{1,0:T(8,128)(2,1)S(1)} %shard_map.71), channel_id=1, source_target_pairs={{0,0},{1,1},{16,2},{17,3},{2,16},{3,17},{18,18},{19,19},{4,4},{5,5... | collective-permute-start | bytes 393224 | tf_op jit(solution)/shard_map/ppermute | solution.py:325
  99.1 2.3 %shard_map.72 = bf16[64,1024]{1,0:T(8,128)(2,1)S(1)} custom-call(bf16[512,640]{1,0:T(8,128)(2,1)S(1)} %shard_map.69.q1_ref.q_ref, bf16[4,288,512]{2,1,0:T(8,128)(2,1)S(1)} %collective-permute-done.5.other_ref, f32[512,512]{1,0:T(8,128)S(1)} %get-tuple-element.48.blend_ref, f32[512,256]{1,0:T(8,128)S(1)} %get-tuple-element.49.stat_ref, ...), custom_call_target="tpu_custom_call" | custom-call | tf_op jit(solution)/shard_map/pallas_call | solution.py:316
  101.4 2.6 %collective-permute-start.7 = (bf16[64,1024]{1,0:T(8,128)(2,1)S(1)}, bf16[64,1024]{1,0:T(8,128)(2,1)S(1)}, u32[]{:S(2)}, u32[]{:S(2)}) collective-permute-start(bf16[64,1024]{1,0:T(8,128)(2,1)S(1)} %shard_map.72), channel_id=1, source_target_pairs={{1,0},{0,1},{17,2},{16,3},{3,16},{2,17},{19,18},{18,19},{5,4},{4,5... | collective-permute-start | bytes 393224 | tf_op jit(solution)/shard_map/ppermute | solution.py:325
  104.0 0.0 collective-permute-done.6
  104.0 4.9 %collective-permute-done.7 = bf16[64,1024]{1,0:T(8,128)(2,1)S(1)} collective-permute-done((bf16[64,1024]{1,0:T(8,128)(2,1)S(1)}, bf16[64,1024]{1,0:T(8,128)(2,1)S(1)}, u32[]{:S(2)}, u32[]{:S(2)}) %collective-permute-start.7) | collective-permute-done | bytes 131104 | tf_op jit(solution)/shard_map/ppermute | solution.py:325
  109.0 0.7 pad_maximum_fusion.2
  (8 shorter events, 0.1 us)
Async XLA Ops:
  0.0 1.2 %copy-start.1 = (bf16[16,64,512]{2,1,0:T(8,128)(2,1)S(1)}, bf16[16,64,512]{2,1,0:T(8,128)(2,1)}, u32[]{:S(2)}) copy-start(bf16[16,64,512]{2,1,0:T(8,128)(2,1)} %kv_ref.1) | copy-start | bytes 3145732
  1.2 0.9 copy-start.2
  2.1 0.7 copy-start.3
  2.8 10.0 %copy-start.4 = (s32[2,32]{1,0:T(2,128)S(1)}, s32[2,32]{1,0:T(2,128)}, u32[]{:S(2)}) copy-start(s32[2,32]{1,0:T(2,128)} %selection_ref.5) | copy-start | bytes 772
  2.8 21.5 %copy-start.8 = (bf16[128,512]{1,0:T(8,128)(2,1)S(1)}, bf16[128,512]{1,0:T(8,128)(2,1)}, u32[]{:S(2)}) copy-start(bf16[128,512]{1,0:T(8,128)(2,1)} %param.7) | copy-start | bytes 393220
  2.8 22.1 %copy-start.5 = (bf16[128,4096]{1,0:T(8,128)(2,1)S(1)}, bf16[128,4096]{1,0:T(8,128)(2,1)}, u32[]{:S(2)}) copy-start(bf16[128,4096]{1,0:T(8,128)(2,1)} %param.6) | copy-start | bytes 3145732
  2.9 9.9 %collective-permute-start = (bf16[152,512]{1,0:T(8,128)(2,1)S(1)}, bf16[152,512]{1,0:T(8,128)(2,1)S(1)}, u32[]{:S(2)}, u32[]{:S(2)}) collective-permute-start(bf16[152,512]{1,0:T(8,128)(2,1)S(1)} %get-tuple-element.29), channel_id=1, source_target_pairs={{0,16},{16,0},{1,17},{17,1},{2,18},{18,2},{3,19},{19,3},{4,20},{20... | collective-permute-start | bytes 466952 | tf_op jit(solution)/shard_map/ppermute | solution.py:230
  14.7 21.5 %all-to-all-start = ((bf16[16,24,128]{2,1,0:T(8,128)(2,1)}), bf16[16,24,128]{2,1,0:T(8,128)(2,1)S(1)}, u32[]{:S(2)}, u32[]{:S(2)}) async-start(bf16[16,24,128]{2,1,0:T(8,128)(2,1)} %bitcast.1), calls=%async_computation | async-start | bytes 196608 | tf_op jit(solution)/shard_map/all_to_all | solution.py:247
  25.1 13.0 %collective-permute-start.1 = (bf16[64,4608]{1,0:T(8,128)(2,1)S(1)}, bf16[64,4608]{1,0:T(8,128)(2,1)S(1)}, u32[]{:S(2)}, u32[]{:S(2)}) collective-permute-start(bf16[64,4608]{1,0:T(8,128)(2,1)S(1)} %pad_maximum_fusion), channel_id=1, source_target_pairs={{0,0},{1,1},{2,16},{3,17},{16,2},{17,3},{18,18},{19,19},{4,4},{5,5... | collective-permute-start | bytes 1769480 | tf_op jit(solution)/shard_map/ppermute | solution.py:274
  37.7 19.4 %copy-start.7 = (bf16[64,512]{1,0:T(8,128)(2,1)S(1)}, bf16[64,512]{1,0:T(8,128)(2,1)}, u32[]{:S(2)}) copy-start(bf16[64,512]{1,0:T(8,128)(2,1)} %get-tuple-element.55) | copy-start | bytes 196612
  38.2 29.6 %all-to-all-start.1 = ((bf16[16,24,512]{2,1,0:T(8,128)(2,1)}), bf16[16,24,512]{2,1,0:T(8,128)(2,1)S(1)}, u32[]{:S(2)}, u32[]{:S(2)}) async-start(bf16[16,24,512]{2,1,0:T(8,128)(2,1)} %shard_map.66), calls=%async_computation.1 | async-start | bytes 786432 | tf_op jit(solution)/shard_map/all_to_all | solution.py:287
  49.7 37.6 %collective-permute-start.4 = (bf16[8,512,128]{2,1,0:T(8,128)(2,1)}, bf16[8,512,128]{2,1,0:T(8,128)(2,1)S(1)}, u32[]{:S(2)}, u32[]{:S(2)}) collective-permute-start(bf16[8,512,128]{2,1,0:T(8,128)(2,1)} %param.11), channel_id=1, source_target_pairs={{0,1},{1,0},{2,17},{3,16},{16,3},{17,2},{18,19},{19,18},{4,5},{5,4... | collective-permute-start | bytes 3145736 | tf_op jit(solution)/shard_map/ppermute | solution.py:276
  54.8 32.5 %collective-permute-start.3 = (bf16[8,512,128]{2,1,0:T(8,128)(2,1)}, bf16[8,512,128]{2,1,0:T(8,128)(2,1)}, u32[]{:S(2)}, u32[]{:S(2)}) collective-permute-start(bf16[8,512,128]{2,1,0:T(8,128)(2,1)} %param.11), channel_id=1, source_target_pairs={{0,0},{1,1},{2,16},{3,17},{16,2},{17,3},{18,18},{19,19},{4,4},{5,5... | collective-permute-start | bytes 3145736 | tf_op jit(solution)/shard_map/ppermute | solution.py:276
  68.8 1.0 copy-start
  69.8 4.3 %copy-start.6 = (bf16[64,4608]{1,0:T(8,128)(2,1)S(1)}, bf16[64,4608]{1,0:T(8,128)(2,1)}, u32[]{:S(2)}) copy-start(bf16[64,4608]{1,0:T(8,128)(2,1)} %pad_maximum_fusion.1) | copy-start | bytes 1769476
  69.8 17.5 %all-to-all-start.2 = ((bf16[4,288,512]{2,1,0:T(8,128)(2,1)}), bf16[4,288,512]{2,1,0:T(8,128)(2,1)S(1)}, u32[]{:S(2)}, u32[]{:S(2)}) async-start(bf16[4,288,512]{2,1,0:T(8,128)(2,1)} %copy-done), calls=%async_computation.2 | async-start | bytes 2359296 | tf_op jit(solution)/shard_map/all_to_all | solution.py:298
  74.2 13.0 %collective-permute-start.2 = (bf16[64,4608]{1,0:T(8,128)(2,1)S(1)}, bf16[64,4608]{1,0:T(8,128)(2,1)S(1)}, u32[]{:S(2)}, u32[]{:S(2)}) collective-permute-start(bf16[64,4608]{1,0:T(8,128)(2,1)S(1)} %copy-done.6), channel_id=1, source_target_pairs={{0,1},{1,0},{2,17},{3,16},{16,3},{17,2},{18,19},{19,18},{4,5},{5,4... | collective-permute-start | bytes 1769480 | tf_op jit(solution)/shard_map/ppermute | solution.py:274
  87.3 5.4 %collective-permute-start.5 = (bf16[4,288,512]{2,1,0:T(8,128)(2,1)S(1)}, bf16[4,288,512]{2,1,0:T(8,128)(2,1)S(1)}, u32[]{:S(2)}, u32[]{:S(2)}) collective-permute-start(bf16[4,288,512]{2,1,0:T(8,128)(2,1)S(1)} %all-to-all-done.2.mine_ref), channel_id=1, source_target_pairs={{0,16},{16,0},{1,17},{17,1},{2,18},{18,2},{3,19},{19,3},{4,20},{20... | collective-permute-start | bytes 3538952 | tf_op jit(solution)/shard_map/ppermute | solution.py:300
  94.9 9.1 %collective-permute-start.6 = (bf16[64,1024]{1,0:T(8,128)(2,1)S(1)}, bf16[64,1024]{1,0:T(8,128)(2,1)S(1)}, u32[]{:S(2)}, u32[]{:S(2)}) collective-permute-start(bf16[64,1024]{1,0:T(8,128)(2,1)S(1)} %shard_map.71), channel_id=1, source_target_pairs={{0,0},{1,1},{16,2},{17,3},{2,16},{3,17},{18,18},{19,19},{4,4},{5,5... | collective-permute-start | bytes 393224 | tf_op jit(solution)/shard_map/ppermute | solution.py:325
  101.4 7.5 %collective-permute-start.7 = (bf16[64,1024]{1,0:T(8,128)(2,1)S(1)}, bf16[64,1024]{1,0:T(8,128)(2,1)S(1)}, u32[]{:S(2)}, u32[]{:S(2)}) collective-permute-start(bf16[64,1024]{1,0:T(8,128)(2,1)S(1)} %shard_map.72), channel_id=1, source_target_pairs={{1,0},{0,1},{17,2},{16,3},{3,16},{2,17},{19,18},{18,19},{5,4},{4,5... | collective-permute-start | bytes 393224 | tf_op jit(solution)/shard_map/ppermute | solution.py:325

commit v6 on v5

--- a/solution.py
+++ b/solution.py
@@ -86,13 +86,14 @@
         match = cold & (owner.astype(i32) == z * 2 + c) & (part == 18)
         want = jnp.sum(jnp.where(match, place, 0.0), axis=1, keepdims=True) + c * 16
         rows = jnp.where((part == 18) & (lane == c), want, rows)
+    tokens = pick(one_hot(hot * 8 + iota((64, 1), 0), 256), lat_ref[...]).astype(bf16)
+    places = pick(one_hot(hot + iota((16, 1), 0), 32), rope_ref[...]).astype(bf16)
     for c in range(4):
-        chosen = (part < 16) & (part % 4 == c)
-        index = jnp.where(chosen, hot * 8 + z * 4 + part // 4, -1)
-        rows = rows + pick(one_hot(index, 256), lat_ref[:, c * 128 : c * 128 + 128])
-        index = jnp.where(z % 2 * 2 + part - 16 == c, hot + z // 2, -1)
+        index = jnp.where((part < 16) & (part % 4 == c), z * 4 + part // 4, -1)
+        rows = rows + pick(one_hot(index, 64), tokens[:, c * 128 : c * 128 + 128])
+        index = jnp.where(z % 2 * 2 + part - 16 == c, z // 2, -1)
         index = jnp.where((part == 16) | (part == 17), index, -1)
-        rows = rows + pick(one_hot(index, 32), rope_ref[:, c * 128 : c * 128 + 128])
+        rows = rows + pick(one_hot(index, 16), places[:, c * 128 : c * 128 + 128])
     first_ref[...] = rows.astype(bf16)
 
 
@@ -154,14 +155,18 @@
         out_ref[rows, LAT:WIDE] = jnp.concatenate([part, part], axis=1)
 
 
-def attend(q_ref, ref, places):
+def spread(ref, places):
     lane = iota((32, 2 * ROPE), 1)
-    scores = []
     for n in range(4):
         for t in range(SHARE):
             pair = ref[n, 256:ROWS, t // 2 * 128 : t // 2 * 128 + 128]
             own = lane < ROPE if t % 2 == 0 else lane >= ROPE
             places[n, t * 32 : t * 32 + 32, :] = jnp.where(own, pair, 0)
+
+
+def attend(q_ref, ref, places):
+    scores = []
+    for n in range(4):
         keys = jnp.concatenate([ref[n, 0:256, :], places[n]], axis=1)
         scores.append(
             lax.dot_general(
@@ -182,6 +187,7 @@
 def first_half_kernel(
     q0_ref, q1_ref, mine_ref, blend0_ref, stat0_ref, blend1_ref, stat1_ref, places
 ):
+    spread(mine_ref, places)
     outs = ((q0_ref, blend0_ref, stat0_ref), (q1_ref, blend1_ref, stat1_ref))
     for q_ref, blend_ref, stat_ref in outs:
         top, total, blended = attend(q_ref, mine_ref, places)
@@ -193,6 +199,7 @@
 def second_half_kernel(q_ref, other_ref, blend_ref, stat_ref, w_ref, o_ref, places, w, sem):
     up = pltpu.make_async_copy(w_ref, w, sem)
     up.start()
+    spread(other_ref, places)
     top, total, blended = attend(q_ref, other_ref, places)
     top0, total0 = stat_ref[:, 0:1], stat_ref[:, 128:129]
     both = jnp.maximum(top, top0)
@@ -212,13 +219,14 @@
     smem = pl.BlockSpec(memory_space=pltpu.SMEM)
     params = pltpu.CompilerParams(vmem_limit_bytes=12 * 1024 * 1024)
     anywhere = pl.BlockSpec(memory_space=pl.ANY)
+    hbm = pl.BlockSpec(memory_space=pltpu.HBM)
     swap = [(0, 1), (1, 0)]
 
     pack = jax.ShapeDtypeStruct((152, LAT), bf16)
     own, theirs = pl.pallas_call(
         read_kernel,
         out_shape=[pack, pack],
-        in_specs=[vmem, anywhere, anywhere],
+        in_specs=[vmem, hbm, hbm],
         out_specs=[vmem, vmem],
         scratch_shapes=[
             pltpu.VMEM((16, 16, LAT), bf16),

time: 111 us -> 111 us (level)
  no operation moved by 1% of the time
where the time goes in v6:
time: 111 us; the launch traced here: 110 us
  starting transfers between devices  61 us (55%)
  waiting for transfers between devices  29.9 us (27%)
  Pallas kernels  12.4 us (11%)
  local copies, waits for them, and re-layouts  4.66 us (4%)
  other arithmetic  1.64 us (1%)
    all_to_all x1, starting transfers between devices, local(): lax.all_to_all(second, 'z', split_axis=0, concat_axis=0, tiled=True)  11.5 us
    ppermute x2, starting transfers between devices, travel(): lax.ppermute(queries[r], ('core', 'x'), pairs(r))  10.7 us
    all_to_all x1, waiting for transfers between devices, local(): lax.all_to_all(second, 'z', split_axis=0, concat_axis=0, tiled=True)  9.8 us
    all_to_all x1, starting transfers between devices, local(): first = lax.all_to_all(first, 'z', split_axis=0, concat_axis=0, tiled=True)  9.54 us
    ppermute x1, starting transfers between devices, local(): swapped = lax.ppermute(theirs, 'core', swap)  8.92 us
    ppermute x2, waiting for transfers between devices, travel(): lax.ppermute(queries[r], ('core', 'x'), pairs(r))  7.97 us
    ppermute x2, starting transfers between devices, local(): ups = [lax.ppermute(w_uv, ('core', 'x'), pairs(r)) for r in range(2)]  7.35 us
    ppermute x2, starting transfers between devices, local(): outs.append(lax.ppermute(out, ('core', 'x'), [(d, s) for s, d in pairs(r)]))  6.82 us
  transfers between devices with their start and end apart: 11, of which 6 were waited for; matrix products, arithmetic and copies ran while one was open for 2% of the time, Pallas kernels for 8%

profile of v6, /device:TPU:1, one launch (start us, length us, event | category | flops | bytes accessed | tf_op | source)
XLA Modules:
  0.0 109.8 jit_solution(2907086304160780429)
XLA Ops:
  0.0 0.0 copy-start.1
  0.0 1.2 %copy-done.1 = bf16[16,64,512]{2,1,0:T(8,128)(2,1)S(1)} copy-done((bf16[16,64,512]{2,1,0:T(8,128)(2,1)S(1)}, bf16[16,64,512]{2,1,0:T(8,128)(2,1)}, u32[]{:S(2)}) %copy-start.1) | copy-done | bytes 1048600
  1.2 0.9 copy-done.2
  2.1 0.0 copy-start.3
  2.1 0.7 copy-done.3
  2.8 0.1 shard_map.64
  2.9 8.9 %collective-permute-start = (bf16[152,512]{1,0:T(8,128)(2,1)S(1)}, bf16[152,512]{1,0:T(8,128)(2,1)S(1)}, u32[]{:S(2)}, u32[]{:S(2)}) collective-permute-start(bf16[152,512]{1,0:T(8,128)(2,1)S(1)} %get-tuple-element.29), channel_id=1, source_target_pairs={{0,16},{16,0},{1,17},{17,1},{2,18},{18,2},{3,19},{19,3},{4,20},{20... | collective-permute-start | bytes 466952 | tf_op jit(solution)/shard_map/ppermute | solution.py:238
  11.9 1.0 collective-permute-done.other_ref
  12.8 0.0 copy-done.4
  12.8 1.7 %shard_map.65 = (bf16[256,512]{1,0:T(8,128)(2,1)S(1)}, bf16[32,512]{1,0:T(8,128)(2,1)S(1)}, bf16[384,128]{1,0:T(8,128)(2,1)}, s32[8,128]{1,0:T(8,128)S(1)}) custom-call(s32[2,32]{1,0:T(2,128)S(1)} %copy-done.4, bf16[152,512]{1,0:T(8,128)(2,1)S(1)} %get-tuple-element.28.own_ref, bf16[152,512]{1,0:T(8,128)(2,1)S(1)} %collective-permute-done.other_ref), custom_call_target="tpu_custom_call" | custom-call | tf_op jit(solution)/shard_map/pallas_call | solution.py:240
  14.6 9.5 %all-to-all-start = ((bf16[16,24,128]{2,1,0:T(8,128)(2,1)}), bf16[16,24,128]{2,1,0:T(8,128)(2,1)S(1)}, u32[]{:S(2)}, u32[]{:S(2)}) async-start(bf16[16,24,128]{2,1,0:T(8,128)(2,1)} %bitcast.1), calls=%async_computation | async-start | bytes 196608 | tf_op jit(solution)/shard_map/all_to_all | solution.py:255
  24.1 0.0 copy-done.8
  24.1 0.6 constant_dynamic-slice_fusion
  24.8 0.0 copy-done.5
  24.8 0.1 constant_dynamic-slice_fusion.1
  24.9 5.2 %collective-permute-start.1 = (bf16[64,4608]{1,0:T(8,128)(2,1)S(1)}, bf16[64,4608]{1,0:T(8,128)(2,1)S(1)}, u32[]{:S(2)}, u32[]{:S(2)}) collective-permute-start(bf16[64,4608]{1,0:T(8,128)(2,1)S(1)} %pad_maximum_fusion), channel_id=1, source_target_pairs={{0,0},{1,1},{2,16},{3,17},{16,2},{17,3},{18,18},{19,19},{4,4},{5,5... | collective-permute-start | bytes 1769480 | tf_op jit(solution)/shard_map/ppermute | solution.py:282
  30.1 5.9 %all-to-all-done = bf16[16,24,128]{2,1,0:T(8,128)(2,1)S(1)} async-done(((bf16[16,24,128]{2,1,0:T(8,128)(2,1)}), bf16[16,24,128]{2,1,0:T(8,128)(2,1)S(1)}, u32[]{:S(2)}, u32[]{:S(2)}) %all-to-all-start) | async-done | bytes 98336 | tf_op jit(solution)/shard_map/all_to_all | solution.py:255
  36.0 1.5 %shard_map.66 = bf16[16,24,512]{2,1,0:T(8,128)(2,1)} custom-call(s32[2,32]{1,0:T(2,128)S(1)} %copy-done.4, bf16[384,128]{1,0:T(8,128)(2,1)S(1)} %bitcast.4, bf16[256,512]{1,0:T(8,128)(2,1)S(1)} %get-tuple-element.33.lat_ref, bf16[32,512]{1,0:T(8,128)(2,1)S(1)} %get-tuple-element.34.rope_ref), custom_call_target="tpu_custom_call" | custom-call | flops 5000000000 | tf_op jit(solution)/shard_map/pallas_call | solution.py:286
  37.5 0.4 collective-permute-done.1.q_ref
  38.0 0.1 shard_map.67.q0_ref.q_ref
  38.1 11.5 %all-to-all-start.1 = ((bf16[16,24,512]{2,1,0:T(8,128)(2,1)}), bf16[16,24,512]{2,1,0:T(8,128)(2,1)S(1)}, u32[]{:S(2)}, u32[]{:S(2)}) async-start(bf16[16,24,512]{2,1,0:T(8,128)(2,1)} %shard_map.66), calls=%async_computation.1 | async-start | bytes 786432 | tf_op jit(solution)/shard_map/all_to_all | solution.py:295
  49.5 5.2 %collective-permute-start.4 = (bf16[8,512,128]{2,1,0:T(8,128)(2,1)}, bf16[8,512,128]{2,1,0:T(8,128)(2,1)S(1)}, u32[]{:S(2)}, u32[]{:S(2)}) collective-permute-start(bf16[8,512,128]{2,1,0:T(8,128)(2,1)} %param.11), channel_id=1, source_target_pairs={{0,1},{1,0},{2,17},{3,16},{16,3},{17,2},{18,19},{19,18},{4,5},{5,4... | collective-permute-start | bytes 3145736 | tf_op jit(solution)/shard_map/ppermute | solution.py:284
  54.7 2.2 %collective-permute-start.3 = (bf16[8,512,128]{2,1,0:T(8,128)(2,1)}, bf16[8,512,128]{2,1,0:T(8,128)(2,1)}, u32[]{:S(2)}, u32[]{:S(2)}) collective-permute-start(bf16[8,512,128]{2,1,0:T(8,128)(2,1)} %param.11), channel_id=1, source_target_pairs={{0,0},{1,1},{2,16},{3,17},{16,2},{17,3},{18,18},{19,19},{4,4},{5,5... | collective-permute-start | bytes 3145736 | tf_op jit(solution)/shard_map/ppermute | solution.py:284
  56.9 0.0 copy-done.7
  56.9 0.9 pad_maximum_fusion.1
  57.8 0.1 slice_bitcast_fusion.owners_ref
  57.8 9.8 %all-to-all-done.1.got_ref = bf16[16,24,512]{2,1,0:T(8,128)(2,1)S(1)} async-done(((bf16[16,24,512]{2,1,0:T(8,128)(2,1)}), bf16[16,24,512]{2,1,0:T(8,128)(2,1)S(1)}, u32[]{:S(2)}, u32[]{:S(2)}) %all-to-all-start.1) | async-done | bytes 393248 | tf_op jit(solution)/shard_map/all_to_all | solution.py:295
  67.6 1.0 shard_map.68
  68.7 0.0 copy-start
  68.7 1.0 copy-done
  69.7 4.3 %all-to-all-start.2 = ((bf16[4,288,512]{2,1,0:T(8,128)(2,1)}), bf16[4,288,512]{2,1,0:T(8,128)(2,1)S(1)}, u32[]{:S(2)}, u32[]{:S(2)}) async-start(bf16[4,288,512]{2,1,0:T(8,128)(2,1)} %copy-done), calls=%async_computation.2 | async-start | bytes 2359296 | tf_op jit(solution)/shard_map/all_to_all | solution.py:306
  74.0 0.0 copy-done.6
  74.0 5.5 %collective-permute-start.2 = (bf16[64,4608]{1,0:T(8,128)(2,1)S(1)}, bf16[64,4608]{1,0:T(8,128)(2,1)S(1)}, u32[]{:S(2)}, u32[]{:S(2)}) collective-permute-start(bf16[64,4608]{1,0:T(8,128)(2,1)S(1)} %copy-done.6), channel_id=1, source_target_pairs={{0,1},{1,0},{2,17},{3,16},{16,3},{17,2},{18,19},{19,18},{4,5},{5,4... | collective-permute-start | bytes 1769480 | tf_op jit(solution)/shard_map/ppermute | solution.py:282
  79.5 7.6 %collective-permute-done.2.q_ref = bf16[64,4608]{1,0:T(8,128)(2,1)S(1)} collective-permute-done((bf16[64,4608]{1,0:T(8,128)(2,1)S(1)}, bf16[64,4608]{1,0:T(8,128)(2,1)S(1)}, u32[]{:S(2)}, u32[]{:S(2)}) %collective-permute-start.2) | collective-permute-done | bytes 589856 | tf_op jit(solution)/shard_map/ppermute | solution.py:282
  87.1 0.1 shard_map.69.q1_ref.q_ref
  87.2 0.0 collective-permute-done.4.w_ref
  87.2 0.0 collective-permute-done.3.w_ref
  87.2 0.0 all-to-all-done.2.mine_ref
  87.2 1.9 %collective-permute-start.5 = (bf16[4,288,512]{2,1,0:T(8,128)(2,1)S(1)}, bf16[4,288,512]{2,1,0:T(8,128)(2,1)S(1)}, u32[]{:S(2)}, u32[]{:S(2)}) collective-permute-start(bf16[4,288,512]{2,1,0:T(8,128)(2,1)S(1)} %all-to-all-done.2.mine_ref), channel_id=1, source_target_pairs={{0,16},{16,0},{1,17},{17,1},{2,18},{18,2},{3,19},{19,3},{4,20},{20... | collective-permute-start | bytes 3538952 | tf_op jit(solution)/shard_map/ppermute | solution.py:308
  89.1 3.4 %shard_map.70 = (f32[512,512]{1,0:T(8,128)S(1)}, f32[512,256]{1,0:T(8,128)S(1)}, f32[512,512]{1,0:T(8,128)S(1)}, f32[512,256]{1,0:T(8,128)S(1)}) custom-call(bf16[512,640]{1,0:T(8,128)(2,1)S(1)} %shard_map.67.q0_ref.q_ref, bf16[512,640]{1,0:T(8,128)(2,1)S(1)} %shard_map.69.q1_ref.q_ref, bf16[4,288,512]{2,1,0:T(8,128)(2,1)S(1)} %all-to-all-done.2.mine_ref), custom_call_target="tpu_custom_call" | custom-call | tf_op jit(solution)/shard_map/pallas_call | solution.py:314
  92.5 0.0 collective-permute-done.5.other_ref
  92.5 2.2 %shard_map.71 = bf16[64,1024]{1,0:T(8,128)(2,1)S(1)} custom-call(bf16[512,640]{1,0:T(8,128)(2,1)S(1)} %shard_map.67.q0_ref.q_ref, bf16[4,288,512]{2,1,0:T(8,128)(2,1)S(1)} %collective-permute-done.5.other_ref, f32[512,512]{1,0:T(8,128)S(1)} %get-tuple-element.45.blend_ref, f32[512,256]{1,0:T(8,128)S(1)} %get-tuple-element.46.stat_ref, ...), custom_call_target="tpu_custom_call" | custom-call | tf_op jit(solution)/shard_map/pallas_call | solution.py:324
  94.7 4.6 %collective-permute-start.6 = (bf16[64,1024]{1,0:T(8,128)(2,1)S(1)}, bf16[64,1024]{1,0:T(8,128)(2,1)S(1)}, u32[]{:S(2)}, u32[]{:S(2)}) collective-permute-start(bf16[64,1024]{1,0:T(8,128)(2,1)S(1)} %shard_map.71), channel_id=1, source_target_pairs={{0,0},{1,1},{16,2},{17,3},{2,16},{3,17},{18,18},{19,19},{4,4},{5,5... | collective-permute-start | bytes 393224 | tf_op jit(solution)/shard_map/ppermute | solution.py:333
  99.3 2.3 %shard_map.72 = bf16[64,1024]{1,0:T(8,128)(2,1)S(1)} custom-call(bf16[512,640]{1,0:T(8,128)(2,1)S(1)} %shard_map.69.q1_ref.q_ref, bf16[4,288,512]{2,1,0:T(8,128)(2,1)S(1)} %collective-permute-done.5.other_ref, f32[512,512]{1,0:T(8,128)S(1)} %get-tuple-element.48.blend_ref, f32[512,256]{1,0:T(8,128)S(1)} %get-tuple-element.49.stat_ref, ...), custom_call_target="tpu_custom_call" | custom-call | tf_op jit(solution)/shard_map/pallas_call | solution.py:324
  101.6 2.3 %collective-permute-start.7 = (bf16[64,1024]{1,0:T(8,128)(2,1)S(1)}, bf16[64,1024]{1,0:T(8,128)(2,1)S(1)}, u32[]{:S(2)}, u32[]{:S(2)}) collective-permute-start(bf16[64,1024]{1,0:T(8,128)(2,1)S(1)} %shard_map.72), channel_id=1, source_target_pairs={{1,0},{0,1},{17,2},{16,3},{3,16},{2,17},{19,18},{18,19},{5,4},{4,5... | collective-permute-start | bytes 393224 | tf_op jit(solution)/shard_map/ppermute | solution.py:333
  103.9 0.0 collective-permute-done.6
  103.9 5.2 %collective-permute-done.7 = bf16[64,1024]{1,0:T(8,128)(2,1)S(1)} collective-permute-done((bf16[64,1024]{1,0:T(8,128)(2,1)S(1)}, bf16[64,1024]{1,0:T(8,128)(2,1)S(1)}, u32[]{:S(2)}, u32[]{:S(2)}) %collective-permute-start.7) | collective-permute-done | bytes 131104 | tf_op jit(solution)/shard_map/ppermute | solution.py:333
  109.1 0.7 pad_maximum_fusion.2
  (8 shorter events, 0.1 us)
Async XLA Ops:
  0.0 1.2 %copy-start.1 = (bf16[16,64,512]{2,1,0:T(8,128)(2,1)S(1)}, bf16[16,64,512]{2,1,0:T(8,128)(2,1)}, u32[]{:S(2)}) copy-start(bf16[16,64,512]{2,1,0:T(8,128)(2,1)} %kv_ref.1) | copy-start | bytes 3145732
  1.2 0.9 copy-start.2
  2.1 0.7 copy-start.3
  2.8 10.0 %copy-start.4 = (s32[2,32]{1,0:T(2,128)S(1)}, s32[2,32]{1,0:T(2,128)}, u32[]{:S(2)}) copy-start(s32[2,32]{1,0:T(2,128)} %selection_ref.5) | copy-start | bytes 772
  2.8 21.3 %copy-start.8 = (bf16[128,512]{1,0:T(8,128)(2,1)S(1)}, bf16[128,512]{1,0:T(8,128)(2,1)}, u32[]{:S(2)}) copy-start(bf16[128,512]{1,0:T(8,128)(2,1)} %param.7) | copy-start | bytes 393220
  2.8 22.0 %copy-start.5 = (bf16[128,4096]{1,0:T(8,128)(2,1)S(1)}, bf16[128,4096]{1,0:T(8,128)(2,1)}, u32[]{:S(2)}) copy-start(bf16[128,4096]{1,0:T(8,128)(2,1)} %param.6) | copy-start | bytes 3145732
  2.9 9.9 %collective-permute-start = (bf16[152,512]{1,0:T(8,128)(2,1)S(1)}, bf16[152,512]{1,0:T(8,128)(2,1)S(1)}, u32[]{:S(2)}, u32[]{:S(2)}) collective-permute-start(bf16[152,512]{1,0:T(8,128)(2,1)S(1)} %get-tuple-element.29), channel_id=1, source_target_pairs={{0,16},{16,0},{1,17},{17,1},{2,18},{18,2},{3,19},{19,3},{4,20},{20... | collective-permute-start | bytes 466952 | tf_op jit(solution)/shard_map/ppermute | solution.py:238
  14.6 21.5 %all-to-all-start = ((bf16[16,24,128]{2,1,0:T(8,128)(2,1)}), bf16[16,24,128]{2,1,0:T(8,128)(2,1)S(1)}, u32[]{:S(2)}, u32[]{:S(2)}) async-start(bf16[16,24,128]{2,1,0:T(8,128)(2,1)} %bitcast.1), calls=%async_computation | async-start | bytes 196608 | tf_op jit(solution)/shard_map/all_to_all | solution.py:255
  24.9 13.0 %collective-permute-start.1 = (bf16[64,4608]{1,0:T(8,128)(2,1)S(1)}, bf16[64,4608]{1,0:T(8,128)(2,1)S(1)}, u32[]{:S(2)}, u32[]{:S(2)}) collective-permute-start(bf16[64,4608]{1,0:T(8,128)(2,1)S(1)} %pad_maximum_fusion), channel_id=1, source_target_pairs={{0,0},{1,1},{2,16},{3,17},{16,2},{17,3},{18,18},{19,19},{4,4},{5,5... | collective-permute-start | bytes 1769480 | tf_op jit(solution)/shard_map/ppermute | solution.py:282
  37.5 19.4 %copy-start.7 = (bf16[64,512]{1,0:T(8,128)(2,1)S(1)}, bf16[64,512]{1,0:T(8,128)(2,1)}, u32[]{:S(2)}) copy-start(bf16[64,512]{1,0:T(8,128)(2,1)} %get-tuple-element.55) | copy-start | bytes 196612
  38.1 29.6 %all-to-all-start.1 = ((bf16[16,24,512]{2,1,0:T(8,128)(2,1)}), bf16[16,24,512]{2,1,0:T(8,128)(2,1)S(1)}, u32[]{:S(2)}, u32[]{:S(2)}) async-start(bf16[16,24,512]{2,1,0:T(8,128)(2,1)} %shard_map.66), calls=%async_computation.1 | async-start | bytes 786432 | tf_op jit(solution)/shard_map/all_to_all | solution.py:295
  49.5 37.6 %collective-permute-start.4 = (bf16[8,512,128]{2,1,0:T(8,128)(2,1)}, bf16[8,512,128]{2,1,0:T(8,128)(2,1)S(1)}, u32[]{:S(2)}, u32[]{:S(2)}) collective-permute-start(bf16[8,512,128]{2,1,0:T(8,128)(2,1)} %param.11), channel_id=1, source_target_pairs={{0,1},{1,0},{2,17},{3,16},{16,3},{17,2},{18,19},{19,18},{4,5},{5,4... | collective-permute-start | bytes 3145736 | tf_op jit(solution)/shard_map/ppermute | solution.py:284
  54.7 32.5 %collective-permute-start.3 = (bf16[8,512,128]{2,1,0:T(8,128)(2,1)}, bf16[8,512,128]{2,1,0:T(8,128)(2,1)}, u32[]{:S(2)}, u32[]{:S(2)}) collective-permute-start(bf16[8,512,128]{2,1,0:T(8,128)(2,1)} %param.11), channel_id=1, source_target_pairs={{0,0},{1,1},{2,16},{3,17},{16,2},{17,3},{18,18},{19,19},{4,4},{5,5... | collective-permute-start | bytes 3145736 | tf_op jit(solution)/shard_map/ppermute | solution.py:284
  68.7 1.0 copy-start
  69.7 4.3 %copy-start.6 = (bf16[64,4608]{1,0:T(8,128)(2,1)S(1)}, bf16[64,4608]{1,0:T(8,128)(2,1)}, u32[]{:S(2)}) copy-start(bf16[64,4608]{1,0:T(8,128)(2,1)} %pad_maximum_fusion.1) | copy-start | bytes 1769476
  69.7 17.5 %all-to-all-start.2 = ((bf16[4,288,512]{2,1,0:T(8,128)(2,1)}), bf16[4,288,512]{2,1,0:T(8,128)(2,1)S(1)}, u32[]{:S(2)}, u32[]{:S(2)}) async-start(bf16[4,288,512]{2,1,0:T(8,128)(2,1)} %copy-done), calls=%async_computation.2 | async-start | bytes 2359296 | tf_op jit(solution)/shard_map/all_to_all | solution.py:306
  74.0 13.0 %collective-permute-start.2 = (bf16[64,4608]{1,0:T(8,128)(2,1)S(1)}, bf16[64,4608]{1,0:T(8,128)(2,1)S(1)}, u32[]{:S(2)}, u32[]{:S(2)}) collective-permute-start(bf16[64,4608]{1,0:T(8,128)(2,1)S(1)} %copy-done.6), channel_id=1, source_target_pairs={{0,1},{1,0},{2,17},{3,16},{16,3},{17,2},{18,19},{19,18},{4,5},{5,4... | collective-permute-start | bytes 1769480 | tf_op jit(solution)/shard_map/ppermute | solution.py:282
  87.2 5.3 %collective-permute-start.5 = (bf16[4,288,512]{2,1,0:T(8,128)(2,1)S(1)}, bf16[4,288,512]{2,1,0:T(8,128)(2,1)S(1)}, u32[]{:S(2)}, u32[]{:S(2)}) collective-permute-start(bf16[4,288,512]{2,1,0:T(8,128)(2,1)S(1)} %all-to-all-done.2.mine_ref), channel_id=1, source_target_pairs={{0,16},{16,0},{1,17},{17,1},{2,18},{18,2},{3,19},{19,3},{4,20},{20... | collective-permute-start | bytes 3538952 | tf_op jit(solution)/shard_map/ppermute | solution.py:308
  94.7 9.1 %collective-permute-start.6 = (bf16[64,1024]{1,0:T(8,128)(2,1)S(1)}, bf16[64,1024]{1,0:T(8,128)(2,1)S(1)}, u32[]{:S(2)}, u32[]{:S(2)}) collective-permute-start(bf16[64,1024]{1,0:T(8,128)(2,1)S(1)} %shard_map.71), channel_id=1, source_target_pairs={{0,0},{1,1},{16,2},{17,3},{2,16},{3,17},{18,18},{19,19},{4,4},{5,5... | collective-permute-start | bytes 393224 | tf_op jit(solution)/shard_map/ppermute | solution.py:333
  101.6 7.5 %collective-permute-start.7 = (bf16[64,1024]{1,0:T(8,128)(2,1)S(1)}, bf16[64,1024]{1,0:T(8,128)(2,1)S(1)}, u32[]{:S(2)}, u32[]{:S(2)}) collective-permute-start(bf16[64,1024]{1,0:T(8,128)(2,1)S(1)} %shard_map.72), channel_id=1, source_target_pairs={{1,0},{0,1},{17,2},{16,3},{3,16},{2,17},{19,18},{18,19},{5,4},{4,5... | collective-permute-start | bytes 393224 | tf_op jit(solution)/shard_map/ppermute | solution.py:333
